TPU v7x, 256 devices: a whole 4x4x8 slice. The times are simulated.
256 devices in a mesh: head: 8 (over z), seq: 32 (over x, y, core).
Axes of the slice: x: 4, y: 4, z: 8, core: 2. Of those that a mesh axis runs over, the one named last changes fastest.
Arguments:
- queries: bfloat16 [32768, 8192], P(('seq', 'head')), may hold values from -6 to 6
- key_rows: bfloat16 [32768, 8192], P(('seq', 'head')), may hold values from -0.5390625 to 0.5390625
- value_rows: bfloat16 [32768, 8192], P(('seq', 'head')), may hold values from -6 to 6
- log_decay: float32 [32768, 64], P('seq', 'head'), may hold values from -1 to 0, as said below
- initial_state: float32 [64, 128, 128], P('head'), may hold values from -24 to 24
Outputs:
- attended: bfloat16 [32768, 8192], P(('seq', 'head'))
Inputs may be any that keep to these rules, and one draw needn't show every extreme that they name: `log_decay`: entries are negative.
All inputs are finite; a program needn't handle non-finite values.
Results may differ from a plain program's by a relative error of at most 0.005.
Values may be sent and summed in bfloat16 or wider, within the bound.
No kernel may reach another device: no remote copies, remote signals or barrier semaphores. Data moves between devices by JAX's collectives and lax.ppermute only.
A program may use at most 128 MiB of HBM per device.

v0:
```python
import jax
import jax.numpy as jnp
from jax import lax
from jax.sharding import PartitionSpec as P

DH = 128
BLOCK = 256


HIGHEST = lax.Precision.HIGHEST


def entering(part, axis, combine, identity):
    place = lax.axis_index(axis)
    gathered = jax.tree.map(lambda a: lax.all_gather(a, axis), part)
    state = jax.tree.map(lambda a, e: jnp.zeros_like(a) + jnp.asarray(e, a.dtype), part, identity)

    def one(step, state):
        return combine(
            state, jax.tree.map(lambda a: lax.dynamic_index_in_dim(a, step, 0, False), gathered)
        )

    return lax.fori_loop(0, place, one, state)


def split_blocks(rows_in, head_count):
    length = rows_in.shape[0]
    block_len = min(BLOCK, length)
    return rows_in.reshape(length // block_len, block_len, head_count, DH)


def block_parts(q_blocks, k_blocks, v_blocks, decays):
    block_len = q_blocks.shape[1]
    query_f32 = q_blocks.astype(jnp.float32)
    key_f32 = k_blocks.astype(jnp.float32)
    value_f32 = v_blocks.astype(jnp.float32)
    cum_decay = jnp.cumsum(decays, axis=1)
    per_head_values = jnp.swapaxes(cum_decay, 1, 2)
    gaps = per_head_values[:, :, :, None] - per_head_values[:, :, None, :]
    rowsidx = jnp.arange(block_len, dtype=jnp.int32)
    causal = rowsidx[:, None] >= rowsidx[None, :]
    weight = jnp.where(causal[None, None], jnp.exp(jnp.minimum(gaps, 0.0)), 0.0)
    scores = jnp.einsum("nihd,njhd->nhij", query_f32, key_f32, precision=HIGHEST)
    local_part = jnp.einsum("nhij,njhd->nihd", scores * weight, value_f32, precision=HIGHEST)
    closing_running_total = cum_decay[:, -1, :]
    carried = jnp.exp(closing_running_total[:, None, :] - cum_decay)
    segment_memory_matrix = jnp.einsum(
        "njhd,njhe->nhde", key_f32 * carried[..., None], value_f32, precision=HIGHEST
    )
    return (local_part, cum_decay, segment_memory_matrix, jnp.exp(closing_running_total))


def exclusive_fold(states, decays):

    def advance(carried, element):
        held_state, held_decay = carried
        new_state, new_decay = element
        return (
            (new_decay[:, None, None] * held_state + new_state, held_decay * new_decay),
            (held_state, held_decay),
        )

    starting = (jnp.zeros_like(states[0]), jnp.ones_like(decays[0]))
    (total_state, total_decay), (before_state, before_decay) = lax.scan(
        advance, starting, (states, decays)
    )
    return (before_state, before_decay, total_state, total_decay)


def group_entry(total_decay, total_state, initial_state):

    def combine(earlier, later):
        return (earlier[0] * later[0], later[0][:, None, None] * earlier[1] + later[1])

    identity = (jnp.ones_like(total_decay), jnp.zeros_like(total_state))
    prefix_decay, prefix_state = entering((total_decay, total_state), "seq", combine, identity)
    return prefix_decay[:, None, None] * initial_state + prefix_state


def finish(q_blocks, local_part, cum_decay, before_state, before_decay, entry_state):
    incoming_state = before_state + before_decay[:, :, None, None] * entry_state[None]
    query_f32 = q_blocks.astype(jnp.float32)
    result = local_part + jnp.exp(cum_decay)[..., None] * jnp.einsum(
        "nihd,nhde->nihe", query_f32, incoming_state, precision=HIGHEST
    )
    factor = lax.rsqrt(jnp.mean(result * result, axis=-1, keepdims=True) + 1e-05)
    return (result * factor).astype(jnp.bfloat16)


def local(queries, key_rows, value_rows, log_decay, initial_state):
    q_group, k_group, v_group = (
        lax.all_to_all(queries, "head", split_axis=1, concat_axis=0, tiled=True),
        lax.all_to_all(key_rows, "head", split_axis=1, concat_axis=0, tiled=True),
        lax.all_to_all(value_rows, "head", split_axis=1, concat_axis=0, tiled=True),
    )
    head_count = q_group.shape[1] // DH
    q_blocks = split_blocks(q_group, head_count)
    k_blocks = split_blocks(k_group, head_count)
    v_blocks = split_blocks(v_group, head_count)
    decays = log_decay.reshape(q_blocks.shape[0], q_blocks.shape[1], head_count)
    local_part, cum_decay, segment_memory_matrix, block_decay = block_parts(
        q_blocks, k_blocks, v_blocks, decays
    )
    before_state, before_decay, total_state, total_decay = exclusive_fold(
        segment_memory_matrix, block_decay
    )
    entry_state = group_entry(total_decay, total_state, initial_state)
    result = finish(q_blocks, local_part, cum_decay, before_state, before_decay, entry_state)
    result = result.reshape(q_group.shape[0], head_count * DH)
    return lax.all_to_all(result, "head", split_axis=0, concat_axis=1, tiled=True)


def solution(mesh):
    placed = (
        P(("seq", "head"), None),
        P(("seq", "head"), None),
        P(("seq", "head"), None),
        P("seq", "head"),
        P("head", None, None),
    )
    return jax.shard_map(
        local, mesh=mesh, in_specs=placed, out_specs=P(("seq", "head"), None), check_vma=False
    )
```

profile of v0, /device:TPU:31, one launch (start us, length us, event | category | flops | bytes accessed | tf_op | source)
XLA Modules:
  0.0 345.0 jit_solution(6950354205862807619)
XLA Ops:
  6.5 3.1 copy.83
  9.7 8.2 %all-to-all-start.1 = ((bf16[128,8,1024]{2,0,1:T(8,128)(2,1)}), bf16[128,8,1024]{2,0,1:T(8,128)(2,1)S(1)}, u32[]{:S(2)}, u32[]{:S(2)}) async-start(bf16[128,8,1024]{2,0,1:T(8,128)(2,1)} %bitcast.82), calls=%async_computation.1 | async-start | bytes 4194304 | tf_op jit(solution)/shard_map/all_to_all | solution.py:93
  17.9 3.1 copy.82
  21.0 45.3 %all-to-all-done.1 = bf16[128,8,1024]{2,0,1:T(8,128)(2,1)S(1)} async-done(((bf16[128,8,1024]{2,0,1:T(8,128)(2,1)}), bf16[128,8,1024]{2,0,1:T(8,128)(2,1)S(1)}, u32[]{:S(2)}, u32[]{:S(2)}) %all-to-all-start.1) | async-done | bytes 2097184 | tf_op jit(solution)/shard_map/all_to_all | solution.py:93
  66.3 1.3 copy-done.3
  67.6 4.6 %all-to-all-start.2 = ((bf16[128,8,1024]{2,0,1:T(8,128)(2,1)}), bf16[128,8,1024]{2,0,1:T(8,128)(2,1)}, u32[]{:S(2)}, u32[]{:S(2)}) async-start(bf16[128,8,1024]{2,0,1:T(8,128)(2,1)} %bitcast.80), calls=%async_computation.2 | async-start | bytes 4194304 | tf_op jit(solution)/shard_map/all_to_all | solution.py:94
  72.3 2.3 reduce-window.6
  75.4 2.2 copy.63
  77.6 43.3 %all-to-all-done.2 = bf16[128,8,1024]{2,0,1:T(8,128)(2,1)} async-done(((bf16[128,8,1024]{2,0,1:T(8,128)(2,1)}), bf16[128,8,1024]{2,0,1:T(8,128)(2,1)}, u32[]{:S(2)}, u32[]{:S(2)}) %all-to-all-start.2) | async-done | bytes 2097184 | tf_op jit(solution)/shard_map/all_to_all | solution.py:94
  120.9 2.2 copy.64
  123.1 1.2 convert_multiply_fusion
  124.5 5.1 %fusion.10 = f32[4,8,128,128]{3,2,1,0:T(8,128)} fusion(f32[4,256,8,128]{3,2,1,0:T(8,128)S(1)} %convert_multiply_fusion, bf16[4,256,8,128]{3,2,1,0:T(8,128)(2,1)S(1)} %bitcast.85), kind=kOutput, calls=%fused_computation.17 | convolution fusion | flops 1610612736 | bytes 8388608 | tf_op jit(solution)/shard_map/njhd,njhe->nhde/dot_general | solution.py:47
  129.5 8.3 %while.30 = (s32[]{:T(128)}, f32[8,128,128]{2,1,0:T(8,128)S(1)}, f32[8]{0:T(128)S(1)}, f32[4,8,128,128]{3,2,1,0:T(8,128)}, f32[4,8]{1,0:T(4,128)S(1)}, /*index=5...) while((s32[]{:T(128)}, f32[8,128,128]{2,1,0:T(8,128)S(1)}, ...), condition=%wide.region_3.4_spmd.clone, body=%wide.region_2.3_spmd.clone.sunk | while | flops 524307 | bytes 2622325 | solution.py:64
  138.7 3.2 copy.84
  141.8 4.5 %all-to-all-start = ((bf16[128,8,1024]{2,0,1:T(8,128)(2,1)}), bf16[128,8,1024]{2,0,1:T(8,128)(2,1)}, u32[]{:S(2)}, u32[]{:S(2)}) async-start(bf16[128,8,1024]{2,0,1:T(8,128)(2,1)} %bitcast.81), calls=%async_computation | async-start | bytes 4194304 | tf_op jit(solution)/shard_map/all_to_all | solution.py:92
  147.9 63.9 %all-reduce = f32[256]{0:T(256)S(1)} all-reduce(f32[256]{0:T(256)S(1)} %dynamic-update-slice), channel_id=2, replica_groups=mesh['head'=8,'seq'=32] {'seq'}, use_global_device_ids=true, to_apply=%add | all-reduce | flops 256 | bytes 2048
  211.9 2.4 copy.62
  214.3 1.3 copy-done.1
  215.6 1.3 fusion.16
  217.2 8.8 %fusion.3 = f32[4,8,256,128]{2,3,1,0:T(8,128)} fusion(f32[4,8,256,256]{3,2,1,0:T(8,128)S(1)} %fusion.16, f32[4,8,256]{2,1,0:T(8,128)S(1)} %add_bitcast_fusion.1, pred[256,256]{1,0:T(8,128)(4,1)S(1)} %iota_compare_fusion, bf16[4,256,8,128]{3,2,1,0:T(8,128)(2,1)S(1)} %bitcast.86), kind=kOutput, calls=%fused_computation.9 | convolution fusion | flops 3229614080 | bytes 14778368 | tf_op jit(solution)/shard_map/nhij,njhd->nihd/dot_general | solution.py:44
  226.0 38.7 %while.29 = (s32[]{:T(128)}, f32[8]{0:T(128)S(1)}, f32[8,128,128]{2,1,0:T(8,128)S(1)}, s32[]{:T(128)}, f32[32,8]{1,0:T(8,128)S(1)}, /*index=5*/f32[32,8,128,128]{3,2,1,0:T(8,128)}, s32[]{:T(128)}, s32[]{:T(128)}, s32[]{:T(128)}) while((s32[]{:T(128)}, f32[8]{0:T(128)S(1)}, f32[8,128,128]{2,1,0:T(8,128)S(1)}, s32[]{:T(128)}, ...), condition=%wide.region_5.6_spmd, body=%wide.region_4.5_spmd.sunk | while | flops 262157 | bytes 1573159 | solution.py:23
  226.0 1.3 bitcast_add_fusion.4
  231.1 1.2 bitcast_add_fusion.4
  236.1 1.2 bitcast_add_fusion.4
  241.0 1.2 bitcast_add_fusion.4
  244.7 1.2 bitcast_add_fusion.4
  264.8 5.7 %multiply_reduce_fusion = (f32[4,256,8]{1,2,0:T(8,128)S(1)}, f32[4,256,8,128]{1,3,2,0:T(8,128)S(1)}) fusion(bf16[4,256,8,128]{3,2,1,0:T(8,128)(2,1)S(1)} %bitcast.78, f32[4,8,128,128]{3,2,1,0:T(8,128)} %get-tuple-element.79, f32[8,128,128]{2,1,0:T(8,128)S(1)} %multiply_add_fusion, f32[4,8]{1,0:T(4,128)S(1)} %get-tuple-element.80, ...), kind=kOutput, calls=%fused_computation.20 | convolution fusion | flops 1615847424 | bytes 13172864 | tf_op jit(solution)/shard_map/nihd,nhde->nihe/dot_general | solution.py:83
  271.2 2.6 copy.55
  273.7 2.8 all_to_all.59
  276.6 55.7 %all_to_all.67 = bf16[8,128,1024]{2,1,0:T(8,128)(2,1)} all-to-all(bf16[8,128,1024]{2,1,0:T(8,128)(2,1)S(1)} %all_to_all.59), channel_id=1, replica_groups=mesh['head'=8,'seq'=32] {'head'}, dimensions={0} | all-to-all | bytes 4194304 | tf_op jit(solution)/shard_map/all_to_all | solution.py:110
  332.2 3.0 copy.56
  335.3 2.9 copy.57
  (118 shorter events, 43.6 us)
Async XLA Ops:
  9.7 56.6 %all-to-all-start.1 = ((bf16[128,8,1024]{2,0,1:T(8,128)(2,1)}), bf16[128,8,1024]{2,0,1:T(8,128)(2,1)S(1)}, u32[]{:S(2)}, u32[]{:S(2)}) async-start(bf16[128,8,1024]{2,0,1:T(8,128)(2,1)} %bitcast.82), calls=%async_computation.1 | async-start | bytes 4194304 | tf_op jit(solution)/shard_map/all_to_all | solution.py:93
  66.3 1.3 copy-start.3
  66.3 6.0 %copy-start.7 = (f32[1024,8]{0,1:T(8,128)S(1)}, f32[1024,8]{0,1:T(8,128)}, u32[]{:S(2)}) copy-start(f32[1024,8]{0,1:T(8,128)} %param.12) | copy-start | bytes 98308
  67.6 53.3 %all-to-all-start.2 = ((bf16[128,8,1024]{2,0,1:T(8,128)(2,1)}), bf16[128,8,1024]{2,0,1:T(8,128)(2,1)}, u32[]{:S(2)}, u32[]{:S(2)}) async-start(bf16[128,8,1024]{2,0,1:T(8,128)(2,1)} %bitcast.80), calls=%async_computation.2 | async-start | bytes 4194304 | tf_op jit(solution)/shard_map/all_to_all | solution.py:94
  72.2 153.7 %all-gather.4.cloned.1.call-start = ((), (), s32[]{:S(2)}) async-start(), calls=%async_computation.4 | async-start | bytes 17301504 | tf_op jit(solution)/shard_map/all_gather | solution.py:15
  123.1 1.3 copy-start.4
  137.8 0.8 copy-start
  141.8 4.5 %copy-start.8 = (u32[256]{0:T(256)S(1)}, u32[256]{0:T(256)}, u32[]{:S(2)}) copy-start(u32[256]{0:T(256)} %constant.52) | copy-start | bytes 3076
  141.8 70.0 %all-to-all-start = ((bf16[128,8,1024]{2,0,1:T(8,128)(2,1)}), bf16[128,8,1024]{2,0,1:T(8,128)(2,1)}, u32[]{:S(2)}, u32[]{:S(2)}) async-start(bf16[128,8,1024]{2,0,1:T(8,128)(2,1)} %bitcast.81), calls=%async_computation | async-start | bytes 4194304 | tf_op jit(solution)/shard_map/all_to_all | solution.py:92
  214.2 1.3 copy-start.1
  215.6 1.6 copy-start.5
  217.2 47.5 %copy-start.6 = (f32[8,128,128]{2,1,0:T(8,128)S(1)}, f32[8,128,128]{2,1,0:T(8,128)}, u32[]{:S(2)}) copy-start(f32[8,128,128]{2,1,0:T(8,128)} %param.13) | copy-start | bytes 1572868
  226.0 38.9 %copy-start.2 = (bf16[128,8,8,128]{3,2,1,0:T(8,128)(2,1)S(1)}, bf16[128,8,8,128]{3,2,1,0:T(8,128)(2,1)}, u32[]{:S(2)}) copy-start(bf16[128,8,8,128]{3,2,1,0:T(8,128)(2,1)} %copy-done.1) | copy-start | bytes 6291460
Sparse Core Ops, SparseCore 0:
  138.8 75.6 all-gather.3
where the time goes:
time: 347 us; the launch traced here: 345 us
  blocking collectives  120 us (35%)
  waiting for transfers between devices  88.6 us (26%)
  other arithmetic  50.2 us (14%)
  local copies, waits for them, and re-layouts  33.1 us (10%)
  matrix products  20.8 us (6%)
  starting transfers between devices  17.3 us (5%)
  between operations  14.3 us (4%)
    unnamed x1, blocking collectives  63.9 us
    all_to_all x1, blocking collectives, local(): lax.all_to_all(result, 'head', split_axis=0, concat_axis=1, tiled=True)  55.7 us
    all_to_all x1, waiting for transfers between devices, local(): lax.all_to_all(key_rows, 'head', split_axis=1, concat_axis=0, tiled=True)  45.3 us
    all_to_all x1, waiting for transfers between devices, local(): lax.all_to_all(value_rows, 'head', split_axis=1, concat_axis=0, tiled=True)  43.3 us
    add x31, other arithmetic, combine(): later[0][:, None, None] * earlier[1] + later[1]  37 us
    unnamed x24, local copies, waits for them, and re-layouts  11.5 us
    dot_general x1, matrix products, block_parts(): jnp.einsum('nhij,njhd->nihd', scores * weight, value_f32, precision=HIGHEST)  8.76 us
    all_to_all x3, local copies, waits for them, and re-layouts, local(): lax.all_to_all(result, 'head', split_axis=0, concat_axis=1, tiled=True)  8.74 us
  transfers between devices with their start and end apart: 4, of which 2 were waited for; matrix products, arithmetic and copies ran while one was open for 7% of the time, Pallas kernels for 0%

commit v1 on v0

v1 whole, which is shorter than its diff:
```python
import functools

import jax
import jax.numpy as jnp
from jax import lax
from jax.experimental import pallas as pl
from jax.experimental.pallas import tpu as pltpu
from jax.sharding import PartitionSpec as P

DH = 128
ROWS = 128
GROUP = 8
HEADS = 64
PAIR = GROUP // 2
NZ = 8
NX = 4
NY = 4
WIDE = GROUP * DH
LIMIT = 16 * 1024 * 1024
HIGHEST = lax.Precision.HIGHEST
F32 = jnp.float32
BF16 = jnp.bfloat16
ORDER = (4, 3, 5, 2, 6, 1, 7)
LISTED = (6, 1, 7, 4, 3, 5, 2)
SENDS = ((4, 3, 5), (2, 6, 1, 7, 0))
GROUPS = ((0, 4, 3), (5, 2, 6, 1, 7))
TAIL = 8
TAIL16 = 16


VM = pl.BlockSpec(memory_space=pltpu.VMEM)
SM = pl.BlockSpec(memory_space=pltpu.SMEM)
ANY = pl.BlockSpec(memory_space=pl.ANY)
BLOCK = pl.BlockSpec((ROWS, WIDE), lambda i: (0, i))
STATE = jax.ShapeDtypeStruct((GROUP, DH, DH), BF16)


def params():
    return pltpu.CompilerParams(vmem_limit_bytes=LIMIT)


def cost(flops, nbytes, trans=0):
    return pl.CostEstimate(flops=flops, bytes_accessed=nbytes, transcendentals=trans)


def split(x):
    hi = x.astype(BF16)
    return hi, (x - hi.astype(F32)).astype(BF16)


def dot(a, b, dims):
    return lax.dot_general(a, b, (dims, ((), ())), preferred_element_type=F32)


def iota2(axis):
    return lax.broadcasted_iota(jnp.int32, (ROWS, ROWS), axis)


def exact(a, b):
    return lax.dot_general(
        a, b, (((1,), (0,)), ((), ())), precision=HIGHEST, preferred_element_type=F32
    )


def state_kernel(count, chunks, k_ref, v_ref, ld_ref, *refs):
    outs, held, sems = refs[:count], refs[count], refs[count + 1]
    step = pl.program_id(0)
    later = (iota2(0) > iota2(1)).astype(F32)
    carried = jnp.exp(jnp.minimum(exact(ld_ref[0], later), 0.0))
    for i in range(GROUP):
        cols = slice(i * DH, (i + 1) * DH)
        hi, lo = split(k_ref[:, cols].astype(F32).T * carried[i : i + 1, :])
        v = v_ref[:, cols]
        both = jnp.concatenate([hi, lo], axis=1)
        held[step, i] = dot(both, jnp.concatenate([v, v], axis=0), ((1,), (0,))).astype(BF16)
    copies = [pltpu.make_async_copy(held.at[k], outs[k], sems.at[k]) for k in range(count)]
    for k in range(count):

        @pl.when(step == k)
        def _():
            copies[k].start()

    @pl.when(step == count - 1)
    def _():
        for copy in copies:
            copy.wait()


def block_states(chunks, count, k, v, ld):
    wide = pl.BlockSpec((ROWS, WIDE), lambda i, c: (0, c[i]))
    return pl.pallas_call(
        functools.partial(state_kernel, count),
        grid_spec=pltpu.PrefetchScalarGridSpec(
            num_scalar_prefetch=1,
            grid=(count,),
            in_specs=[wide, wide, pl.BlockSpec((1, GROUP, ROWS), lambda i, c: (c[i], 0, 0))],
            out_specs=[ANY] * count,
            scratch_shapes=[
                pltpu.VMEM((count, GROUP, DH, DH), BF16),
                pltpu.SemaphoreType.DMA((count,)),
            ],
        ),
        out_shape=[STATE] * count,
        compiler_params=params(),
        cost_estimate=cost(count * GROUP * 4 * 128**3, count * 800000, 1 << 10),
    )(chunks, k, v, ld)


def intra_kernel(q_ref, k_ref, v_ref, ld_ref, after_ref, out_ref, qd_ref):
    ld = ld_ref[0]
    cum_t = exact(ld, (iota2(0) <= iota2(1)).astype(F32))
    causal = iota2(0) >= iota2(1)
    for i in range(GROUP):
        cols = slice(i * DH, (i + 1) * DH)
        across = jnp.broadcast_to(cum_t[i : i + 1, :], (ROWS, ROWS))
        down = across.T
        weight = jnp.where(causal, jnp.exp(jnp.minimum(down - across, 0.0)), 0.0)
        q = q_ref[:, cols]
        scores = dot(q, k_ref[:, cols], ((1,), (1,)))
        hi, lo = split(scores * weight)
        v = v_ref[:, cols]
        both = jnp.concatenate([hi, lo], axis=1)
        out_ref[:, cols] = dot(both, jnp.concatenate([v, v], axis=0), ((1,), (0,)))
        hi, lo = split(q.astype(F32) * jnp.exp(down))
        qd_ref[:, 2 * i * DH : (2 * i + 1) * DH] = hi
        qd_ref[:, (2 * i + 1) * DH : (2 * i + 2) * DH] = lo


def intra(q, k, v, ld, after):
    return pl.pallas_call(
        intra_kernel,
        grid=(NZ,),
        in_specs=[BLOCK, BLOCK, BLOCK, pl.BlockSpec((1, GROUP, ROWS), lambda i: (i, 0, 0)), ANY],
        out_specs=[BLOCK, pl.BlockSpec((ROWS, 2 * WIDE), lambda i: (0, i))],
        out_shape=[
            jax.ShapeDtypeStruct((ROWS, NZ * WIDE), F32),
            jax.ShapeDtypeStruct((ROWS, 2 * NZ * WIDE), BF16),
        ],
        compiler_params=params(),
        cost_estimate=cost(64 * 6 * 128**3, 14 << 20, 1 << 21),
    )(q, k, v, ld, after)


def row_kernel(place, w_ref, r_ref, *refs):
    turns = (0,) + LISTED
    pieces, sides = refs[:NZ], refs[-2:]
    z, core = place[0], place[1]
    for ref, side in zip(sides, (core, 1 - core)):
        for i in range(PAIR):
            h = side * PAIR + i
            total = None
            for k, piece in zip(turns, pieces):
                block = lax.rem(z + NZ - k, NZ)
                term = piece[h].astype(F32) * w_ref[block * GROUP + h]
                total = term if total is None else total + term
            ref[i, :DH, :] = total
            ref[i, DH:, :] = jnp.full((TAIL, DH), r_ref[h], F32)


def row_states(place, weights, rows, pieces, after):
    shape = jax.ShapeDtypeStruct((PAIR, DH + TAIL, DH), F32)
    return pl.pallas_call(
        row_kernel,
        in_specs=[SM, SM, SM] + [VM] * NZ + [ANY],
        out_specs=[VM, VM],
        out_shape=[shape, shape],
        compiler_params=params(),
        cost_estimate=cost(GROUP * DH * DH * 16, 3 << 20),
    )(place, weights, rows, *pieces, after)


def put(ref, i, state, decay):
    hi = decay.astype(BF16).astype(F32)
    mid = (decay - hi).astype(BF16).astype(F32)
    low = decay - hi - mid
    row = lax.broadcasted_iota(jnp.int32, (TAIL16, DH), 0)
    tail = jnp.where(row == 0, hi, jnp.where(row == 1, mid, jnp.where(row == 2, low, 0.0)))
    ref[i, :DH, :] = state.astype(BF16)
    ref[i, DH:, :] = tail.astype(BF16)


def decay_of(ref, i):
    return jnp.sum(ref[i, DH:, :].astype(F32), axis=0, keepdims=True)


def picked(values, flags):
    total = jnp.zeros_like(values[0])
    for value, flag in zip(values, flags):
        total = total + jnp.where(flag, value, 0.0)
    return total


def behind(at, n):
    return [lax.rem(at + n - k, n) for k in range(n)]


def ordered(core, mine_ref, got_ref, i):
    first = jnp.where(core == 0, mine_ref[i], got_ref[i])
    second = jnp.where(core == 0, got_ref[i], mine_ref[i])
    return first[:DH], first[DH : DH + 1], second[:DH], second[DH : DH + 1]


def pair_kernel(place, mine_ref, got_ref, out_ref):
    for i in range(PAIR):
        first, over_first, second, over_second = ordered(place[1], mine_ref, got_ref, i)
        put(out_ref, i, jnp.exp(over_second) * first + second, over_first + over_second)


def line_kernel(place, *refs):
    pairs, out_ref = refs[:NY], refs[-1]
    ys = behind(place[3], NY)
    for i in range(PAIR):
        decays = [decay_of(p, i) for p in pairs]
        total = None
        for k in range(NY):
            gap = picked(decays, [other > ys[k] for other in ys])
            term = jnp.exp(gap) * pairs[k][i, :DH, :].astype(F32)
            total = term if total is None else total + term
        put(out_ref, i, total, sum(decays))


def entry_kernel(place, start_ref, mine_ref, got_ref, *refs):
    pairs, lines, (keep_ref, give_ref) = refs[:NY], refs[NY : NY + NX], refs[-2:]
    core, x, y = place[1], place[2], place[3]
    xs, ys = behind(x, NX), behind(y, NY)
    for i in range(PAIR):
        over_pairs = [decay_of(p, i) for p in pairs]
        over_lines = [decay_of(p, i) for p in lines]
        in_line = picked(over_pairs, [at < y for at in ys])
        gap = in_line + picked(over_lines, [at < x for at in xs])
        entry = jnp.exp(gap) * start_ref[core * PAIR + i]
        for k in range(1, NY):
            gap = picked(over_pairs, [(at > ys[k]) & (at < y) for at in ys])
            weight = jnp.where(ys[k] < y, jnp.exp(gap), 0.0)
            entry = entry + weight * pairs[k][i, :DH, :].astype(F32)
        for k in range(1, NX):
            gap = in_line + picked(over_lines, [(at > xs[k]) & (at < x) for at in xs])
            weight = jnp.where(xs[k] < x, jnp.exp(gap), 0.0)
            entry = entry + weight * lines[k][i, :DH, :].astype(F32)
        first, over_first, _, _ = ordered(core, mine_ref, got_ref, i)
        later = jnp.exp(over_first) * entry + first
        keep_ref[i] = jnp.where(core == 0, entry, later)
        give_ref[i] = jnp.where(core == 0, later, entry)


def small(kernel, out_shape, place, *args):
    single = not isinstance(out_shape, list)
    return pl.pallas_call(
        kernel,
        in_specs=[SM] + [VM] * len(args),
        out_specs=VM if single else [VM] * len(out_shape),
        out_shape=out_shape,
        compiler_params=params(),
        cost_estimate=cost(PAIR * DH * DH * 16, 1 << 20),
    )(place, *args)


def seq_scan(place, mine, give, start):
    message = jax.ShapeDtypeStruct((PAIR, DH + TAIL16, DH), BF16)
    state = jax.ShapeDtypeStruct((PAIR, DH, DH), F32)
    got = swap_core(give)
    pairs = around(small(pair_kernel, message, place, mine, got), from_y, NY)
    lines = around(small(line_kernel, message, place, *pairs), from_x, NX)
    keep, give = small(
        entry_kernel, [state, state], place, start, mine, got, *pairs, *lines
    )
    return keep, swap_core(give)


def spread_kernel(place, d_ref, keep_ref, got_ref, *refs):
    turns = (0,) + LISTED
    pieces, outs, states, entries = refs[:NZ], refs[NZ : 2 * NZ], refs[-2], refs[-1]
    z, core = place[0], place[1]
    for k, piece in zip(turns, pieces):
        states[lax.rem(z + NZ - k, NZ)] = piece[...]
    for ref, side in ((keep_ref, core), (got_ref, 1 - core)):
        for i in range(PAIR):
            h = side * PAIR + i
            state = ref[i]
            for j in range(NZ):
                entries[j, h] = state.astype(BF16)
                if j < NZ - 1:
                    state = state * d_ref[j * GROUP + h] + states[j, h].astype(F32)
    for k, out in zip(turns, outs):
        out[...] = entries[lax.rem(z + k, NZ)]


def spread(place, decays, keep, got, pieces):
    outs = pl.pallas_call(
        spread_kernel,
        in_specs=[SM, SM] + [VM] * (NZ + 2),
        out_specs=[VM] * NZ,
        out_shape=[STATE] * NZ,
        scratch_shapes=[pltpu.VMEM((NZ, GROUP, DH, DH), BF16)] * 2,
        compiler_params=params(),
        cost_estimate=cost(GROUP * DH * DH * 16, 5 << 20),
    )(place, decays, keep, got, *pieces)
    return dict(zip((0,) + LISTED, outs))


def finish_kernel(count, chunks, qd_ref, o_ref, *refs):
    entries, out_ref, held = refs[:count], refs[-2], refs[-1]
    step = pl.program_id(0)
    for k in range(count):

        @pl.when(step == k)
        def _():
            for i in range(GROUP):
                cols = slice(i * DH, (i + 1) * DH)
                entry = entries[k][i]
                far = dot(
                    qd_ref[:, 2 * i * DH : (2 * i + 2) * DH],
                    jnp.concatenate([entry, entry], axis=0),
                    ((1,), (0,)),
                )
                held[i * ROWS : (i + 1) * ROWS, :] = o_ref[:, cols] + far

    o = held[...]
    ones = jnp.ones((2 * DH, DH), BF16)
    mean = dot(jnp.concatenate(split(o * o), axis=1), ones, ((1,), (0,))) * (1.0 / DH)
    o = (o * lax.rsqrt(mean + 1e-5)).astype(BF16)
    for i in range(GROUP):
        out_ref[:, i * DH : (i + 1) * DH] = o[i * ROWS : (i + 1) * ROWS, :]


def finish(chunks, qd, o, entries, held):
    count = len(entries)
    wide = pl.BlockSpec((ROWS, WIDE), lambda i, c: (0, c[i]))
    specs = [pl.BlockSpec((ROWS, 2 * WIDE), lambda i, c: (0, c[i])), wide]
    specs += [pl.BlockSpec((GROUP, DH, DH), lambda i, c: (0, 0, 0))] * count
    args = [chunks, qd, o, *entries]
    aliases = {}
    if held is not None:
        specs.append(ANY)
        args.append(held)
        aliases = {len(args) - 1: 0}
    return pl.pallas_call(
        functools.partial(finish_kernel, count),
        grid_spec=pltpu.PrefetchScalarGridSpec(
            num_scalar_prefetch=1,
            grid=(count,),
            in_specs=specs,
            out_specs=wide,
            scratch_shapes=[pltpu.VMEM((GROUP * ROWS, DH), F32)],
        ),
        out_shape=jax.ShapeDtypeStruct(o.shape, BF16),
        input_output_aliases=aliases,
        compiler_params=params(),
        cost_estimate=cost(8 * count * 4 * 128**3, count * 1500000, 1 << 14),
    )(*args)


def send(pieces, turns):
    return {
        t: lax.ppermute(pieces[t], "head", [(i, (i + t) % NZ) for i in range(NZ)]) for t in turns
    }


def seq_index(x, y, core):
    return (x * NY + y) * 2 + core


def swap_core(a):
    return lax.ppermute(a, "seq", [(i, i ^ 1) for i in range(NX * NY * 2)])


def from_y(a, k):
    pairs = [
        (seq_index(x, y, c), seq_index(x, (y + k) % NY, c))
        for x in range(NX)
        for y in range(NY)
        for c in range(2)
    ]
    return lax.ppermute(a, "seq", pairs)


def from_x(a, k):
    pairs = [
        (seq_index(x, y, c), seq_index((x + k) % NX, y, c))
        for x in range(NX)
        for y in range(NY)
        for c in range(2)
    ]
    return lax.ppermute(a, "seq", pairs)


def around(a, move, n):
    return [a] + [move(a, k) for k in range(1, n)]


def local(queries, key_rows, value_rows, log_decay, initial_state):
    queries, key_rows, value_rows = (
        pltpu.with_memory_space_constraint(a, pltpu.HBM) for a in (queries, key_rows, value_rows)
    )
    z = lax.axis_index("head").astype(jnp.int32)
    s = lax.axis_index("seq").astype(jnp.int32)
    place = jnp.stack([z, s % 2, s // (2 * NY), (s // 2) % NY])
    by_block = jnp.swapaxes(log_decay.T.reshape(GROUP, NZ, ROWS), 0, 1)
    ld = lax.all_to_all(by_block, "head", 0, 0, tiled=True)

    total = jnp.sum(by_block, axis=2)
    cells = jnp.arange(NZ)
    after = (cells[None, :] > cells[:, None])[..., None]
    closing = jnp.exp(jnp.sum(jnp.where(after, total[None], 0.0), axis=1)).reshape(-1)
    decays = jnp.exp(total).reshape(-1)
    rows = jnp.sum(total, axis=0)

    states = {}
    for turns in SENDS:
        chunks = jnp.stack([(z + t) % NZ for t in turns])
        states |= zip(turns, block_states(chunks, len(turns), key_rows, value_rows, ld))
    come = send(states, ORDER)
    come = [states[0]] + [come[t] for t in LISTED]
    o, qd = intra(queries, key_rows, value_rows, ld, states[0])

    mine, give = row_states(place, closing, rows, come, qd)
    keep, got = seq_scan(place, mine, give, initial_state)
    leave = spread(place, decays, keep, got, come)
    back = send(leave, ORDER)
    back[0] = leave[0]

    out = None
    for turns in GROUPS:
        chunks = jnp.stack([(z + NZ - t) % NZ for t in turns])
        out = finish(chunks, qd, o, [back[t] for t in turns], out)
    return out


def solution(mesh):
    placed = (
        P(("seq", "head"), None),
        P(("seq", "head"), None),
        P(("seq", "head"), None),
        P("seq", "head"),
        P("head", None, None),
    )
    return jax.shard_map(
        local, mesh=mesh, in_specs=placed, out_specs=P(("seq", "head"), None), check_vma=False
    )
```

time: 347 us -> 159 us (0.46)
  the two profiles are of different devices: /device:TPU:31 before, /device:TPU:1 now
where the time goes in v1:
time: 159 us
  waiting for transfers between devices  66 us (42%)
  starting transfers between devices  53.2 us (33%)
  Pallas kernels  32.3 us (20%)
  local copies, waits for them, and re-layouts  6.67 us (4%)
    ppermute x14, waiting for transfers between devices, send(): lax.ppermute(pieces[t], 'head', [(i, (i + t) % NZ) for i in range(NZ)])  38.2 us
    ppermute x14, starting transfers between devices, send(): lax.ppermute(pieces[t], 'head', [(i, (i + t) % NZ) for i in range(NZ)])  34.4 us
    pallas_call x1, Pallas kernels, intra(): pl.pallas_call(intra_kernel, grid=(NZ,), in_specs=[BLOCK, BLOCK, BLOCK, p...  9.53 us
    ppermute x3, waiting for transfers between devices, from_y(): return lax.ppermute(a, 'seq', pairs)  9.39 us
    ppermute x3, waiting for transfers between devices, from_x(): return lax.ppermute(a, 'seq', pairs)  9.31 us
    pallas_call x2, Pallas kernels, block_states(): pl.pallas_call(functools.partial(state_kernel, count), grid_spec=pltpu.Pr...  9.22 us
    all_to_all x1, starting transfers between devices, local(): ld = lax.all_to_all(by_block, 'head', 0, 0, tiled=True)  9.01 us
    pallas_call x2, Pallas kernels, finish(): pl.pallas_call(functools.partial(finish_kernel, count), grid_spec=pltpu.P...  8.3 us
  transfers between devices with their start and end apart: 23, of which 14 were waited for; matrix products, arithmetic and copies ran while one was open for 1% of the time, Pallas kernels for 12%

profile of v1, /device:TPU:1, one launch (start us, length us, event | category | flops | bytes accessed | tf_op | source)
XLA Modules:
  0.0 158.8 jit_solution(10179621661905824020)
XLA Ops:
  0.0 9.0 %all-to-all-start = ((f32[8,8,128]{2,1,0:T(8,128)}), f32[8,8,128]{2,1,0:T(8,128)S(1)}, u32[]{:S(2)}, u32[]{:S(2)}) async-start(f32[8,8,128]{2,1,0:T(8,128)} %bitcast.19), calls=%async_computation | async-start | bytes 65536 | tf_op jit(solution)/shard_map/all_to_all | solution.py:399
  9.1 6.8 %all-to-all-done.ld_ref = f32[8,8,128]{2,1,0:T(8,128)S(1)} async-done(((f32[8,8,128]{2,1,0:T(8,128)}), f32[8,8,128]{2,1,0:T(8,128)S(1)}, u32[]{:S(2)}, u32[]{:S(2)}) %all-to-all-start) | async-done | bytes 32800 | tf_op jit(solution)/shard_map/all_to_all | solution.py:399
  15.9 3.8 %shard_map.57 = (bf16[8,128,128]{2,1,0:T(8,128)(2,1)S(1)}, bf16[8,128,128]{2,1,0:T(8,128)(2,1)S(1)}, bf16[8,128,128]{2,1,0:T(8,128)(2,1)S(1)}) custom-call(s32[3]{0:T(128)S(1)} %add_add_fusion.chunks, bf16[128,8192]{1,0:T(8,128)(2,1)} %k_ref.5, bf16[128,8192]{1,0:T(8,128)(2,1)} %v_ref.5, f32[8,8,128]{2,1,0:T(8,128)S(1)} %all-to-all-done.ld_ref), custom_call_target="tpu_custom_call" | custom-call | flops 201326592 | bytes 2400000 | tf_op jit(solution)/shard_map/pallas_call | solution.py:91
  20.3 2.7 %collective-permute-start.4 = (bf16[8,128,128]{2,1,0:T(8,128)(2,1)S(1)}, bf16[8,128,128]{2,1,0:T(8,128)(2,1)S(1)}, u32[]{:S(2)}, u32[]{:S(2)}) collective-permute-start(bf16[8,128,128]{2,1,0:T(8,128)(2,1)S(1)} %get-tuple-element.34), channel_id=1, source_target_pairs={{0,96},{32,128},{64,160},{96,192},{128,224},{160,0},{192,32},{224,... | collective-permute-start | bytes 786440 | tf_op jit(solution)/shard_map/ppermute | solution.py:355
  23.4 1.8 %collective-permute-start.5 = (bf16[8,128,128]{2,1,0:T(8,128)(2,1)S(1)}, bf16[8,128,128]{2,1,0:T(8,128)(2,1)S(1)}, u32[]{:S(2)}, u32[]{:S(2)}) collective-permute-start(bf16[8,128,128]{2,1,0:T(8,128)(2,1)S(1)} %get-tuple-element.35), channel_id=1, source_target_pairs={{0,160},{32,192},{64,224},{96,0},{128,32},{160,64},{192,96},{224,1... | collective-permute-start | bytes 786440 | tf_op jit(solution)/shard_map/ppermute | solution.py:355
  25.1 5.4 %shard_map.55 = (bf16[8,128,128]{2,1,0:T(8,128)(2,1)S(1)}, bf16[8,128,128]{2,1,0:T(8,128)(2,1)}, bf16[8,128,128]{2,1,0:T(8,128)(2,1)S(1)}, bf16[8,128,128]{2,1,0:T(8,128)(2,1)S(1)}, bf16[8,128,128]{2,1,0:T(8,128)(2,1)S(1)}) custom-call(s32[5]{0:T(128)S(1)} %stack.68.chunks, bf16[128,8192]{1,0:T(8,128)(2,1)} %k_ref.5, bf16[128,8192]{1,0:T(8,128)(2,1)} %v_ref.5, ...), custom_call_target="tpu_custom_call" | custom-call | flops 335544320 | bytes 4000000 | tf_op jit(solution)/shard_map/pallas_call | solution.py:91
  30.6 3.0 %collective-permute-start = (bf16[8,128,128]{2,1,0:T(8,128)(2,1)}, bf16[8,128,128]{2,1,0:T(8,128)(2,1)S(1)}, u32[]{:S(2)}, u32[]{:S(2)}) collective-permute-start(bf16[8,128,128]{2,1,0:T(8,128)(2,1)} %get-tuple-element.30), channel_id=1, source_target_pairs={{0,192},{32,224},{64,0},{96,32},{128,64},{160,96},{192,128},{224,1... | collective-permute-start | bytes 786440 | tf_op jit(solution)/shard_map/ppermute | solution.py:355
  33.6 2.7 %collective-permute-start.2 = (bf16[8,128,128]{2,1,0:T(8,128)(2,1)S(1)}, bf16[8,128,128]{2,1,0:T(8,128)(2,1)S(1)}, u32[]{:S(2)}, u32[]{:S(2)}) collective-permute-start(bf16[8,128,128]{2,1,0:T(8,128)(2,1)S(1)} %get-tuple-element.32), channel_id=1, source_target_pairs={{0,224},{32,0},{64,32},{96,64},{128,96},{160,128},{192,160},{224,1... | collective-permute-start | bytes 786440 | tf_op jit(solution)/shard_map/ppermute | solution.py:355
  36.2 14.3 %collective-permute-done.4.refs_5_ = bf16[8,128,128]{2,1,0:T(8,128)(2,1)S(1)} collective-permute-done((bf16[8,128,128]{2,1,0:T(8,128)(2,1)S(1)}, bf16[8,128,128]{2,1,0:T(8,128)(2,1)S(1)}, u32[]{:S(2)}, u32[]{:S(2)}) %collective-permute-start.4) | collective-permute-done | bytes 262176 | tf_op jit(solution)/shard_map/ppermute | solution.py:355
  50.5 3.0 %collective-permute-start.6 = (bf16[8,128,128]{2,1,0:T(8,128)(2,1)S(1)}, bf16[8,128,128]{2,1,0:T(8,128)(2,1)S(1)}, u32[]{:S(2)}, u32[]{:S(2)}) collective-permute-start(bf16[8,128,128]{2,1,0:T(8,128)(2,1)S(1)} %get-tuple-element.36), channel_id=1, source_target_pairs={{0,64},{32,96},{64,128},{96,160},{128,192},{160,224},{192,0},{224,... | collective-permute-start | bytes 786440 | tf_op jit(solution)/shard_map/ppermute | solution.py:355
  53.8 9.5 %shard_map.56 = (f32[128,8192]{1,0:T(8,128)S(1)}, bf16[128,16384]{1,0:T(8,128)(2,1)S(1)}) custom-call(bf16[128,8192]{1,0:T(8,128)(2,1)} %q_ref.1, bf16[128,8192]{1,0:T(8,128)(2,1)} %k_ref.5, bf16[128,8192]{1,0:T(8,128)(2,1)} %v_ref.5, f32[8,8,128]{2,1,0:T(8,128)S(1)} %all-to-all-done.ld_ref, bf16[8,128,128]{2,1,0:T(8,128)(2,1)S(1)} %get-tuple-element.27.after_ref.refs_0_), custom_call_target="tpu_custom_call" | custom-call | flops 805306368 | bytes 14680064 | tf_op jit(solution)/shard_map/pallas_call | solution.py:130
  63.3 1.9 %copy-done.2 = f32[128,8192]{1,0:T(8,128)} copy-done((f32[128,8192]{1,0:T(8,128)}, f32[128,8192]{1,0:T(8,128)S(1)}, u32[]{:S(2)}) %copy-start.2) | copy-done | bytes 4194328
  67.4 1.6 %collective-permute-start.7 = (f32[4,136,128]{2,1,0:T(8,128)S(1)}, f32[4,136,128]{2,1,0:T(8,128)S(1)}, u32[]{:S(2)}, u32[]{:S(2)}) collective-permute-start(f32[4,136,128]{2,1,0:T(8,128)S(1)} %get-tuple-element.38), channel_id=1, source_target_pairs={{0,1},{1,0},{2,3},{3,2},{4,5},{5,4},{6,7},{7,6},{8,9},{9,8},{10,11... | collective-permute-start | bytes 835592 | tf_op jit(solution)/shard_map/ppermute | solution.py:364
  70.8 2.8 %collective-permute-start.10 = (bf16[4,144,128]{2,1,0:T(8,128)(2,1)S(1)}, bf16[4,144,128]{2,1,0:T(8,128)(2,1)S(1)}, u32[]{:S(2)}, u32[]{:S(2)}) collective-permute-start(bf16[4,144,128]{2,1,0:T(8,128)(2,1)S(1)} %shard_map.59.refs_0_), channel_id=1, source_target_pairs={{0,6},{1,7},{2,0},{3,1},{4,2},{5,3},{6,4},{7,5},{8,14},{9,15},{10,... | collective-permute-start | bytes 442376 | tf_op jit(solution)/shard_map/ppermute | solution.py:374
  74.7 4.8 %collective-permute-done.10.refs_3_ = bf16[4,144,128]{2,1,0:T(8,128)(2,1)S(1)} collective-permute-done((bf16[4,144,128]{2,1,0:T(8,128)(2,1)S(1)}, bf16[4,144,128]{2,1,0:T(8,128)(2,1)S(1)}, u32[]{:S(2)}, u32[]{:S(2)}) %collective-permute-start.10) | collective-permute-done | bytes 147488 | tf_op jit(solution)/shard_map/ppermute | solution.py:374
  79.9 4.1 %collective-permute-done.8.refs_1_ = bf16[4,144,128]{2,1,0:T(8,128)(2,1)S(1)} collective-permute-done((bf16[4,144,128]{2,1,0:T(8,128)(2,1)S(1)}, bf16[4,144,128]{2,1,0:T(8,128)(2,1)S(1)}, u32[]{:S(2)}, u32[]{:S(2)}) %collective-permute-start.8) | collective-permute-done | bytes 147488 | tf_op jit(solution)/shard_map/ppermute | solution.py:374
  84.8 2.6 %collective-permute-start.13 = (bf16[4,144,128]{2,1,0:T(8,128)(2,1)S(1)}, bf16[4,144,128]{2,1,0:T(8,128)(2,1)S(1)}, u32[]{:S(2)}, u32[]{:S(2)}) collective-permute-start(bf16[4,144,128]{2,1,0:T(8,128)(2,1)S(1)} %shard_map.60.refs_4_), channel_id=1, source_target_pairs={{0,24},{1,25},{2,26},{3,27},{4,28},{5,29},{6,30},{7,31},{8,0},{9,1... | collective-permute-start | bytes 442376 | tf_op jit(solution)/shard_map/ppermute | solution.py:384
  88.5 2.4 %collective-permute-done.13.refs_7_ = bf16[4,144,128]{2,1,0:T(8,128)(2,1)S(1)} collective-permute-done((bf16[4,144,128]{2,1,0:T(8,128)(2,1)S(1)}, bf16[4,144,128]{2,1,0:T(8,128)(2,1)S(1)}, u32[]{:S(2)}, u32[]{:S(2)}) %collective-permute-start.13) | collective-permute-done | bytes 147488 | tf_op jit(solution)/shard_map/ppermute | solution.py:384
  90.9 2.6 %collective-permute-done.12.refs_6_ = bf16[4,144,128]{2,1,0:T(8,128)(2,1)S(1)} collective-permute-done((bf16[4,144,128]{2,1,0:T(8,128)(2,1)S(1)}, bf16[4,144,128]{2,1,0:T(8,128)(2,1)S(1)}, u32[]{:S(2)}, u32[]{:S(2)}) %collective-permute-start.12) | collective-permute-done | bytes 147488 | tf_op jit(solution)/shard_map/ppermute | solution.py:384
  93.5 4.3 %collective-permute-done.11.refs_5_ = bf16[4,144,128]{2,1,0:T(8,128)(2,1)S(1)} collective-permute-done((bf16[4,144,128]{2,1,0:T(8,128)(2,1)S(1)}, bf16[4,144,128]{2,1,0:T(8,128)(2,1)S(1)}, u32[]{:S(2)}, u32[]{:S(2)}) %collective-permute-start.11) | collective-permute-done | bytes 147488 | tf_op jit(solution)/shard_map/ppermute | solution.py:384
  100.4 2.1 %shard_map.62 = (bf16[8,128,128]{2,1,0:T(8,128)(2,1)S(1)}, bf16[8,128,128]{2,1,0:T(8,128)(2,1)}, bf16[8,128,128]{2,1,0:T(8,128)(2,1)S(1)}, bf16[8,128,128]{2,1,0...) custom-call(s32[4]{0:T(128)S(1)} %pad_add_fusion.place, ...), custom_call_target="tpu_custom_call" | custom-call | flops 2097152 | bytes 5242880 | tf_op jit(solution)/shard_map/pallas_call | solution.py:289
  102.5 4.1 %collective-permute-start.20 = (bf16[8,128,128]{2,1,0:T(8,128)(2,1)S(1)}, bf16[8,128,128]{2,1,0:T(8,128)(2,1)S(1)}, u32[]{:S(2)}, u32[]{:S(2)}) collective-permute-start(bf16[8,128,128]{2,1,0:T(8,128)(2,1)S(1)} %get-tuple-element.47), channel_id=1, source_target_pairs={{0,128},{32,160},{64,192},{96,224},{128,0},{160,32},{192,64},{224,... | collective-permute-start | bytes 786440 | tf_op jit(solution)/shard_map/ppermute | solution.py:355
  106.6 2.6 %collective-permute-start.21 = (bf16[8,128,128]{2,1,0:T(8,128)(2,1)S(1)}, bf16[8,128,128]{2,1,0:T(8,128)(2,1)S(1)}, u32[]{:S(2)}, u32[]{:S(2)}) collective-permute-start(bf16[8,128,128]{2,1,0:T(8,128)(2,1)S(1)} %get-tuple-element.48), channel_id=1, source_target_pairs={{0,96},{32,128},{64,160},{96,192},{128,224},{160,0},{192,32},{224,... | collective-permute-start | bytes 786440 | tf_op jit(solution)/shard_map/ppermute | solution.py:355
  109.1 1.9 %collective-permute-start.15 = (bf16[8,128,128]{2,1,0:T(8,128)(2,1)}, bf16[8,128,128]{2,1,0:T(8,128)(2,1)S(1)}, u32[]{:S(2)}, u32[]{:S(2)}) collective-permute-start(bf16[8,128,128]{2,1,0:T(8,128)(2,1)} %get-tuple-element.41), channel_id=1, source_target_pairs={{0,160},{32,192},{64,224},{96,0},{128,32},{160,64},{192,96},{224,1... | collective-permute-start | bytes 786440 | tf_op jit(solution)/shard_map/ppermute | solution.py:355
  111.0 2.2 %collective-permute-start.16 = (bf16[8,128,128]{2,1,0:T(8,128)(2,1)}, bf16[8,128,128]{2,1,0:T(8,128)(2,1)S(1)}, u32[]{:S(2)}, u32[]{:S(2)}) collective-permute-start(bf16[8,128,128]{2,1,0:T(8,128)(2,1)} %get-tuple-element.42), channel_id=1, source_target_pairs={{0,64},{32,96},{64,128},{96,160},{128,192},{160,224},{192,0},{224,... | collective-permute-start | bytes 786440 | tf_op jit(solution)/shard_map/ppermute | solution.py:355
  114.6 8.6 %collective-permute-start.18 = (bf16[8,128,128]{2,1,0:T(8,128)(2,1)S(1)}, bf16[8,128,128]{2,1,0:T(8,128)(2,1)S(1)}, u32[]{:S(2)}, u32[]{:S(2)}) collective-permute-start(bf16[8,128,128]{2,1,0:T(8,128)(2,1)S(1)} %get-tuple-element.44), channel_id=1, source_target_pairs={{0,32},{32,64},{64,96},{96,128},{128,160},{160,192},{192,224},{224... | collective-permute-start | bytes 786440 | tf_op jit(solution)/shard_map/ppermute | solution.py:355
  123.2 16.9 %collective-permute-done.21.refs_2_ = bf16[8,128,128]{2,1,0:T(8,128)(2,1)S(1)} collective-permute-done((bf16[8,128,128]{2,1,0:T(8,128)(2,1)S(1)}, bf16[8,128,128]{2,1,0:T(8,128)(2,1)S(1)}, u32[]{:S(2)}, u32[]{:S(2)}) %collective-permute-start.21) | collective-permute-done | bytes 262176 | tf_op jit(solution)/shard_map/ppermute | solution.py:355
  140.3 2.2 %copy-done.1 = bf16[128,16384]{1,0:T(8,128)(2,1)S(1)} copy-done((bf16[128,16384]{1,0:T(8,128)(2,1)S(1)}, bf16[128,16384]{1,0:T(8,128)(2,1)}, u32[]{:S(2)}) %copy-start.1) | copy-done | bytes 4194328
  142.5 2.2 %copy-done.3 = f32[128,8192]{1,0:T(8,128)S(1)} copy-done((f32[128,8192]{1,0:T(8,128)S(1)}, f32[128,8192]{1,0:T(8,128)}, u32[]{:S(2)}) %copy-start.3) | copy-done | bytes 4194328
  144.7 3.4 %shard_map.63.refs_5_ = bf16[128,8192]{1,0:T(8,128)(2,1)} custom-call(s32[3]{0:T(128)S(1)} %add_add_fusion.1.chunks, bf16[128,16384]{1,0:T(8,128)(2,1)S(1)} %copy-done.1, f32[128,8192]{1,0:T(8,128)S(1)} %copy-done.3, bf16[8,128,128]{2,1,0:T(8,128)(2,1)S(1)} %get-tuple-element.46.refs_0_, bf16[8,128,128]{2,1,0:T(8,128)(2,1)S(1)} %collective-permute-done.20.refs_1_, ...), custom_call_target="tpu_custom_call" | custom-call | flops 201326592 | bytes 4500000 | tf_op jit(solution)/shard_map/pallas_call | solution.py:337
  149.7 4.2 %collective-permute-done.18.refs_3_ = bf16[8,128,128]{2,1,0:T(8,128)(2,1)S(1)} collective-permute-done((bf16[8,128,128]{2,1,0:T(8,128)(2,1)S(1)}, bf16[8,128,128]{2,1,0:T(8,128)(2,1)S(1)}, u32[]{:S(2)}, u32[]{:S(2)}) %collective-permute-start.18) | collective-permute-done | bytes 262176 | tf_op jit(solution)/shard_map/ppermute | solution.py:355
  153.9 4.9 %shard_map.64 = bf16[128,8192]{1,0:T(8,128)(2,1)} custom-call(s32[5]{0:T(128)S(1)} %stack.66.chunks, bf16[128,16384]{1,0:T(8,128)(2,1)S(1)} %copy-done.1, f32[128,8192]{1,0:T(8,128)S(1)} %copy-done.3, bf16[8,128,128]{2,1,0:T(8,128)(2,1)S(1)} %collective-permute-done.15.refs_0_, ...), custom_call_target="tpu_custom_call", output_to_operand_aliasing={{}: (8, {})} | custom-call | flops 335544320 | bytes 7500000 | tf_op jit(solution)/shard_map/pallas_call | solution.py:337
  (49 shorter events, 14.2 us)
Async XLA Ops:
  0.0 15.9 %all-to-all-start = ((f32[8,8,128]{2,1,0:T(8,128)}), f32[8,8,128]{2,1,0:T(8,128)S(1)}, u32[]{:S(2)}, u32[]{:S(2)}) async-start(f32[8,8,128]{2,1,0:T(8,128)} %bitcast.19), calls=%async_computation | async-start | bytes 65536 | tf_op jit(solution)/shard_map/all_to_all | solution.py:399
  9.1 13.9 %copy-start.5 = (f32[1024,8]{0,1:T(8,128)S(1)}, f32[1024,8]{0,1:T(8,128)}, u32[]{:S(2)}) copy-start(f32[1024,8]{0,1:T(8,128)} %param.8) | copy-start | bytes 98308
  19.7 13.9 %collective-permute-start.3 = (bf16[8,128,128]{2,1,0:T(8,128)(2,1)S(1)}, bf16[8,128,128]{2,1,0:T(8,128)(2,1)S(1)}, u32[]{:S(2)}, u32[]{:S(2)}) collective-permute-start(bf16[8,128,128]{2,1,0:T(8,128)(2,1)S(1)} %get-tuple-element.33), channel_id=1, source_target_pairs={{0,128},{32,160},{64,192},{96,224},{128,0},{160,32},{192,64},{224,... | collective-permute-start | bytes 786440 | tf_op jit(solution)/shard_map/ppermute | solution.py:355
  20.3 30.2 %collective-permute-start.4 = (bf16[8,128,128]{2,1,0:T(8,128)(2,1)S(1)}, bf16[8,128,128]{2,1,0:T(8,128)(2,1)S(1)}, u32[]{:S(2)}, u32[]{:S(2)}) collective-permute-start(bf16[8,128,128]{2,1,0:T(8,128)(2,1)S(1)} %get-tuple-element.34), channel_id=1, source_target_pairs={{0,96},{32,128},{64,160},{96,192},{128,224},{160,0},{192,32},{224,... | collective-permute-start | bytes 786440 | tf_op jit(solution)/shard_map/ppermute | solution.py:355
  23.4 41.9 %collective-permute-start.5 = (bf16[8,128,128]{2,1,0:T(8,128)(2,1)S(1)}, bf16[8,128,128]{2,1,0:T(8,128)(2,1)S(1)}, u32[]{:S(2)}, u32[]{:S(2)}) collective-permute-start(bf16[8,128,128]{2,1,0:T(8,128)(2,1)S(1)} %get-tuple-element.35), channel_id=1, source_target_pairs={{0,160},{32,192},{64,224},{96,0},{128,32},{160,64},{192,96},{224,1... | collective-permute-start | bytes 786440 | tf_op jit(solution)/shard_map/ppermute | solution.py:355
  30.6 34.7 %collective-permute-start = (bf16[8,128,128]{2,1,0:T(8,128)(2,1)}, bf16[8,128,128]{2,1,0:T(8,128)(2,1)S(1)}, u32[]{:S(2)}, u32[]{:S(2)}) collective-permute-start(bf16[8,128,128]{2,1,0:T(8,128)(2,1)} %get-tuple-element.30), channel_id=1, source_target_pairs={{0,192},{32,224},{64,0},{96,32},{128,64},{160,96},{192,128},{224,1... | collective-permute-start | bytes 786440 | tf_op jit(solution)/shard_map/ppermute | solution.py:355
  33.6 31.7 %collective-permute-start.1 = (bf16[8,128,128]{2,1,0:T(8,128)(2,1)S(1)}, bf16[8,128,128]{2,1,0:T(8,128)(2,1)S(1)}, u32[]{:S(2)}, u32[]{:S(2)}) collective-permute-start(bf16[8,128,128]{2,1,0:T(8,128)(2,1)S(1)} %get-tuple-element.31), channel_id=1, source_target_pairs={{0,32},{32,64},{64,96},{96,128},{128,160},{160,192},{192,224},{224... | collective-permute-start | bytes 786440 | tf_op jit(solution)/shard_map/ppermute | solution.py:355
  33.6 32.8 %collective-permute-start.2 = (bf16[8,128,128]{2,1,0:T(8,128)(2,1)S(1)}, bf16[8,128,128]{2,1,0:T(8,128)(2,1)S(1)}, u32[]{:S(2)}, u32[]{:S(2)}) collective-permute-start(bf16[8,128,128]{2,1,0:T(8,128)(2,1)S(1)} %get-tuple-element.32), channel_id=1, source_target_pairs={{0,224},{32,0},{64,32},{96,64},{128,96},{160,128},{192,160},{224,1... | collective-permute-start | bytes 786440 | tf_op jit(solution)/shard_map/ppermute | solution.py:355
  50.5 15.9 %collective-permute-start.6 = (bf16[8,128,128]{2,1,0:T(8,128)(2,1)S(1)}, bf16[8,128,128]{2,1,0:T(8,128)(2,1)S(1)}, u32[]{:S(2)}, u32[]{:S(2)}) collective-permute-start(bf16[8,128,128]{2,1,0:T(8,128)(2,1)S(1)} %get-tuple-element.36), channel_id=1, source_target_pairs={{0,64},{32,96},{64,128},{96,160},{128,192},{160,224},{192,0},{224,... | collective-permute-start | bytes 786440 | tf_op jit(solution)/shard_map/ppermute | solution.py:355
  63.3 2.0 %copy-start.2 = (f32[128,8192]{1,0:T(8,128)}, f32[128,8192]{1,0:T(8,128)S(1)}, u32[]{:S(2)}) copy-start(f32[128,8192]{1,0:T(8,128)S(1)} %get-tuple-element.29.o_ref) | copy-start | bytes 12582916
  65.3 2.1 %copy-start = (bf16[128,16384]{1,0:T(8,128)(2,1)}, bf16[128,16384]{1,0:T(8,128)(2,1)S(1)}, u32[]{:S(2)}) copy-start(bf16[128,16384]{1,0:T(8,128)(2,1)S(1)} %get-tuple-element.28.refs_8_.qd_ref) | copy-start | bytes 12582916
  66.4 31.4 %copy-start.4 = (f32[8,128,128]{2,1,0:T(8,128)S(1)}, f32[8,128,128]{2,1,0:T(8,128)}, u32[]{:S(2)}) copy-start(f32[8,128,128]{2,1,0:T(8,128)} %start_ref.1) | copy-start | bytes 1572868
  67.4 2.8 %collective-permute-start.7 = (f32[4,136,128]{2,1,0:T(8,128)S(1)}, f32[4,136,128]{2,1,0:T(8,128)S(1)}, u32[]{:S(2)}, u32[]{:S(2)}) collective-permute-start(f32[4,136,128]{2,1,0:T(8,128)S(1)} %get-tuple-element.38), channel_id=1, source_target_pairs={{0,1},{1,0},{2,3},{3,2},{4,5},{5,4},{6,7},{7,6},{8,9},{9,8},{10,11... | collective-permute-start | bytes 835592 | tf_op jit(solution)/shard_map/ppermute | solution.py:364
  70.8 8.7 %collective-permute-start.10 = (bf16[4,144,128]{2,1,0:T(8,128)(2,1)S(1)}, bf16[4,144,128]{2,1,0:T(8,128)(2,1)S(1)}, u32[]{:S(2)}, u32[]{:S(2)}) collective-permute-start(bf16[4,144,128]{2,1,0:T(8,128)(2,1)S(1)} %shard_map.59.refs_0_), channel_id=1, source_target_pairs={{0,6},{1,7},{2,0},{3,1},{4,2},{5,3},{6,4},{7,5},{8,14},{9,15},{10,... | collective-permute-start | bytes 442376 | tf_op jit(solution)/shard_map/ppermute | solution.py:374
  73.6 6.3 %collective-permute-start.9 = (bf16[4,144,128]{2,1,0:T(8,128)(2,1)S(1)}, bf16[4,144,128]{2,1,0:T(8,128)(2,1)S(1)}, u32[]{:S(2)}, u32[]{:S(2)}) collective-permute-start(bf16[4,144,128]{2,1,0:T(8,128)(2,1)S(1)} %shard_map.59.refs_0_), channel_id=1, source_target_pairs={{0,4},{1,5},{2,6},{3,7},{4,0},{5,1},{6,2},{7,3},{8,12},{9,13},{10,... | collective-permute-start | bytes 442376 | tf_op jit(solution)/shard_map/ppermute | solution.py:374
  74.0 10.1 %collective-permute-start.8 = (bf16[4,144,128]{2,1,0:T(8,128)(2,1)S(1)}, bf16[4,144,128]{2,1,0:T(8,128)(2,1)S(1)}, u32[]{:S(2)}, u32[]{:S(2)}) collective-permute-start(bf16[4,144,128]{2,1,0:T(8,128)(2,1)S(1)} %shard_map.59.refs_0_), channel_id=1, source_target_pairs={{0,2},{1,3},{2,4},{3,5},{4,6},{5,7},{6,0},{7,1},{8,10},{9,11},{10,... | collective-permute-start | bytes 442376 | tf_op jit(solution)/shard_map/ppermute | solution.py:374
  84.8 6.1 %collective-permute-start.13 = (bf16[4,144,128]{2,1,0:T(8,128)(2,1)S(1)}, bf16[4,144,128]{2,1,0:T(8,128)(2,1)S(1)}, u32[]{:S(2)}, u32[]{:S(2)}) collective-permute-start(bf16[4,144,128]{2,1,0:T(8,128)(2,1)S(1)} %shard_map.60.refs_4_), channel_id=1, source_target_pairs={{0,24},{1,25},{2,26},{3,27},{4,28},{5,29},{6,30},{7,31},{8,0},{9,1... | collective-permute-start | bytes 442376 | tf_op jit(solution)/shard_map/ppermute | solution.py:384
  87.3 6.1 %collective-permute-start.12 = (bf16[4,144,128]{2,1,0:T(8,128)(2,1)S(1)}, bf16[4,144,128]{2,1,0:T(8,128)(2,1)S(1)}, u32[]{:S(2)}, u32[]{:S(2)}) collective-permute-start(bf16[4,144,128]{2,1,0:T(8,128)(2,1)S(1)} %shard_map.60.refs_4_), channel_id=1, source_target_pairs={{0,16},{1,17},{2,18},{3,19},{4,20},{5,21},{6,22},{7,23},{8,24},{9,... | collective-permute-start | bytes 442376 | tf_op jit(solution)/shard_map/ppermute | solution.py:384
  87.9 9.9 %collective-permute-start.11 = (bf16[4,144,128]{2,1,0:T(8,128)(2,1)S(1)}, bf16[4,144,128]{2,1,0:T(8,128)(2,1)S(1)}, u32[]{:S(2)}, u32[]{:S(2)}) collective-permute-start(bf16[4,144,128]{2,1,0:T(8,128)(2,1)S(1)} %shard_map.60.refs_4_), channel_id=1, source_target_pairs={{0,8},{1,9},{2,10},{3,11},{4,12},{5,13},{6,14},{7,15},{8,16},{9,17... | collective-permute-start | bytes 442376 | tf_op jit(solution)/shard_map/ppermute | solution.py:384
  98.6 1.7 %collective-permute-start.14 = (f32[4,128,128]{2,1,0:T(8,128)S(1)}, f32[4,128,128]{2,1,0:T(8,128)S(1)}, u32[]{:S(2)}, u32[]{:S(2)}) collective-permute-start(f32[4,128,128]{2,1,0:T(8,128)S(1)} %get-tuple-element.40), channel_id=1, source_target_pairs={{0,1},{1,0},{2,3},{3,2},{4,5},{5,4},{6,7},{7,6},{8,9},{9,8},{10,11... | collective-permute-start | bytes 786440 | tf_op jit(solution)/shard_map/ppermute | solution.py:364
  102.5 12.1 %collective-permute-start.20 = (bf16[8,128,128]{2,1,0:T(8,128)(2,1)S(1)}, bf16[8,128,128]{2,1,0:T(8,128)(2,1)S(1)}, u32[]{:S(2)}, u32[]{:S(2)}) collective-permute-start(bf16[8,128,128]{2,1,0:T(8,128)(2,1)S(1)} %get-tuple-element.47), channel_id=1, source_target_pairs={{0,128},{32,160},{64,192},{96,224},{128,0},{160,32},{192,64},{224,... | collective-permute-start | bytes 786440 | tf_op jit(solution)/shard_map/ppermute | solution.py:355
  106.6 33.6 %collective-permute-start.21 = (bf16[8,128,128]{2,1,0:T(8,128)(2,1)S(1)}, bf16[8,128,128]{2,1,0:T(8,128)(2,1)S(1)}, u32[]{:S(2)}, u32[]{:S(2)}) collective-permute-start(bf16[8,128,128]{2,1,0:T(8,128)(2,1)S(1)} %get-tuple-element.48), channel_id=1, source_target_pairs={{0,96},{32,128},{64,160},{96,192},{128,224},{160,0},{192,32},{224,... | collective-permute-start | bytes 786440 | tf_op jit(solution)/shard_map/ppermute | solution.py:355
  109.1 38.9 %collective-permute-start.15 = (bf16[8,128,128]{2,1,0:T(8,128)(2,1)}, bf16[8,128,128]{2,1,0:T(8,128)(2,1)S(1)}, u32[]{:S(2)}, u32[]{:S(2)}) collective-permute-start(bf16[8,128,128]{2,1,0:T(8,128)(2,1)} %get-tuple-element.41), channel_id=1, source_target_pairs={{0,160},{32,192},{64,224},{96,0},{128,32},{160,64},{192,96},{224,1... | collective-permute-start | bytes 786440 | tf_op jit(solution)/shard_map/ppermute | solution.py:355
  111.0 37.0 %collective-permute-start.16 = (bf16[8,128,128]{2,1,0:T(8,128)(2,1)}, bf16[8,128,128]{2,1,0:T(8,128)(2,1)S(1)}, u32[]{:S(2)}, u32[]{:S(2)}) collective-permute-start(bf16[8,128,128]{2,1,0:T(8,128)(2,1)} %get-tuple-element.42), channel_id=1, source_target_pairs={{0,64},{32,96},{64,128},{96,160},{128,192},{160,224},{192,0},{224,... | collective-permute-start | bytes 786440 | tf_op jit(solution)/shard_map/ppermute | solution.py:355
  113.2 36.5 %collective-permute-start.17 = (bf16[8,128,128]{2,1,0:T(8,128)(2,1)}, bf16[8,128,128]{2,1,0:T(8,128)(2,1)S(1)}, u32[]{:S(2)}, u32[]{:S(2)}) collective-permute-start(bf16[8,128,128]{2,1,0:T(8,128)(2,1)} %get-tuple-element.43), channel_id=1, source_target_pairs={{0,192},{32,224},{64,0},{96,32},{128,64},{160,96},{192,128},{224,1... | collective-permute-start | bytes 786440 | tf_op jit(solution)/shard_map/ppermute | solution.py:355
  114.6 39.3 %collective-permute-start.18 = (bf16[8,128,128]{2,1,0:T(8,128)(2,1)S(1)}, bf16[8,128,128]{2,1,0:T(8,128)(2,1)S(1)}, u32[]{:S(2)}, u32[]{:S(2)}) collective-permute-start(bf16[8,128,128]{2,1,0:T(8,128)(2,1)S(1)} %get-tuple-element.44), channel_id=1, source_target_pairs={{0,32},{32,64},{64,96},{96,128},{128,160},{160,192},{192,224},{224... | collective-permute-start | bytes 786440 | tf_op jit(solution)/shard_map/ppermute | solution.py:355
  140.1 13.8 %collective-permute-start.19 = (bf16[8,128,128]{2,1,0:T(8,128)(2,1)S(1)}, bf16[8,128,128]{2,1,0:T(8,128)(2,1)S(1)}, u32[]{:S(2)}, u32[]{:S(2)}) collective-permute-start(bf16[8,128,128]{2,1,0:T(8,128)(2,1)S(1)} %get-tuple-element.45), channel_id=1, source_target_pairs={{0,224},{32,0},{64,32},{96,64},{128,96},{160,128},{192,160},{224,1... | collective-permute-start | bytes 786440 | tf_op jit(solution)/shard_map/ppermute | solution.py:355
  140.3 2.2 %copy-start.1 = (bf16[128,16384]{1,0:T(8,128)(2,1)S(1)}, bf16[128,16384]{1,0:T(8,128)(2,1)}, u32[]{:S(2)}) copy-start(bf16[128,16384]{1,0:T(8,128)(2,1)} %copy-done) | copy-start | bytes 12582916
  142.5 2.2 %copy-start.3 = (f32[128,8192]{1,0:T(8,128)S(1)}, f32[128,8192]{1,0:T(8,128)}, u32[]{:S(2)}) copy-start(f32[128,8192]{1,0:T(8,128)} %copy-done.2) | copy-start | bytes 12582916

commit v2 on v1

--- a/solution.py
+++ b/solution.py
@@ -22,7 +22,8 @@
 BF16 = jnp.bfloat16
 ORDER = (4, 3, 5, 2, 6, 1, 7)
 LISTED = (6, 1, 7, 4, 3, 5, 2)
-SENDS = ((4, 3, 5), (2, 6, 1, 7, 0))
+SENDS = ((4, 3), (5, 2, 6, 1, 7, 0))
+STEPS = (0, 1, 3, 2)
 GROUPS = ((0, 4, 3), (5, 2, 6, 1, 7))
 TAIL = 8
 TAIL16 = 16
@@ -191,7 +192,7 @@
 
 
 def behind(at, n):
-    return [lax.rem(at + n - k, n) for k in range(n)]
+    return [lax.rem(at + n - k, n) for k in STEPS]
 
 
 def ordered(core, mine_ref, got_ref, i):
@@ -385,7 +386,7 @@
 
 
 def around(a, move, n):
-    return [a] + [move(a, k) for k in range(1, n)]
+    return [a] + [move(a, k) for k in STEPS[1:]]
 
 
 def local(queries, key_rows, value_rows, log_decay, initial_state):

time: 159 us -> 153 us (0.962)
  waiting for transfers between devices: 66 us -> 53.2 us
  starting transfers between devices: 53.2 us -> 58.4 us
    ppermute x14, waiting for transfers between devices: 38.2 us -> 34.1 us  [send(): lax.ppermute(pieces[t], 'head', [(i, (i + t) % NZ) for i in range(NZ)])]
    ppermute x3, waiting for transfers between devices: 9.31 us -> 5.4 us  [from_x(): return lax.ppermute(a, 'seq', pairs)]
    ppermute x3, waiting for transfers between devices: 9.39 us -> 5.71 us  [from_y(): return lax.ppermute(a, 'seq', pairs)]
    ppermute x14, starting transfers between devices: 34.4 us -> 37.2 us  [send(): lax.ppermute(pieces[t], 'head', [(i, (i + t) % NZ) for i in range(NZ)])]
  transfers between devices with their start and end apart: 23 -> 23, of which waited for: 14 -> 13; matrix products, arithmetic and copies ran while one was open for 1% -> 1% of each run, Pallas kernels for 12% -> 12%
where the time goes in v2:
time: 153 us
  starting transfers between devices  58.4 us (38%)
  waiting for transfers between devices  53.2 us (35%)
  Pallas kernels  32 us (21%)
  local copies, waits for them, and re-layouts  7.66 us (5%)
    ppermute x14, starting transfers between devices, send(): lax.ppermute(pieces[t], 'head', [(i, (i + t) % NZ) for i in range(NZ)])  37.2 us
    ppermute x14, waiting for transfers between devices, send(): lax.ppermute(pieces[t], 'head', [(i, (i + t) % NZ) for i in range(NZ)])  34.1 us
    pallas_call x1, Pallas kernels, intra(): pl.pallas_call(intra_kernel, grid=(NZ,), in_specs=[BLOCK, BLOCK, BLOCK, p...  9.53 us
    all_to_all x1, starting transfers between devices, local(): ld = lax.all_to_all(by_block, 'head', 0, 0, tiled=True)  9.01 us
    pallas_call x2, Pallas kernels, block_states(): pl.pallas_call(functools.partial(state_kernel, count), grid_spec=pltpu.Pr...  8.87 us
    pallas_call x2, Pallas kernels, finish(): pl.pallas_call(functools.partial(finish_kernel, count), grid_spec=pltpu.P...  8.29 us
    unnamed x12, local copies, waits for them, and re-layouts  7.32 us
    all_to_all x1, waiting for transfers between devices, local(): ld = lax.all_to_all(by_block, 'head', 0, 0, tiled=True)  5.73 us
  transfers between devices with their start and end apart: 23, of which 13 were waited for; matrix products, arithmetic and copies ran while one was open for 1% of the time, Pallas kernels for 12%

profile of v2, /device:TPU:1, one launch (start us, length us, event | category | flops | bytes accessed | tf_op | source)
XLA Modules:
  0.0 152.8 jit_solution(2365194197271939794)
XLA Ops:
  0.0 9.0 %all-to-all-start = ((f32[8,8,128]{2,1,0:T(8,128)}), f32[8,8,128]{2,1,0:T(8,128)S(1)}, u32[]{:S(2)}, u32[]{:S(2)}) async-start(f32[8,8,128]{2,1,0:T(8,128)} %bitcast.19), calls=%async_computation | async-start | bytes 65536 | tf_op jit(solution)/shard_map/all_to_all | solution.py:400
  10.2 5.7 %all-to-all-done.ld_ref = f32[8,8,128]{2,1,0:T(8,128)S(1)} async-done(((f32[8,8,128]{2,1,0:T(8,128)}), f32[8,8,128]{2,1,0:T(8,128)S(1)}, u32[]{:S(2)}, u32[]{:S(2)}) %all-to-all-start) | async-done | bytes 32800 | tf_op jit(solution)/shard_map/all_to_all | solution.py:400
  15.9 2.7 %shard_map.57 = (bf16[8,128,128]{2,1,0:T(8,128)(2,1)S(1)}, bf16[8,128,128]{2,1,0:T(8,128)(2,1)S(1)}) custom-call(s32[2]{0:T(128)S(1)} %pad_add_fusion.1.chunks, bf16[128,8192]{1,0:T(8,128)(2,1)} %k_ref.5, bf16[128,8192]{1,0:T(8,128)(2,1)} %v_ref.5, f32[8,8,128]{2,1,0:T(8,128)S(1)} %all-to-all-done.ld_ref), custom_call_target="tpu_custom_call" | custom-call | flops 134217728 | bytes 1600000 | tf_op jit(solution)/shard_map/pallas_call | solution.py:92
  19.3 2.7 %collective-permute-start.4 = (bf16[8,128,128]{2,1,0:T(8,128)(2,1)S(1)}, bf16[8,128,128]{2,1,0:T(8,128)(2,1)S(1)}, u32[]{:S(2)}, u32[]{:S(2)}) collective-permute-start(bf16[8,128,128]{2,1,0:T(8,128)(2,1)S(1)} %get-tuple-element.34), channel_id=1, source_target_pairs={{0,96},{32,128},{64,160},{96,192},{128,224},{160,0},{192,32},{224,... | collective-permute-start | bytes 786440 | tf_op jit(solution)/shard_map/ppermute | solution.py:356
  22.1 6.1 %shard_map.55 = (bf16[8,128,128]{2,1,0:T(8,128)(2,1)S(1)}, bf16[8,128,128]{2,1,0:T(8,128)(2,1)S(1)}, bf16[8,128,128]{2,1,0:T(8,128)(2,1)}, bf16[8,128,128]{2,1,0...) custom-call(s32[6]{0:T(128)S(1)} %stack.69.chunks, bf16[128,8192]{1,0:T(8,128)(2,1)} %k_ref.5, ...), custom_call_target="tpu_custom_call" | custom-call | flops 402653184 | bytes 4800000 | tf_op jit(solution)/shard_map/pallas_call | solution.py:92
  28.2 1.7 %collective-permute-start = (bf16[8,128,128]{2,1,0:T(8,128)(2,1)}, bf16[8,128,128]{2,1,0:T(8,128)(2,1)S(1)}, u32[]{:S(2)}, u32[]{:S(2)}) collective-permute-start(bf16[8,128,128]{2,1,0:T(8,128)(2,1)} %get-tuple-element.30), channel_id=1, source_target_pairs={{0,192},{32,224},{64,0},{96,32},{128,64},{160,96},{192,128},{224,1... | collective-permute-start | bytes 786440 | tf_op jit(solution)/shard_map/ppermute | solution.py:356
  31.0 1.5 %collective-permute-start.2 = (bf16[8,128,128]{2,1,0:T(8,128)(2,1)S(1)}, bf16[8,128,128]{2,1,0:T(8,128)(2,1)S(1)}, u32[]{:S(2)}, u32[]{:S(2)}) collective-permute-start(bf16[8,128,128]{2,1,0:T(8,128)(2,1)S(1)} %get-tuple-element.32), channel_id=1, source_target_pairs={{0,224},{32,0},{64,32},{96,64},{128,96},{160,128},{192,160},{224,1... | collective-permute-start | bytes 786440 | tf_op jit(solution)/shard_map/ppermute | solution.py:356
  32.6 2.5 %collective-permute-start.5 = (bf16[8,128,128]{2,1,0:T(8,128)(2,1)S(1)}, bf16[8,128,128]{2,1,0:T(8,128)(2,1)S(1)}, u32[]{:S(2)}, u32[]{:S(2)}) collective-permute-start(bf16[8,128,128]{2,1,0:T(8,128)(2,1)S(1)} %get-tuple-element.35), channel_id=1, source_target_pairs={{0,160},{32,192},{64,224},{96,0},{128,32},{160,64},{192,96},{224,1... | collective-permute-start | bytes 786440 | tf_op jit(solution)/shard_map/ppermute | solution.py:356
  35.1 14.4 %collective-permute-done.4.refs_5_ = bf16[8,128,128]{2,1,0:T(8,128)(2,1)S(1)} collective-permute-done((bf16[8,128,128]{2,1,0:T(8,128)(2,1)S(1)}, bf16[8,128,128]{2,1,0:T(8,128)(2,1)S(1)}, u32[]{:S(2)}, u32[]{:S(2)}) %collective-permute-start.4) | collective-permute-done | bytes 262176 | tf_op jit(solution)/shard_map/ppermute | solution.py:356
  49.5 3.0 %collective-permute-start.6 = (bf16[8,128,128]{2,1,0:T(8,128)(2,1)S(1)}, bf16[8,128,128]{2,1,0:T(8,128)(2,1)S(1)}, u32[]{:S(2)}, u32[]{:S(2)}) collective-permute-start(bf16[8,128,128]{2,1,0:T(8,128)(2,1)S(1)} %get-tuple-element.36), channel_id=1, source_target_pairs={{0,64},{32,96},{64,128},{96,160},{128,192},{160,224},{192,0},{224,... | collective-permute-start | bytes 786440 | tf_op jit(solution)/shard_map/ppermute | solution.py:356
  52.7 9.5 %shard_map.56 = (f32[128,8192]{1,0:T(8,128)S(1)}, bf16[128,16384]{1,0:T(8,128)(2,1)S(1)}) custom-call(bf16[128,8192]{1,0:T(8,128)(2,1)} %q_ref.1, bf16[128,8192]{1,0:T(8,128)(2,1)} %k_ref.5, bf16[128,8192]{1,0:T(8,128)(2,1)} %v_ref.5, f32[8,8,128]{2,1,0:T(8,128)S(1)} %all-to-all-done.ld_ref, bf16[8,128,128]{2,1,0:T(8,128)(2,1)S(1)} %get-tuple-element.27.after_ref.refs_0_), custom_call_target="tpu_custom_call" | custom-call | flops 805306368 | bytes 14680064 | tf_op jit(solution)/shard_map/pallas_call | solution.py:131
  62.3 1.9 %copy-done.2 = f32[128,8192]{1,0:T(8,128)} copy-done((f32[128,8192]{1,0:T(8,128)}, f32[128,8192]{1,0:T(8,128)S(1)}, u32[]{:S(2)}) %copy-start.2) | copy-done | bytes 4194328
  69.2 3.0 %collective-permute-start.10 = (bf16[4,144,128]{2,1,0:T(8,128)(2,1)S(1)}, bf16[4,144,128]{2,1,0:T(8,128)(2,1)S(1)}, u32[]{:S(2)}, u32[]{:S(2)}) collective-permute-start(bf16[4,144,128]{2,1,0:T(8,128)(2,1)S(1)} %shard_map.59.refs_0_), channel_id=1, source_target_pairs={{0,4},{1,5},{2,6},{3,7},{4,0},{5,1},{6,2},{7,3},{8,12},{9,13},{10,... | collective-permute-start | bytes 442376 | tf_op jit(solution)/shard_map/ppermute | solution.py:375
  73.6 2.2 %collective-permute-done.10.refs_3_ = bf16[4,144,128]{2,1,0:T(8,128)(2,1)S(1)} collective-permute-done((bf16[4,144,128]{2,1,0:T(8,128)(2,1)S(1)}, bf16[4,144,128]{2,1,0:T(8,128)(2,1)S(1)}, u32[]{:S(2)}, u32[]{:S(2)}) %collective-permute-start.10) | collective-permute-done | bytes 147488 | tf_op jit(solution)/shard_map/ppermute | solution.py:375
  75.8 3.5 %collective-permute-done.9.refs_2_ = bf16[4,144,128]{2,1,0:T(8,128)(2,1)S(1)} collective-permute-done((bf16[4,144,128]{2,1,0:T(8,128)(2,1)S(1)}, bf16[4,144,128]{2,1,0:T(8,128)(2,1)S(1)}, u32[]{:S(2)}, u32[]{:S(2)}) %collective-permute-start.9) | collective-permute-done | bytes 147488 | tf_op jit(solution)/shard_map/ppermute | solution.py:375
  80.1 2.8 %collective-permute-start.13 = (bf16[4,144,128]{2,1,0:T(8,128)(2,1)S(1)}, bf16[4,144,128]{2,1,0:T(8,128)(2,1)S(1)}, u32[]{:S(2)}, u32[]{:S(2)}) collective-permute-start(bf16[4,144,128]{2,1,0:T(8,128)(2,1)S(1)} %shard_map.60.refs_4_), channel_id=1, source_target_pairs={{0,16},{1,17},{2,18},{3,19},{4,20},{5,21},{6,22},{7,23},{8,24},{9,... | collective-permute-start | bytes 442376 | tf_op jit(solution)/shard_map/ppermute | solution.py:385
  85.6 3.2 %collective-permute-done.12.refs_6_ = bf16[4,144,128]{2,1,0:T(8,128)(2,1)S(1)} collective-permute-done((bf16[4,144,128]{2,1,0:T(8,128)(2,1)S(1)}, bf16[4,144,128]{2,1,0:T(8,128)(2,1)S(1)}, u32[]{:S(2)}, u32[]{:S(2)}) %collective-permute-start.12) | collective-permute-done | bytes 147488 | tf_op jit(solution)/shard_map/ppermute | solution.py:385
  90.6 2.4 %collective-permute-start.14 = (f32[4,128,128]{2,1,0:T(8,128)S(1)}, f32[4,128,128]{2,1,0:T(8,128)S(1)}, u32[]{:S(2)}, u32[]{:S(2)}) collective-permute-start(f32[4,128,128]{2,1,0:T(8,128)S(1)} %get-tuple-element.40), channel_id=1, source_target_pairs={{0,1},{1,0},{2,3},{3,2},{4,5},{5,4},{6,7},{7,6},{8,9},{9,8},{10,11... | collective-permute-start | bytes 786440 | tf_op jit(solution)/shard_map/ppermute | solution.py:365
  94.1 2.1 %shard_map.62 = (bf16[8,128,128]{2,1,0:T(8,128)(2,1)S(1)}, bf16[8,128,128]{2,1,0:T(8,128)(2,1)}, bf16[8,128,128]{2,1,0:T(8,128)(2,1)S(1)}, bf16[8,128,128]{2,1,0...) custom-call(s32[4]{0:T(128)S(1)} %pad_add_fusion.place, ...), custom_call_target="tpu_custom_call" | custom-call | flops 2097152 | bytes 5242880 | tf_op jit(solution)/shard_map/pallas_call | solution.py:290
  96.3 4.8 %collective-permute-start.20 = (bf16[8,128,128]{2,1,0:T(8,128)(2,1)S(1)}, bf16[8,128,128]{2,1,0:T(8,128)(2,1)S(1)}, u32[]{:S(2)}, u32[]{:S(2)}) collective-permute-start(bf16[8,128,128]{2,1,0:T(8,128)(2,1)S(1)} %get-tuple-element.47), channel_id=1, source_target_pairs={{0,128},{32,160},{64,192},{96,224},{128,0},{160,32},{192,64},{224,... | collective-permute-start | bytes 786440 | tf_op jit(solution)/shard_map/ppermute | solution.py:356
  101.1 2.7 %collective-permute-start.21 = (bf16[8,128,128]{2,1,0:T(8,128)(2,1)S(1)}, bf16[8,128,128]{2,1,0:T(8,128)(2,1)S(1)}, u32[]{:S(2)}, u32[]{:S(2)}) collective-permute-start(bf16[8,128,128]{2,1,0:T(8,128)(2,1)S(1)} %get-tuple-element.48), channel_id=1, source_target_pairs={{0,96},{32,128},{64,160},{96,192},{128,224},{160,0},{192,32},{224,... | collective-permute-start | bytes 786440 | tf_op jit(solution)/shard_map/ppermute | solution.py:356
  103.8 1.7 %collective-permute-start.15 = (bf16[8,128,128]{2,1,0:T(8,128)(2,1)}, bf16[8,128,128]{2,1,0:T(8,128)(2,1)S(1)}, u32[]{:S(2)}, u32[]{:S(2)}) collective-permute-start(bf16[8,128,128]{2,1,0:T(8,128)(2,1)} %get-tuple-element.41), channel_id=1, source_target_pairs={{0,160},{32,192},{64,224},{96,0},{128,32},{160,64},{192,96},{224,1... | collective-permute-start | bytes 786440 | tf_op jit(solution)/shard_map/ppermute | solution.py:356
  105.5 2.0 %collective-permute-start.16 = (bf16[8,128,128]{2,1,0:T(8,128)(2,1)}, bf16[8,128,128]{2,1,0:T(8,128)(2,1)S(1)}, u32[]{:S(2)}, u32[]{:S(2)}) collective-permute-start(bf16[8,128,128]{2,1,0:T(8,128)(2,1)} %get-tuple-element.42), channel_id=1, source_target_pairs={{0,64},{32,96},{64,128},{96,160},{128,192},{160,224},{192,0},{224,... | collective-permute-start | bytes 786440 | tf_op jit(solution)/shard_map/ppermute | solution.py:356
  107.6 1.5 collective-permute-start.17
  109.1 11.1 %collective-permute-start.18 = (bf16[8,128,128]{2,1,0:T(8,128)(2,1)S(1)}, bf16[8,128,128]{2,1,0:T(8,128)(2,1)S(1)}, u32[]{:S(2)}, u32[]{:S(2)}) collective-permute-start(bf16[8,128,128]{2,1,0:T(8,128)(2,1)S(1)} %get-tuple-element.44), channel_id=1, source_target_pairs={{0,32},{32,64},{64,96},{96,128},{128,160},{160,192},{192,224},{224... | collective-permute-start | bytes 786440 | tf_op jit(solution)/shard_map/ppermute | solution.py:356
  120.2 14.2 %collective-permute-done.21.refs_2_ = bf16[8,128,128]{2,1,0:T(8,128)(2,1)S(1)} collective-permute-done((bf16[8,128,128]{2,1,0:T(8,128)(2,1)S(1)}, bf16[8,128,128]{2,1,0:T(8,128)(2,1)S(1)}, u32[]{:S(2)}, u32[]{:S(2)}) %collective-permute-start.21) | collective-permute-done | bytes 262176 | tf_op jit(solution)/shard_map/ppermute | solution.py:356
  134.6 2.2 %copy-done.1 = bf16[128,16384]{1,0:T(8,128)(2,1)S(1)} copy-done((bf16[128,16384]{1,0:T(8,128)(2,1)S(1)}, bf16[128,16384]{1,0:T(8,128)(2,1)}, u32[]{:S(2)}) %copy-start.1) | copy-done | bytes 4194328
  136.8 2.2 %copy-done.3 = f32[128,8192]{1,0:T(8,128)S(1)} copy-done((f32[128,8192]{1,0:T(8,128)S(1)}, f32[128,8192]{1,0:T(8,128)}, u32[]{:S(2)}) %copy-start.3) | copy-done | bytes 4194328
  138.9 3.4 %shard_map.63.refs_5_ = bf16[128,8192]{1,0:T(8,128)(2,1)} custom-call(s32[3]{0:T(128)S(1)} %pad_add_fusion.2.chunks, bf16[128,16384]{1,0:T(8,128)(2,1)S(1)} %copy-done.1, f32[128,8192]{1,0:T(8,128)S(1)} %copy-done.3, bf16[8,128,128]{2,1,0:T(8,128)(2,1)S(1)} %get-tuple-element.46.refs_0_, bf16[8,128,128]{2,1,0:T(8,128)(2,1)S(1)} %collective-permute-done.20.refs_1_, ...), custom_call_target="tpu_custom_call" | custom-call | flops 201326592 | bytes 4500000 | tf_op jit(solution)/shard_map/pallas_call | solution.py:338
  142.4 2.0 %collective-permute-done.17.refs_2_ = bf16[8,128,128]{2,1,0:T(8,128)(2,1)S(1)} collective-permute-done((bf16[8,128,128]{2,1,0:T(8,128)(2,1)}, bf16[8,128,128]{2,1,0:T(8,128)(2,1)S(1)}, u32[]{:S(2)}, u32[]{:S(2)}) %collective-permute-start.17) | collective-permute-done | bytes 262176 | tf_op jit(solution)/shard_map/ppermute | solution.py:356
  144.3 3.4 %collective-permute-done.18.refs_3_ = bf16[8,128,128]{2,1,0:T(8,128)(2,1)S(1)} collective-permute-done((bf16[8,128,128]{2,1,0:T(8,128)(2,1)S(1)}, bf16[8,128,128]{2,1,0:T(8,128)(2,1)S(1)}, u32[]{:S(2)}, u32[]{:S(2)}) %collective-permute-start.18) | collective-permute-done | bytes 262176 | tf_op jit(solution)/shard_map/ppermute | solution.py:356
  147.9 4.9 %shard_map.64 = bf16[128,8192]{1,0:T(8,128)(2,1)} custom-call(s32[5]{0:T(128)S(1)} %stack.66.chunks, bf16[128,16384]{1,0:T(8,128)(2,1)S(1)} %copy-done.1, f32[128,8192]{1,0:T(8,128)S(1)} %copy-done.3, bf16[8,128,128]{2,1,0:T(8,128)(2,1)S(1)} %collective-permute-done.15.refs_0_, ...), custom_call_target="tpu_custom_call", output_to_operand_aliasing={{}: (8, {})} | custom-call | flops 335544320 | bytes 7500000 | tf_op jit(solution)/shard_map/pallas_call | solution.py:338
  (49 shorter events, 16.2 us)
Async XLA Ops:
  0.0 15.9 %all-to-all-start = ((f32[8,8,128]{2,1,0:T(8,128)}), f32[8,8,128]{2,1,0:T(8,128)S(1)}, u32[]{:S(2)}, u32[]{:S(2)}) async-start(f32[8,8,128]{2,1,0:T(8,128)} %bitcast.19), calls=%async_computation | async-start | bytes 65536 | tf_op jit(solution)/shard_map/all_to_all | solution.py:400
  10.2 11.8 %copy-start.5 = (f32[1024,8]{0,1:T(8,128)S(1)}, f32[1024,8]{0,1:T(8,128)}, u32[]{:S(2)}) copy-start(f32[1024,8]{0,1:T(8,128)} %param.8) | copy-start | bytes 98308
  18.6 13.9 %collective-permute-start.3 = (bf16[8,128,128]{2,1,0:T(8,128)(2,1)S(1)}, bf16[8,128,128]{2,1,0:T(8,128)(2,1)S(1)}, u32[]{:S(2)}, u32[]{:S(2)}) collective-permute-start(bf16[8,128,128]{2,1,0:T(8,128)(2,1)S(1)} %get-tuple-element.33), channel_id=1, source_target_pairs={{0,128},{32,160},{64,192},{96,224},{128,0},{160,32},{192,64},{224,... | collective-permute-start | bytes 786440 | tf_op jit(solution)/shard_map/ppermute | solution.py:356
  19.3 30.2 %collective-permute-start.4 = (bf16[8,128,128]{2,1,0:T(8,128)(2,1)S(1)}, bf16[8,128,128]{2,1,0:T(8,128)(2,1)S(1)}, u32[]{:S(2)}, u32[]{:S(2)}) collective-permute-start(bf16[8,128,128]{2,1,0:T(8,128)(2,1)S(1)} %get-tuple-element.34), channel_id=1, source_target_pairs={{0,96},{32,128},{64,160},{96,192},{128,224},{160,0},{192,32},{224,... | collective-permute-start | bytes 786440 | tf_op jit(solution)/shard_map/ppermute | solution.py:356
  28.2 36.0 %collective-permute-start = (bf16[8,128,128]{2,1,0:T(8,128)(2,1)}, bf16[8,128,128]{2,1,0:T(8,128)(2,1)S(1)}, u32[]{:S(2)}, u32[]{:S(2)}) collective-permute-start(bf16[8,128,128]{2,1,0:T(8,128)(2,1)} %get-tuple-element.30), channel_id=1, source_target_pairs={{0,192},{32,224},{64,0},{96,32},{128,64},{160,96},{192,128},{224,1... | collective-permute-start | bytes 786440 | tf_op jit(solution)/shard_map/ppermute | solution.py:356
  29.9 34.4 %collective-permute-start.1 = (bf16[8,128,128]{2,1,0:T(8,128)(2,1)S(1)}, bf16[8,128,128]{2,1,0:T(8,128)(2,1)S(1)}, u32[]{:S(2)}, u32[]{:S(2)}) collective-permute-start(bf16[8,128,128]{2,1,0:T(8,128)(2,1)S(1)} %get-tuple-element.31), channel_id=1, source_target_pairs={{0,32},{32,64},{64,96},{96,128},{128,160},{160,192},{192,224},{224... | collective-permute-start | bytes 786440 | tf_op jit(solution)/shard_map/ppermute | solution.py:356
  31.0 33.2 %collective-permute-start.2 = (bf16[8,128,128]{2,1,0:T(8,128)(2,1)S(1)}, bf16[8,128,128]{2,1,0:T(8,128)(2,1)S(1)}, u32[]{:S(2)}, u32[]{:S(2)}) collective-permute-start(bf16[8,128,128]{2,1,0:T(8,128)(2,1)S(1)} %get-tuple-element.32), channel_id=1, source_target_pairs={{0,224},{32,0},{64,32},{96,64},{128,96},{160,128},{192,160},{224,1... | collective-permute-start | bytes 786440 | tf_op jit(solution)/shard_map/ppermute | solution.py:356
  32.6 31.7 %collective-permute-start.5 = (bf16[8,128,128]{2,1,0:T(8,128)(2,1)S(1)}, bf16[8,128,128]{2,1,0:T(8,128)(2,1)S(1)}, u32[]{:S(2)}, u32[]{:S(2)}) collective-permute-start(bf16[8,128,128]{2,1,0:T(8,128)(2,1)S(1)} %get-tuple-element.35), channel_id=1, source_target_pairs={{0,160},{32,192},{64,224},{96,0},{128,32},{160,64},{192,96},{224,1... | collective-permute-start | bytes 786440 | tf_op jit(solution)/shard_map/ppermute | solution.py:356
  49.5 14.8 %collective-permute-start.6 = (bf16[8,128,128]{2,1,0:T(8,128)(2,1)S(1)}, bf16[8,128,128]{2,1,0:T(8,128)(2,1)S(1)}, u32[]{:S(2)}, u32[]{:S(2)}) collective-permute-start(bf16[8,128,128]{2,1,0:T(8,128)(2,1)S(1)} %get-tuple-element.36), channel_id=1, source_target_pairs={{0,64},{32,96},{64,128},{96,160},{128,192},{160,224},{192,0},{224,... | collective-permute-start | bytes 786440 | tf_op jit(solution)/shard_map/ppermute | solution.py:356
  62.3 2.0 %copy-start.2 = (f32[128,8192]{1,0:T(8,128)}, f32[128,8192]{1,0:T(8,128)S(1)}, u32[]{:S(2)}) copy-start(f32[128,8192]{1,0:T(8,128)S(1)} %get-tuple-element.29.o_ref) | copy-start | bytes 12582916
  64.2 2.0 %copy-start = (bf16[128,16384]{1,0:T(8,128)(2,1)}, bf16[128,16384]{1,0:T(8,128)(2,1)S(1)}, u32[]{:S(2)}) copy-start(bf16[128,16384]{1,0:T(8,128)(2,1)S(1)} %get-tuple-element.28.refs_8_.qd_ref) | copy-start | bytes 12582916
  64.3 25.5 %copy-start.4 = (f32[8,128,128]{2,1,0:T(8,128)S(1)}, f32[8,128,128]{2,1,0:T(8,128)}, u32[]{:S(2)}) copy-start(f32[8,128,128]{2,1,0:T(8,128)} %start_ref.1) | copy-start | bytes 1572868
  66.2 2.3 %collective-permute-start.7 = (f32[4,136,128]{2,1,0:T(8,128)S(1)}, f32[4,136,128]{2,1,0:T(8,128)S(1)}, u32[]{:S(2)}, u32[]{:S(2)}) collective-permute-start(f32[4,136,128]{2,1,0:T(8,128)S(1)} %get-tuple-element.38), channel_id=1, source_target_pairs={{0,1},{1,0},{2,3},{3,2},{4,5},{5,4},{6,7},{7,6},{8,9},{9,8},{10,11... | collective-permute-start | bytes 835592 | tf_op jit(solution)/shard_map/ppermute | solution.py:365
  69.2 6.7 %collective-permute-start.10 = (bf16[4,144,128]{2,1,0:T(8,128)(2,1)S(1)}, bf16[4,144,128]{2,1,0:T(8,128)(2,1)S(1)}, u32[]{:S(2)}, u32[]{:S(2)}) collective-permute-start(bf16[4,144,128]{2,1,0:T(8,128)(2,1)S(1)} %shard_map.59.refs_0_), channel_id=1, source_target_pairs={{0,4},{1,5},{2,6},{3,7},{4,0},{5,1},{6,2},{7,3},{8,12},{9,13},{10,... | collective-permute-start | bytes 442376 | tf_op jit(solution)/shard_map/ppermute | solution.py:375
  72.2 7.2 %collective-permute-start.9 = (bf16[4,144,128]{2,1,0:T(8,128)(2,1)S(1)}, bf16[4,144,128]{2,1,0:T(8,128)(2,1)S(1)}, u32[]{:S(2)}, u32[]{:S(2)}) collective-permute-start(bf16[4,144,128]{2,1,0:T(8,128)(2,1)S(1)} %shard_map.59.refs_0_), channel_id=1, source_target_pairs={{0,6},{1,7},{2,0},{3,1},{4,2},{5,3},{6,4},{7,5},{8,14},{9,15},{10,... | collective-permute-start | bytes 442376 | tf_op jit(solution)/shard_map/ppermute | solution.py:375
  72.9 6.4 %collective-permute-start.8 = (bf16[4,144,128]{2,1,0:T(8,128)(2,1)S(1)}, bf16[4,144,128]{2,1,0:T(8,128)(2,1)S(1)}, u32[]{:S(2)}, u32[]{:S(2)}) collective-permute-start(bf16[4,144,128]{2,1,0:T(8,128)(2,1)S(1)} %shard_map.59.refs_0_), channel_id=1, source_target_pairs={{0,2},{1,3},{2,4},{3,5},{4,6},{5,7},{6,0},{7,1},{8,10},{9,11},{10,... | collective-permute-start | bytes 442376 | tf_op jit(solution)/shard_map/ppermute | solution.py:375
  80.1 5.6 %collective-permute-start.13 = (bf16[4,144,128]{2,1,0:T(8,128)(2,1)S(1)}, bf16[4,144,128]{2,1,0:T(8,128)(2,1)S(1)}, u32[]{:S(2)}, u32[]{:S(2)}) collective-permute-start(bf16[4,144,128]{2,1,0:T(8,128)(2,1)S(1)} %shard_map.60.refs_4_), channel_id=1, source_target_pairs={{0,16},{1,17},{2,18},{3,19},{4,20},{5,21},{6,22},{7,23},{8,24},{9,... | collective-permute-start | bytes 442376 | tf_op jit(solution)/shard_map/ppermute | solution.py:385
  82.9 6.0 %collective-permute-start.12 = (bf16[4,144,128]{2,1,0:T(8,128)(2,1)S(1)}, bf16[4,144,128]{2,1,0:T(8,128)(2,1)S(1)}, u32[]{:S(2)}, u32[]{:S(2)}) collective-permute-start(bf16[4,144,128]{2,1,0:T(8,128)(2,1)S(1)} %shard_map.60.refs_4_), channel_id=1, source_target_pairs={{0,24},{1,25},{2,26},{3,27},{4,28},{5,29},{6,30},{7,31},{8,0},{9,1... | collective-permute-start | bytes 442376 | tf_op jit(solution)/shard_map/ppermute | solution.py:385
  83.8 6.0 %collective-permute-start.11 = (bf16[4,144,128]{2,1,0:T(8,128)(2,1)S(1)}, bf16[4,144,128]{2,1,0:T(8,128)(2,1)S(1)}, u32[]{:S(2)}, u32[]{:S(2)}) collective-permute-start(bf16[4,144,128]{2,1,0:T(8,128)(2,1)S(1)} %shard_map.60.refs_4_), channel_id=1, source_target_pairs={{0,8},{1,9},{2,10},{3,11},{4,12},{5,13},{6,14},{7,15},{8,16},{9,17... | collective-permute-start | bytes 442376 | tf_op jit(solution)/shard_map/ppermute | solution.py:385
  90.6 3.5 %collective-permute-start.14 = (f32[4,128,128]{2,1,0:T(8,128)S(1)}, f32[4,128,128]{2,1,0:T(8,128)S(1)}, u32[]{:S(2)}, u32[]{:S(2)}) collective-permute-start(f32[4,128,128]{2,1,0:T(8,128)S(1)} %get-tuple-element.40), channel_id=1, source_target_pairs={{0,1},{1,0},{2,3},{3,2},{4,5},{5,4},{6,7},{7,6},{8,9},{9,8},{10,11... | collective-permute-start | bytes 786440 | tf_op jit(solution)/shard_map/ppermute | solution.py:365
  96.3 12.9 %collective-permute-start.20 = (bf16[8,128,128]{2,1,0:T(8,128)(2,1)S(1)}, bf16[8,128,128]{2,1,0:T(8,128)(2,1)S(1)}, u32[]{:S(2)}, u32[]{:S(2)}) collective-permute-start(bf16[8,128,128]{2,1,0:T(8,128)(2,1)S(1)} %get-tuple-element.47), channel_id=1, source_target_pairs={{0,128},{32,160},{64,192},{96,224},{128,0},{160,32},{192,64},{224,... | collective-permute-start | bytes 786440 | tf_op jit(solution)/shard_map/ppermute | solution.py:356
  101.1 33.3 %collective-permute-start.21 = (bf16[8,128,128]{2,1,0:T(8,128)(2,1)S(1)}, bf16[8,128,128]{2,1,0:T(8,128)(2,1)S(1)}, u32[]{:S(2)}, u32[]{:S(2)}) collective-permute-start(bf16[8,128,128]{2,1,0:T(8,128)(2,1)S(1)} %get-tuple-element.48), channel_id=1, source_target_pairs={{0,96},{32,128},{64,160},{96,192},{128,224},{160,0},{192,32},{224,... | collective-permute-start | bytes 786440 | tf_op jit(solution)/shard_map/ppermute | solution.py:356
  103.8 38.6 %collective-permute-start.15 = (bf16[8,128,128]{2,1,0:T(8,128)(2,1)}, bf16[8,128,128]{2,1,0:T(8,128)(2,1)S(1)}, u32[]{:S(2)}, u32[]{:S(2)}) collective-permute-start(bf16[8,128,128]{2,1,0:T(8,128)(2,1)} %get-tuple-element.41), channel_id=1, source_target_pairs={{0,160},{32,192},{64,224},{96,0},{128,32},{160,64},{192,96},{224,1... | collective-permute-start | bytes 786440 | tf_op jit(solution)/shard_map/ppermute | solution.py:356
  105.5 36.8 %collective-permute-start.16 = (bf16[8,128,128]{2,1,0:T(8,128)(2,1)}, bf16[8,128,128]{2,1,0:T(8,128)(2,1)S(1)}, u32[]{:S(2)}, u32[]{:S(2)}) collective-permute-start(bf16[8,128,128]{2,1,0:T(8,128)(2,1)} %get-tuple-element.42), channel_id=1, source_target_pairs={{0,64},{32,96},{64,128},{96,160},{128,192},{160,224},{192,0},{224,... | collective-permute-start | bytes 786440 | tf_op jit(solution)/shard_map/ppermute | solution.py:356
  107.6 36.7 %collective-permute-start.17 = (bf16[8,128,128]{2,1,0:T(8,128)(2,1)}, bf16[8,128,128]{2,1,0:T(8,128)(2,1)S(1)}, u32[]{:S(2)}, u32[]{:S(2)}) collective-permute-start(bf16[8,128,128]{2,1,0:T(8,128)(2,1)} %get-tuple-element.43), channel_id=1, source_target_pairs={{0,192},{32,224},{64,0},{96,32},{128,64},{160,96},{192,128},{224,1... | collective-permute-start | bytes 786440 | tf_op jit(solution)/shard_map/ppermute | solution.py:356
  109.1 38.6 %collective-permute-start.18 = (bf16[8,128,128]{2,1,0:T(8,128)(2,1)S(1)}, bf16[8,128,128]{2,1,0:T(8,128)(2,1)S(1)}, u32[]{:S(2)}, u32[]{:S(2)}) collective-permute-start(bf16[8,128,128]{2,1,0:T(8,128)(2,1)S(1)} %get-tuple-element.44), channel_id=1, source_target_pairs={{0,32},{32,64},{64,96},{96,128},{128,160},{160,192},{192,224},{224... | collective-permute-start | bytes 786440 | tf_op jit(solution)/shard_map/ppermute | solution.py:356
  134.4 13.5 %collective-permute-start.19 = (bf16[8,128,128]{2,1,0:T(8,128)(2,1)S(1)}, bf16[8,128,128]{2,1,0:T(8,128)(2,1)S(1)}, u32[]{:S(2)}, u32[]{:S(2)}) collective-permute-start(bf16[8,128,128]{2,1,0:T(8,128)(2,1)S(1)} %get-tuple-element.45), channel_id=1, source_target_pairs={{0,224},{32,0},{64,32},{96,64},{128,96},{160,128},{192,160},{224,1... | collective-permute-start | bytes 786440 | tf_op jit(solution)/shard_map/ppermute | solution.py:356
  134.6 2.2 %copy-start.1 = (bf16[128,16384]{1,0:T(8,128)(2,1)S(1)}, bf16[128,16384]{1,0:T(8,128)(2,1)}, u32[]{:S(2)}) copy-start(bf16[128,16384]{1,0:T(8,128)(2,1)} %copy-done) | copy-start | bytes 12582916
  136.8 2.2 %copy-start.3 = (f32[128,8192]{1,0:T(8,128)S(1)}, f32[128,8192]{1,0:T(8,128)}, u32[]{:S(2)}) copy-start(f32[128,8192]{1,0:T(8,128)} %copy-done.2) | copy-start | bytes 12582916

commit v3 on v2

--- a/solution.py
+++ b/solution.py
@@ -20,14 +20,10 @@
 HIGHEST = lax.Precision.HIGHEST
 F32 = jnp.float32
 BF16 = jnp.bfloat16
-ORDER = (4, 3, 5, 2, 6, 1, 7)
-LISTED = (6, 1, 7, 4, 3, 5, 2)
-SENDS = ((4, 3), (5, 2, 6, 1, 7, 0))
 STEPS = (0, 1, 3, 2)
-GROUPS = ((0, 4, 3), (5, 2, 6, 1, 7))
+FAR = (3, 2, 1)
 TAIL = 8
 TAIL16 = 16
-
 
 VM = pl.BlockSpec(memory_space=pltpu.VMEM)
 SM = pl.BlockSpec(memory_space=pltpu.SMEM)
@@ -61,6 +57,23 @@
     return lax.dot_general(
         a, b, (((1,), (0,)), ((), ())), precision=HIGHEST, preferred_element_type=F32
     )
+
+
+def near_kernel(ld_ref, out_ref):
+    for j in range(NZ):
+        out_ref[j, :GROUP, :] = ld_ref[j]
+        out_ref[j, GROUP:, :] = ld_ref[j ^ 1]
+
+
+def with_near(ld):
+    return pl.pallas_call(
+        near_kernel,
+        in_specs=[VM],
+        out_specs=VM,
+        out_shape=jax.ShapeDtypeStruct((NZ, 2 * GROUP, ROWS), F32),
+        compiler_params=params(),
+        cost_estimate=cost(0, 1 << 17),
+    )(ld)
 
 
 def state_kernel(count, chunks, k_ref, v_ref, ld_ref, *refs):
@@ -142,32 +155,88 @@
     )(q, k, v, ld, after)
 
 
-def row_kernel(place, w_ref, r_ref, *refs):
-    turns = (0,) + LISTED
-    pieces, sides = refs[:NZ], refs[-2:]
+def signed(place):
+    return 1 - 2 * lax.rem(place[0], 2)
+
+
+def group_at(place, a):
+    return lax.rem(place[0] + 2 * NZ - signed(place) * a, NZ)
+
+
+def pair_behind(place, a):
+    own = place[0] // 2
+    return lax.rem(own + 4 + {1: -1, 2: 1, 3: 2}[a] * signed(place), 4)
+
+
+def join_kernel(a, place, d_ref, keep_ref, got_ref, out_ref):
+    even = lax.rem(place[0], 2) == 0
+    group = group_at(place, a)
+    for h in range(GROUP):
+        keep, got = keep_ref[h].astype(F32), got_ref[h].astype(F32)
+        first, second = jnp.where(even, keep, got), jnp.where(even, got, keep)
+        out_ref[h] = (first * d_ref[group * GROUP + h] + second).astype(BF16)
+
+
+def join(a, place, over_odd, keep, got):
+    return pl.pallas_call(
+        functools.partial(join_kernel, a),
+        in_specs=[SM, SM, VM, VM],
+        out_specs=VM,
+        out_shape=STATE,
+        compiler_params=params(),
+        cost_estimate=cost(GROUP * DH * DH * 4, 800000),
+    )(place, over_odd, keep, got)
+
+
+def part_kernel(a, place, d_ref, start_ref, keep_ref, got_ref, *refs):
+    own_ref, pass_ref = refs[-2:]
+    even = lax.rem(place[0], 2) == 0
+    group = group_at(place, a)
+    for h in range(GROUP):
+        start = start_ref[h].astype(F32)
+        state = jnp.where(even, keep_ref[h].astype(F32), got_ref[h].astype(F32))
+        later = start * d_ref[group * GROUP + h] + state
+        own_ref[h] = jnp.where(even, start, later).astype(BF16)
+        pass_ref[h] = jnp.where(even, later, start).astype(BF16)
+
+
+def part(a, place, over_even, start, keep, got, after):
+    return pl.pallas_call(
+        functools.partial(part_kernel, a),
+        in_specs=[SM, SM, VM, VM, VM] + [ANY] * len(after),
+        out_specs=[VM, VM],
+        out_shape=[STATE, STATE],
+        compiler_params=params(),
+        cost_estimate=cost(GROUP * DH * DH * 4, 1300000),
+    )(place, over_even, start, keep, got, *after)
+
+
+def row_kernel(place, w_ref, r_ref, own_ref, near_ref, *refs):
+    far, sides = refs[: len(FAR)], refs[-2:]
     z, core = place[0], place[1]
+    pieces = [(own_ref, z), (near_ref, z + signed(place))]
+    pieces += [(ref, 2 * pair_behind(place, a) + 1) for a, ref in zip(FAR, far)]
     for ref, side in zip(sides, (core, 1 - core)):
         for i in range(PAIR):
             h = side * PAIR + i
             total = None
-            for k, piece in zip(turns, pieces):
-                block = lax.rem(z + NZ - k, NZ)
+            for piece, block in pieces:
                 term = piece[h].astype(F32) * w_ref[block * GROUP + h]
                 total = term if total is None else total + term
             ref[i, :DH, :] = total
             ref[i, DH:, :] = jnp.full((TAIL, DH), r_ref[h], F32)
 
 
-def row_states(place, weights, rows, pieces, after):
+def row_states(place, weights, rows, pieces):
     shape = jax.ShapeDtypeStruct((PAIR, DH + TAIL, DH), F32)
     return pl.pallas_call(
         row_kernel,
-        in_specs=[SM, SM, SM] + [VM] * NZ + [ANY],
+        in_specs=[SM, SM, SM] + [VM] * len(pieces),
         out_specs=[VM, VM],
         out_shape=[shape, shape],
         compiler_params=params(),
-        cost_estimate=cost(GROUP * DH * DH * 16, 3 << 20),
-    )(place, weights, rows, *pieces, after)
+        cost_estimate=cost(GROUP * DH * DH * 10, 2 << 20),
+    )(place, weights, rows, *pieces)
 
 
 def put(ref, i, state, decay):
@@ -268,35 +337,47 @@
     return keep, swap_core(give)
 
 
-def spread_kernel(place, d_ref, keep_ref, got_ref, *refs):
-    turns = (0,) + LISTED
-    pieces, outs, states, entries = refs[:NZ], refs[NZ : 2 * NZ], refs[-2], refs[-1]
+def spread_kernel(place, d_ref, keep_ref, got_ref, own_ref, near_ref, *refs):
+    far, (out_own, out_near, *out_far) = refs[: len(FAR)], refs[len(FAR) : -2]
+    states, entries = refs[-2], refs[-1]
     z, core = place[0], place[1]
-    for k, piece in zip(turns, pieces):
-        states[lax.rem(z + NZ - k, NZ)] = piece[...]
+    even, own = lax.rem(z, 2) == 0, z // 2
+    for a, ref in zip(FAR, far):
+        states[pair_behind(place, a)] = ref[...].astype(F32)
+    for h in range(GROUP):
+        mine, near = own_ref[h].astype(F32), near_ref[h].astype(F32)
+        first, second = jnp.where(even, mine, near), jnp.where(even, near, mine)
+        states[own, h] = first * d_ref[(2 * own + 1) * GROUP + h] + second
     for ref, side in ((keep_ref, core), (got_ref, 1 - core)):
         for i in range(PAIR):
             h = side * PAIR + i
             state = ref[i]
-            for j in range(NZ):
-                entries[j, h] = state.astype(BF16)
-                if j < NZ - 1:
-                    state = state * d_ref[j * GROUP + h] + states[j, h].astype(F32)
-    for k, out in zip(turns, outs):
-        out[...] = entries[lax.rem(z + k, NZ)]
+            for p in range(NZ // 2):
+                entries[p, h] = state
+                if p < NZ // 2 - 1:
+                    over = d_ref[2 * p * GROUP + h] * d_ref[(2 * p + 1) * GROUP + h]
+                    state = state * over + states[p, h]
+    for a, out in zip(FAR, out_far):
+        out[...] = entries[pair_behind(place, a)].astype(BF16)
+    for h in range(GROUP):
+        start = entries[own, h]
+        first = jnp.where(even, own_ref[h].astype(F32), near_ref[h].astype(F32))
+        later = start * d_ref[2 * own * GROUP + h] + first
+        out_own[h] = jnp.where(even, start, later).astype(BF16)
+        out_near[h] = jnp.where(even, later, start).astype(BF16)
 
 
 def spread(place, decays, keep, got, pieces):
-    outs = pl.pallas_call(
+    count = len(pieces)
+    return pl.pallas_call(
         spread_kernel,
-        in_specs=[SM, SM] + [VM] * (NZ + 2),
-        out_specs=[VM] * NZ,
-        out_shape=[STATE] * NZ,
-        scratch_shapes=[pltpu.VMEM((NZ, GROUP, DH, DH), BF16)] * 2,
+        in_specs=[SM, SM] + [VM] * (2 + count),
+        out_specs=[VM] * count,
+        out_shape=[STATE] * count,
+        scratch_shapes=[pltpu.VMEM((NZ // 2, GROUP, DH, DH), F32)] * 2,
         compiler_params=params(),
         cost_estimate=cost(GROUP * DH * DH * 16, 5 << 20),
     )(place, decays, keep, got, *pieces)
-    return dict(zip((0,) + LISTED, outs))
 
 
 def finish_kernel(count, chunks, qd_ref, o_ref, *refs):
@@ -351,10 +432,20 @@
     )(*args)
 
 
-def send(pieces, turns):
-    return {
-        t: lax.ppermute(pieces[t], "head", [(i, (i + t) % NZ) for i in range(NZ)]) for t in turns
-    }
+def swap_near(a):
+    return lax.ppermute(a, "head", [(i, i ^ 1) for i in range(NZ)])
+
+
+def hops(a):
+    return [(i, (i + (a if i % 2 else -a)) % NZ) for i in range(NZ)]
+
+
+def to_owner(x, a):
+    return lax.ppermute(x, "head", hops(a))
+
+
+def from_owner(x, a):
+    return lax.ppermute(x, "head", [(j, i) for i, j in hops(a)])
 
 
 def seq_index(x, y, core):
@@ -397,7 +488,7 @@
     s = lax.axis_index("seq").astype(jnp.int32)
     place = jnp.stack([z, s % 2, s // (2 * NY), (s // 2) % NY])
     by_block = jnp.swapaxes(log_decay.T.reshape(GROUP, NZ, ROWS), 0, 1)
-    ld = lax.all_to_all(by_block, "head", 0, 0, tiled=True)
+    ld = lax.all_to_all(with_near(by_block), "head", 0, 0, tiled=True)
 
     total = jnp.sum(by_block, axis=2)
     cells = jnp.arange(NZ)
@@ -406,25 +497,50 @@
     decays = jnp.exp(total).reshape(-1)
     rows = jnp.sum(total, axis=0)
 
-    states = {}
-    for turns in SENDS:
-        chunks = jnp.stack([(z + t) % NZ for t in turns])
-        states |= zip(turns, block_states(chunks, len(turns), key_rows, value_rows, ld))
-    come = send(states, ORDER)
-    come = [states[0]] + [come[t] for t in LISTED]
-    o, qd = intra(queries, key_rows, value_rows, ld, states[0])
-
-    mine, give = row_states(place, closing, rows, come, qd)
-    keep, got = seq_scan(place, mine, give, initial_state)
-    leave = spread(place, decays, keep, got, come)
-    back = send(leave, ORDER)
-    back[0] = leave[0]
-
-    out = None
-    for turns in GROUPS:
-        chunks = jnp.stack([(z + NZ - t) % NZ for t in turns])
-        out = finish(chunks, qd, o, [back[t] for t in turns], out)
-    return out
+    sign = 1 - 2 * (z % 2)
+
+    def keeps(*turns):
+        return [(z - sign * a) % NZ for a in turns]
+
+    def gives(*turns):
+        return [(z + sign * a) % NZ for a in turns]
+
+    over = jnp.sum(ld, axis=2)
+    mine_over, near_over = over[:, :GROUP].reshape(-1), over[:, GROUP:].reshape(-1)
+    over_even = jnp.exp(jnp.where(z % 2 == 0, mine_over, near_over))
+    over_odd = jnp.exp(jnp.where(z % 2 == 0, near_over, mine_over))
+
+    give, kept, got, joined = {}, {}, {}, {}
+    give[4], give[3] = block_states(jnp.stack(gives(4, 3)), 2, key_rows, value_rows, ld)
+    kept[3], give[2], give[1] = block_states(
+        jnp.stack(keeps(3) + gives(2, 1)), 3, key_rows, value_rows, ld
+    )
+    kept[2], kept[1], kept[0] = block_states(
+        jnp.stack(keeps(2, 1, 0)), 3, key_rows, value_rows, ld
+    )
+    for a in (3, 2, 1, 0):
+        got[a] = swap_near(give[a + 1])
+    for a in FAR:
+        joined[a] = to_owner(join(a, place, over_odd, kept[a], got[a]), a)
+
+    pieces = [kept[0], got[0]] + [joined[a] for a in FAR]
+    mine, other = row_states(place, closing, rows, pieces)
+    keep, other = seq_scan(place, mine, other, initial_state)
+    entry = {}
+    own, near, *far = spread(place, decays, keep, other, pieces)
+    o, qd = intra(queries, key_rows, value_rows, ld, own)
+    entry[0] = own
+    near = swap_near(near)
+    passed = {}
+    for a, x in zip(FAR, far):
+        entry[a], x = part(a, place, over_even, from_owner(x, a), kept[a], got[a], [qd])
+        passed[a] = swap_near(x)
+
+    early = [entry[0], near, entry[1], entry[2]]
+    out = finish(jnp.stack(keeps(0) + gives(1) + keeps(1, 2)), qd, o, early, None)
+    middle = [entry[3], passed[2], passed[1]]
+    out = finish(jnp.stack(keeps(3) + gives(3, 2)), qd, o, middle, out)
+    return finish(jnp.stack(gives(4)), qd, o, [passed[3]], out)
 
 
 def solution(mesh):

time: 153 us -> 134 us (0.88)
  starting transfers between devices: 58.4 us -> 39.5 us
  Pallas kernels: 32 us -> 41 us
  waiting for transfers between devices: 53.2 us -> 46.4 us
  local copies, waits for them, and re-layouts: 7.66 us -> 4.48 us
    ppermute x14, starting transfers between devices: 37.2 us -> 13.4 us  [the longest x8 8.11 us: swap_near(): return lax.ppermute(a, 'head', [(i, i ^ 1) for i in range(NZ)])]
    ppermute x14, waiting for transfers between devices: 34.1 us -> 25.8 us  [the longest x8 15.2 us: swap_near(): return lax.ppermute(a, 'head', [(i, i ^ 1) for i in range(NZ)])]
    pallas_call x2 -> x9, Pallas kernels: 3.08 us -> 8.8 us  [the longest x3 3.43 us: join(): pl.pallas_call(functools.partial(join_kernel, a), in_specs=[SM, SM, VM, V...]
    ppermute x2, starting transfers between devices: 3.46 us -> 8.37 us  [swap_core(): return lax.ppermute(a, 'seq', [(i, i ^ 1) for i in range(NX * NY * 2)])]
    unnamed x12, local copies, waits for them, and re-layouts: 7.32 us -> 4.16 us
    pallas_call x2 -> x3, Pallas kernels: 8.87 us -> 11 us  [block_states(): pl.pallas_call(functools.partial(state_kernel, count), grid_spec=pltpu.Pr...]
    pallas_call x2 -> x3, Pallas kernels: 8.29 us -> 8.76 us  [finish(): pl.pallas_call(functools.partial(finish_kernel, count), grid_spec=pltpu.P...]
  transfers between devices with their start and end apart: 23 -> 23, of which waited for: 13 -> 16; matrix products, arithmetic and copies ran while one was open for 1% -> 1% of each run, Pallas kernels for 12% -> 23%
where the time goes in v3:
time: 134 us; the launch traced here: 132 us
  waiting for transfers between devices  46.4 us (35%)
  Pallas kernels  41 us (31%)
  starting transfers between devices  39.5 us (29%)
  local copies, waits for them, and re-layouts  4.48 us (3%)
    ppermute x8, waiting for transfers between devices, swap_near(): return lax.ppermute(a, 'head', [(i, i ^ 1) for i in range(NZ)])  15.2 us
    pallas_call x3, Pallas kernels, block_states(): pl.pallas_call(functools.partial(state_kernel, count), grid_spec=pltpu.Pr...  11 us
    pallas_call x1, Pallas kernels, intra(): pl.pallas_call(intra_kernel, grid=(NZ,), in_specs=[BLOCK, BLOCK, BLOCK, p...  9.54 us
    all_to_all x1, starting transfers between devices, local(): ld = lax.all_to_all(with_near(by_block), 'head', 0, 0, tiled=True)  9.01 us
    pallas_call x3, Pallas kernels, finish(): pl.pallas_call(functools.partial(finish_kernel, count), grid_spec=pltpu.P...  8.76 us
    ppermute x2, starting transfers between devices, swap_core(): return lax.ppermute(a, 'seq', [(i, i ^ 1) for i in range(NX * NY * 2)])  8.37 us
    ppermute x8, starting transfers between devices, swap_near(): return lax.ppermute(a, 'head', [(i, i ^ 1) for i in range(NZ)])  8.11 us
    all_to_all x1, waiting for transfers between devices, local(): ld = lax.all_to_all(with_near(by_block), 'head', 0, 0, tiled=True)  6.99 us
  transfers between devices with their start and end apart: 23, of which 16 were waited for; matrix products, arithmetic and copies ran while one was open for 1% of the time, Pallas kernels for 23%

profile of v3, /device:TPU:1, one launch (start us, length us, event | category | flops | bytes accessed | tf_op | source)
XLA Modules:
  0.0 132.5 jit_solution(13943808548965582629)
XLA Ops:
  1.4 9.0 %all-to-all-start = ((f32[8,16,128]{2,1,0:T(8,128)}), f32[8,16,128]{2,1,0:T(8,128)S(1)}, u32[]{:S(2)}, u32[]{:S(2)}) async-start(f32[8,16,128]{2,1,0:T(8,128)} %shard_map.55), calls=%async_computation | async-start | bytes 131072 | tf_op jit(solution)/shard_map/all_to_all | solution.py:491
  10.7 7.0 %all-to-all-done.ld_ref = f32[8,16,128]{2,1,0:T(8,128)S(1)} async-done(((f32[8,16,128]{2,1,0:T(8,128)}), f32[8,16,128]{2,1,0:T(8,128)S(1)}, u32[]{:S(2)}, u32[]{:S(2)}) %all-to-all-start) | async-done | bytes 65568 | tf_op jit(solution)/shard_map/all_to_all | solution.py:491
  17.6 2.7 %shard_map.58 = (bf16[8,128,128]{2,1,0:T(8,128)(2,1)S(1)}, bf16[8,128,128]{2,1,0:T(8,128)(2,1)S(1)}) custom-call(s32[2]{0:T(128)S(1)} %pad_add_fusion.3.chunks, bf16[128,8192]{1,0:T(8,128)(2,1)} %k_ref.7, bf16[128,8192]{1,0:T(8,128)(2,1)} %v_ref.7, f32[8,16,128]{2,1,0:T(8,128)S(1)} %all-to-all-done.ld_ref), custom_call_target="tpu_custom_call" | custom-call | flops 134217728 | bytes 1600000 | tf_op jit(solution)/shard_map/pallas_call | solution.py:105
  22.0 4.5 %shard_map.57 = (bf16[8,128,128]{2,1,0:T(8,128)(2,1)S(1)}, bf16[8,128,128]{2,1,0:T(8,128)(2,1)S(1)}, bf16[8,128,128]{2,1,0:T(8,128)(2,1)}) custom-call(s32[3]{0:T(128)S(1)} %pad_add_fusion.2.chunks, bf16[128,8192]{1,0:T(8,128)(2,1)} %k_ref.7, bf16[128,8192]{1,0:T(8,128)(2,1)} %v_ref.7, f32[8,16,128]{2,1,0:T(8,128)S(1)} %all-to-all-done.ld_ref), custom_call_target="tpu_custom_call" | custom-call | flops 201326592 | bytes 2400000 | tf_op jit(solution)/shard_map/pallas_call | solution.py:105
  27.1 1.2 collective-permute-start
  28.3 3.8 %shard_map.56 = (bf16[8,128,128]{2,1,0:T(8,128)(2,1)S(1)}, bf16[8,128,128]{2,1,0:T(8,128)(2,1)S(1)}, bf16[8,128,128]{2,1,0:T(8,128)(2,1)S(1)}) custom-call(s32[3]{0:T(128)S(1)} %pad_add_fusion.1.chunks, bf16[128,8192]{1,0:T(8,128)(2,1)} %k_ref.7, bf16[128,8192]{1,0:T(8,128)(2,1)} %v_ref.7, f32[8,16,128]{2,1,0:T(8,128)S(1)} %all-to-all-done.ld_ref), custom_call_target="tpu_custom_call" | custom-call | flops 201326592 | bytes 2400000 | tf_op jit(solution)/shard_map/pallas_call | solution.py:105
  33.4 7.0 %collective-permute-done.5.got_ref = bf16[8,128,128]{2,1,0:T(8,128)(2,1)S(1)} collective-permute-done((bf16[8,128,128]{2,1,0:T(8,128)(2,1)S(1)}, bf16[8,128,128]{2,1,0:T(8,128)(2,1)S(1)}, u32[]{:S(2)}, u32[]{:S(2)}) %collective-permute-start.5) | collective-permute-done | bytes 262176 | tf_op jit(solution)/shard_map/ppermute | solution.py:436
  40.4 1.4 %shard_map.61 = bf16[8,128,128]{2,1,0:T(8,128)(2,1)} custom-call(s32[4]{0:T(128)S(1)} %pad_add_fusion.place, f32[64]{0:T(128)S(1)} %exp.29.d_ref, bf16[8,128,128]{2,1,0:T(8,128)(2,1)S(1)} %get-tuple-element.36.keep_ref, bf16[8,128,128]{2,1,0:T(8,128)(2,1)S(1)} %collective-permute-done.5.got_ref), custom_call_target="tpu_custom_call" | custom-call | flops 524288 | bytes 800000 | tf_op jit(solution)/shard_map/pallas_call | solution.py:181
  41.8 1.4 %shard_map.60 = bf16[8,128,128]{2,1,0:T(8,128)(2,1)} custom-call(s32[4]{0:T(128)S(1)} %pad_add_fusion.place, f32[64]{0:T(128)S(1)} %exp.29.d_ref, bf16[8,128,128]{2,1,0:T(8,128)(2,1)S(1)} %get-tuple-element.34.keep_ref, bf16[8,128,128]{2,1,0:T(8,128)(2,1)S(1)} %collective-permute-done.3.got_ref), custom_call_target="tpu_custom_call" | custom-call | flops 524288 | bytes 800000 | tf_op jit(solution)/shard_map/pallas_call | solution.py:181
  43.6 5.1 %collective-permute-done.near_ref = bf16[8,128,128]{2,1,0:T(8,128)(2,1)S(1)} collective-permute-done((bf16[8,128,128]{2,1,0:T(8,128)(2,1)}, bf16[8,128,128]{2,1,0:T(8,128)(2,1)S(1)}, u32[]{:S(2)}, u32[]{:S(2)}) %collective-permute-start) | collective-permute-done | bytes 262176 | tf_op jit(solution)/shard_map/ppermute | solution.py:436
  49.7 4.1 %collective-permute-done.4.refs_1_ = bf16[8,128,128]{2,1,0:T(8,128)(2,1)S(1)} collective-permute-done((bf16[8,128,128]{2,1,0:T(8,128)(2,1)}, bf16[8,128,128]{2,1,0:T(8,128)(2,1)S(1)}, u32[]{:S(2)}, u32[]{:S(2)}) %collective-permute-start.4) | collective-permute-done | bytes 262176 | tf_op jit(solution)/shard_map/ppermute | solution.py:444
  54.6 6.1 %collective-permute-start.7 = (f32[4,136,128]{2,1,0:T(8,128)S(1)}, f32[4,136,128]{2,1,0:T(8,128)S(1)}, u32[]{:S(2)}, u32[]{:S(2)}) collective-permute-start(f32[4,136,128]{2,1,0:T(8,128)S(1)} %get-tuple-element.39), channel_id=1, source_target_pairs={{0,1},{1,0},{2,3},{3,2},{4,5},{5,4},{6,7},{7,6},{8,9},{9,8},{10,11... | collective-permute-start | bytes 835592 | tf_op jit(solution)/shard_map/ppermute | solution.py:456
  62.5 3.0 %collective-permute-start.10 = (bf16[4,144,128]{2,1,0:T(8,128)(2,1)S(1)}, bf16[4,144,128]{2,1,0:T(8,128)(2,1)S(1)}, u32[]{:S(2)}, u32[]{:S(2)}) collective-permute-start(bf16[4,144,128]{2,1,0:T(8,128)(2,1)S(1)} %shard_map.63.refs_0_), channel_id=1, source_target_pairs={{0,4},{1,5},{2,6},{3,7},{4,0},{5,1},{6,2},{7,3},{8,12},{9,13},{10,... | collective-permute-start | bytes 442376 | tf_op jit(solution)/shard_map/ppermute | solution.py:466
  67.0 2.2 %collective-permute-done.10.refs_3_ = bf16[4,144,128]{2,1,0:T(8,128)(2,1)S(1)} collective-permute-done((bf16[4,144,128]{2,1,0:T(8,128)(2,1)S(1)}, bf16[4,144,128]{2,1,0:T(8,128)(2,1)S(1)}, u32[]{:S(2)}, u32[]{:S(2)}) %collective-permute-start.10) | collective-permute-done | bytes 147488 | tf_op jit(solution)/shard_map/ppermute | solution.py:466
  69.2 3.5 %collective-permute-done.9.refs_2_ = bf16[4,144,128]{2,1,0:T(8,128)(2,1)S(1)} collective-permute-done((bf16[4,144,128]{2,1,0:T(8,128)(2,1)S(1)}, bf16[4,144,128]{2,1,0:T(8,128)(2,1)S(1)}, u32[]{:S(2)}, u32[]{:S(2)}) %collective-permute-start.9) | collective-permute-done | bytes 147488 | tf_op jit(solution)/shard_map/ppermute | solution.py:466
  73.4 2.8 %collective-permute-start.13 = (bf16[4,144,128]{2,1,0:T(8,128)(2,1)S(1)}, bf16[4,144,128]{2,1,0:T(8,128)(2,1)S(1)}, u32[]{:S(2)}, u32[]{:S(2)}) collective-permute-start(bf16[4,144,128]{2,1,0:T(8,128)(2,1)S(1)} %shard_map.64.refs_4_), channel_id=1, source_target_pairs={{0,16},{1,17},{2,18},{3,19},{4,20},{5,21},{6,22},{7,23},{8,24},{9,... | collective-permute-start | bytes 442376 | tf_op jit(solution)/shard_map/ppermute | solution.py:476
  77.7 1.3 collective-permute-done.13.refs_7_
  79.0 3.2 %collective-permute-done.12.refs_6_ = bf16[4,144,128]{2,1,0:T(8,128)(2,1)S(1)} collective-permute-done((bf16[4,144,128]{2,1,0:T(8,128)(2,1)S(1)}, bf16[4,144,128]{2,1,0:T(8,128)(2,1)S(1)}, u32[]{:S(2)}, u32[]{:S(2)}) %collective-permute-start.12) | collective-permute-done | bytes 147488 | tf_op jit(solution)/shard_map/ppermute | solution.py:476
  84.2 1.6 %shard_map.65 = (f32[4,128,128]{2,1,0:T(8,128)S(1)}, f32[4,128,128]{2,1,0:T(8,128)}) custom-call(s32[4]{0:T(128)S(1)} %pad_add_fusion.place, f32[8,128,128]{2,1,0:T(8,128)S(1)} %copy-done, f32[4,136,128]{2,1,0:T(8,128)S(1)} %get-tuple-element.38.mine_ref, f32[4,136,128]{2,1,0:T(8,128)S(1)} %collective-permute-done.7.got_ref, ...), custom_call_target="tpu_custom_call" | custom-call | flops 1048576 | bytes 1048576 | tf_op jit(solution)/shard_map/pallas_call | solution.py:318
  85.7 2.3 %collective-permute-start.14 = (f32[4,128,128]{2,1,0:T(8,128)}, f32[4,128,128]{2,1,0:T(8,128)S(1)}, u32[]{:S(2)}, u32[]{:S(2)}) collective-permute-start(f32[4,128,128]{2,1,0:T(8,128)} %get-tuple-element.41), channel_id=1, source_target_pairs={{0,1},{1,0},{2,3},{3,2},{4,5},{5,4},{6,7},{7,6},{8,9},{9,8},{10,11... | collective-permute-start | bytes 786440 | tf_op jit(solution)/shard_map/ppermute | solution.py:456
  88.1 1.3 collective-permute-done.14.got_ref
  91.0 1.8 %shard_map.66 = (bf16[8,128,128]{2,1,0:T(8,128)(2,1)S(1)}, bf16[8,128,128]{2,1,0:T(8,128)(2,1)S(1)}, bf16[8,128,128]{2,1,0:T(8,128)(2,1)}, bf16[8,128,128]{2,1,0:T(8,128)(2,1)}, bf16[8,128,128]{2,1,0:T(8,128)(2,1)}) custom-call(s32[4]{0:T(128)S(1)} %pad_add_fusion.place, f32[64]{0:T(128)S(1)} %exp.25.d_ref, f32[4,128,128]{2,1,0:T(8,128)S(1)} %get-tuple-element.40.keep_ref, ...), custom_call_target="tpu_custom_call" | custom-call | flops 2097152 | bytes 5242880 | tf_op jit(solution)/shard_map/pallas_call | solution.py:372
  93.5 2.1 %collective-permute-start.19 = (bf16[8,128,128]{2,1,0:T(8,128)(2,1)}, bf16[8,128,128]{2,1,0:T(8,128)(2,1)S(1)}, u32[]{:S(2)}, u32[]{:S(2)}) collective-permute-start(bf16[8,128,128]{2,1,0:T(8,128)(2,1)} %get-tuple-element.50), channel_id=1, source_target_pairs={{224,0},{64,32},{32,64},{128,96},{96,128},{192,160},{160,192},{0,2... | collective-permute-start | bytes 786440 | tf_op jit(solution)/shard_map/ppermute | solution.py:448
  96.7 1.5 %collective-permute-start.15 = (bf16[8,128,128]{2,1,0:T(8,128)(2,1)}, bf16[8,128,128]{2,1,0:T(8,128)(2,1)S(1)}, u32[]{:S(2)}, u32[]{:S(2)}) collective-permute-start(bf16[8,128,128]{2,1,0:T(8,128)(2,1)} %get-tuple-element.45), channel_id=1, source_target_pairs={{160,0},{128,32},{224,64},{192,96},{32,128},{0,160},{96,192},{64,2... | collective-permute-start | bytes 786440 | tf_op jit(solution)/shard_map/ppermute | solution.py:448
  98.4 9.5 %shard_map.67 = (f32[128,8192]{1,0:T(8,128)S(1)}, bf16[128,16384]{1,0:T(8,128)(2,1)S(1)}) custom-call(bf16[128,8192]{1,0:T(8,128)(2,1)} %q_ref.1, bf16[128,8192]{1,0:T(8,128)(2,1)} %k_ref.7, bf16[128,8192]{1,0:T(8,128)(2,1)} %v_ref.7, f32[8,16,128]{2,1,0:T(8,128)S(1)} %all-to-all-done.ld_ref, bf16[8,128,128]{2,1,0:T(8,128)(2,1)S(1)} %get-tuple-element.42.after_ref.refs_0_), custom_call_target="tpu_custom_call" | custom-call | flops 805306368 | bytes 14680064 | tf_op jit(solution)/shard_map/pallas_call | solution.py:144
  108.8 1.4 %collective-permute-start.20 = (bf16[8,128,128]{2,1,0:T(8,128)(2,1)S(1)}, bf16[8,128,128]{2,1,0:T(8,128)(2,1)S(1)}, u32[]{:S(2)}, u32[]{:S(2)}) collective-permute-start(bf16[8,128,128]{2,1,0:T(8,128)(2,1)S(1)} %get-tuple-element.51), channel_id=1, source_target_pairs={{0,32},{32,0},{64,96},{96,64},{128,160},{160,128},{192,224},{224,1... | collective-permute-start | bytes 786440 | tf_op jit(solution)/shard_map/ppermute | solution.py:436
  111.2 5.3 %collective-permute-done.15.start_ref = bf16[8,128,128]{2,1,0:T(8,128)(2,1)S(1)} collective-permute-done((bf16[8,128,128]{2,1,0:T(8,128)(2,1)}, bf16[8,128,128]{2,1,0:T(8,128)(2,1)S(1)}, u32[]{:S(2)}, u32[]{:S(2)}) %collective-permute-start.15) | collective-permute-done | bytes 262176 | tf_op jit(solution)/shard_map/ppermute | solution.py:448
  117.2 3.3 %collective-permute-start.16 = (bf16[8,128,128]{2,1,0:T(8,128)(2,1)S(1)}, bf16[8,128,128]{2,1,0:T(8,128)(2,1)S(1)}, u32[]{:S(2)}, u32[]{:S(2)}) collective-permute-start(bf16[8,128,128]{2,1,0:T(8,128)(2,1)S(1)} %get-tuple-element.46), channel_id=1, source_target_pairs={{0,32},{32,0},{64,96},{96,64},{128,160},{160,128},{192,224},{224,1... | collective-permute-start | bytes 786440 | tf_op jit(solution)/shard_map/ppermute | solution.py:436
  120.7 4.1 %shard_map.71.refs_3_ = bf16[128,8192]{1,0:T(8,128)(2,1)} custom-call(s32[4]{0:T(128)S(1)} %pad_add_fusion.5.chunks, bf16[128,16384]{1,0:T(8,128)(2,1)S(1)} %get-tuple-element.43.refs_0_.qd_ref, f32[128,8192]{1,0:T(8,128)S(1)} %get-tuple-element.44.o_ref, bf16[8,128,128]{2,1,0:T(8,128)(2,1)S(1)} %get-tuple-element.42.after_ref.refs_0_, ...), custom_call_target="tpu_custom_call" | custom-call | flops 268435456 | bytes 6000000 | tf_op jit(solution)/shard_map/pallas_call | solution.py:419
  125.6 3.4 %shard_map.72.refs_1_ = bf16[128,8192]{1,0:T(8,128)(2,1)} custom-call(s32[3]{0:T(128)S(1)} %pad_add_fusion.4.chunks, bf16[128,16384]{1,0:T(8,128)(2,1)S(1)} %get-tuple-element.43.refs_0_.qd_ref, f32[128,8192]{1,0:T(8,128)S(1)} %get-tuple-element.44.o_ref, bf16[8,128,128]{2,1,0:T(8,128)(2,1)S(1)} %get-tuple-element.47.refs_0_, ...), custom_call_target="tpu_custom_call", output_to_operand_aliasing={{}: (6, {})} | custom-call | flops 201326592 | bytes 4500000 | tf_op jit(solution)/shard_map/pallas_call | solution.py:419
  129.1 2.2 %collective-permute-done.16.refs_0_ = bf16[8,128,128]{2,1,0:T(8,128)(2,1)S(1)} collective-permute-done((bf16[8,128,128]{2,1,0:T(8,128)(2,1)S(1)}, bf16[8,128,128]{2,1,0:T(8,128)(2,1)S(1)}, u32[]{:S(2)}, u32[]{:S(2)}) %collective-permute-start.16) | collective-permute-done | bytes 262176 | tf_op jit(solution)/shard_map/ppermute | solution.py:436
  131.3 1.2 shard_map.73
  (63 shorter events, 22.0 us)
Async XLA Ops:
  0.0 0.8 copy-start.1
  1.4 16.3 %all-to-all-start = ((f32[8,16,128]{2,1,0:T(8,128)}), f32[8,16,128]{2,1,0:T(8,128)S(1)}, u32[]{:S(2)}, u32[]{:S(2)}) async-start(f32[8,16,128]{2,1,0:T(8,128)} %shard_map.55), calls=%async_computation | async-start | bytes 131072 | tf_op jit(solution)/shard_map/all_to_all | solution.py:491
  20.4 11.7 %collective-permute-start.1 = (bf16[8,128,128]{2,1,0:T(8,128)(2,1)S(1)}, bf16[8,128,128]{2,1,0:T(8,128)(2,1)S(1)}, u32[]{:S(2)}, u32[]{:S(2)}) collective-permute-start(bf16[8,128,128]{2,1,0:T(8,128)(2,1)S(1)} %get-tuple-element.33), channel_id=1, source_target_pairs={{0,32},{32,0},{64,96},{96,64},{128,160},{160,128},{192,224},{224,1... | collective-permute-start | bytes 786440 | tf_op jit(solution)/shard_map/ppermute | solution.py:436
  20.8 21.0 %collective-permute-start.3 = (bf16[8,128,128]{2,1,0:T(8,128)(2,1)S(1)}, bf16[8,128,128]{2,1,0:T(8,128)(2,1)S(1)}, u32[]{:S(2)}, u32[]{:S(2)}) collective-permute-start(bf16[8,128,128]{2,1,0:T(8,128)(2,1)S(1)} %get-tuple-element.35), channel_id=1, source_target_pairs={{0,32},{32,0},{64,96},{96,64},{128,160},{160,128},{192,224},{224,1... | collective-permute-start | bytes 786440 | tf_op jit(solution)/shard_map/ppermute | solution.py:436
  26.4 14.0 %collective-permute-start.5 = (bf16[8,128,128]{2,1,0:T(8,128)(2,1)S(1)}, bf16[8,128,128]{2,1,0:T(8,128)(2,1)S(1)}, u32[]{:S(2)}, u32[]{:S(2)}) collective-permute-start(bf16[8,128,128]{2,1,0:T(8,128)(2,1)S(1)} %get-tuple-element.37), channel_id=1, source_target_pairs={{0,32},{32,0},{64,96},{96,64},{128,160},{160,128},{192,224},{224,1... | collective-permute-start | bytes 786440 | tf_op jit(solution)/shard_map/ppermute | solution.py:436
  27.1 21.6 %collective-permute-start = (bf16[8,128,128]{2,1,0:T(8,128)(2,1)}, bf16[8,128,128]{2,1,0:T(8,128)(2,1)S(1)}, u32[]{:S(2)}, u32[]{:S(2)}) collective-permute-start(bf16[8,128,128]{2,1,0:T(8,128)(2,1)} %get-tuple-element.31), channel_id=1, source_target_pairs={{0,32},{32,0},{64,96},{96,64},{128,160},{160,128},{192,224},{224,1... | collective-permute-start | bytes 786440 | tf_op jit(solution)/shard_map/ppermute | solution.py:436
  32.1 11.0 %copy-start.2 = (f32[1024,8]{0,1:T(8,128)S(1)}, f32[1024,8]{0,1:T(8,128)}, u32[]{:S(2)}) copy-start(f32[1024,8]{0,1:T(8,128)} %param.8) | copy-start | bytes 98308
  32.8 15.8 %collective-permute-start.2 = (bf16[8,128,128]{2,1,0:T(8,128)(2,1)S(1)}, bf16[8,128,128]{2,1,0:T(8,128)(2,1)S(1)}, u32[]{:S(2)}, u32[]{:S(2)}) collective-permute-start(bf16[8,128,128]{2,1,0:T(8,128)(2,1)S(1)} %shard_map.59), channel_id=1, source_target_pairs={{0,160},{32,128},{64,224},{96,192},{128,32},{160,0},{192,96},{224,... | collective-permute-start | bytes 786440 | tf_op jit(solution)/shard_map/ppermute | solution.py:444
  41.8 8.0 %collective-permute-start.6 = (bf16[8,128,128]{2,1,0:T(8,128)(2,1)}, bf16[8,128,128]{2,1,0:T(8,128)(2,1)S(1)}, u32[]{:S(2)}, u32[]{:S(2)}) collective-permute-start(bf16[8,128,128]{2,1,0:T(8,128)(2,1)} %shard_map.61), channel_id=1, source_target_pairs={{0,224},{32,64},{64,32},{96,128},{128,96},{160,192},{192,160},{224... | collective-permute-start | bytes 786440 | tf_op jit(solution)/shard_map/ppermute | solution.py:444
  43.1 10.7 %collective-permute-start.4 = (bf16[8,128,128]{2,1,0:T(8,128)(2,1)}, bf16[8,128,128]{2,1,0:T(8,128)(2,1)S(1)}, u32[]{:S(2)}, u32[]{:S(2)}) collective-permute-start(bf16[8,128,128]{2,1,0:T(8,128)(2,1)} %shard_map.60), channel_id=1, source_target_pairs={{0,192},{32,96},{64,0},{96,160},{128,64},{160,224},{192,128},{224,... | collective-permute-start | bytes 786440 | tf_op jit(solution)/shard_map/ppermute | solution.py:444
  54.6 7.3 %collective-permute-start.7 = (f32[4,136,128]{2,1,0:T(8,128)S(1)}, f32[4,136,128]{2,1,0:T(8,128)S(1)}, u32[]{:S(2)}, u32[]{:S(2)}) collective-permute-start(f32[4,136,128]{2,1,0:T(8,128)S(1)} %get-tuple-element.39), channel_id=1, source_target_pairs={{0,1},{1,0},{2,3},{3,2},{4,5},{5,4},{6,7},{7,6},{8,9},{9,8},{10,11... | collective-permute-start | bytes 835592 | tf_op jit(solution)/shard_map/ppermute | solution.py:456
  62.5 6.7 %collective-permute-start.10 = (bf16[4,144,128]{2,1,0:T(8,128)(2,1)S(1)}, bf16[4,144,128]{2,1,0:T(8,128)(2,1)S(1)}, u32[]{:S(2)}, u32[]{:S(2)}) collective-permute-start(bf16[4,144,128]{2,1,0:T(8,128)(2,1)S(1)} %shard_map.63.refs_0_), channel_id=1, source_target_pairs={{0,4},{1,5},{2,6},{3,7},{4,0},{5,1},{6,2},{7,3},{8,12},{9,13},{10,... | collective-permute-start | bytes 442376 | tf_op jit(solution)/shard_map/ppermute | solution.py:466
  65.5 7.2 %collective-permute-start.9 = (bf16[4,144,128]{2,1,0:T(8,128)(2,1)S(1)}, bf16[4,144,128]{2,1,0:T(8,128)(2,1)S(1)}, u32[]{:S(2)}, u32[]{:S(2)}) collective-permute-start(bf16[4,144,128]{2,1,0:T(8,128)(2,1)S(1)} %shard_map.63.refs_0_), channel_id=1, source_target_pairs={{0,6},{1,7},{2,0},{3,1},{4,2},{5,3},{6,4},{7,5},{8,14},{9,15},{10,... | collective-permute-start | bytes 442376 | tf_op jit(solution)/shard_map/ppermute | solution.py:466
  66.3 6.4 %collective-permute-start.8 = (bf16[4,144,128]{2,1,0:T(8,128)(2,1)S(1)}, bf16[4,144,128]{2,1,0:T(8,128)(2,1)S(1)}, u32[]{:S(2)}, u32[]{:S(2)}) collective-permute-start(bf16[4,144,128]{2,1,0:T(8,128)(2,1)S(1)} %shard_map.63.refs_0_), channel_id=1, source_target_pairs={{0,2},{1,3},{2,4},{3,5},{4,6},{5,7},{6,0},{7,1},{8,10},{9,11},{10,... | collective-permute-start | bytes 442376 | tf_op jit(solution)/shard_map/ppermute | solution.py:466
  73.4 5.6 %collective-permute-start.13 = (bf16[4,144,128]{2,1,0:T(8,128)(2,1)S(1)}, bf16[4,144,128]{2,1,0:T(8,128)(2,1)S(1)}, u32[]{:S(2)}, u32[]{:S(2)}) collective-permute-start(bf16[4,144,128]{2,1,0:T(8,128)(2,1)S(1)} %shard_map.64.refs_4_), channel_id=1, source_target_pairs={{0,16},{1,17},{2,18},{3,19},{4,20},{5,21},{6,22},{7,23},{8,24},{9,... | collective-permute-start | bytes 442376 | tf_op jit(solution)/shard_map/ppermute | solution.py:476
  76.2 6.0 %collective-permute-start.12 = (bf16[4,144,128]{2,1,0:T(8,128)(2,1)S(1)}, bf16[4,144,128]{2,1,0:T(8,128)(2,1)S(1)}, u32[]{:S(2)}, u32[]{:S(2)}) collective-permute-start(bf16[4,144,128]{2,1,0:T(8,128)(2,1)S(1)} %shard_map.64.refs_4_), channel_id=1, source_target_pairs={{0,24},{1,25},{2,26},{3,27},{4,28},{5,29},{6,30},{7,31},{8,0},{9,1... | collective-permute-start | bytes 442376 | tf_op jit(solution)/shard_map/ppermute | solution.py:476
  77.1 6.0 %collective-permute-start.11 = (bf16[4,144,128]{2,1,0:T(8,128)(2,1)S(1)}, bf16[4,144,128]{2,1,0:T(8,128)(2,1)S(1)}, u32[]{:S(2)}, u32[]{:S(2)}) collective-permute-start(bf16[4,144,128]{2,1,0:T(8,128)(2,1)S(1)} %shard_map.64.refs_4_), channel_id=1, source_target_pairs={{0,8},{1,9},{2,10},{3,11},{4,12},{5,13},{6,14},{7,15},{8,16},{9,17... | collective-permute-start | bytes 442376 | tf_op jit(solution)/shard_map/ppermute | solution.py:476
  83.1 1.0 copy-start
  85.7 3.6 %collective-permute-start.14 = (f32[4,128,128]{2,1,0:T(8,128)}, f32[4,128,128]{2,1,0:T(8,128)S(1)}, u32[]{:S(2)}, u32[]{:S(2)}) collective-permute-start(f32[4,128,128]{2,1,0:T(8,128)} %get-tuple-element.41), channel_id=1, source_target_pairs={{0,1},{1,0},{2,3},{3,2},{4,5},{5,4},{6,7},{7,6},{8,9},{9,8},{10,11... | collective-permute-start | bytes 786440 | tf_op jit(solution)/shard_map/ppermute | solution.py:456
  89.4 0.7 copy-start.3
  90.1 0.9 copy-start.4
  92.8 0.7 copy-start.5
  93.5 14.6 %collective-permute-start.19 = (bf16[8,128,128]{2,1,0:T(8,128)(2,1)}, bf16[8,128,128]{2,1,0:T(8,128)(2,1)S(1)}, u32[]{:S(2)}, u32[]{:S(2)}) collective-permute-start(bf16[8,128,128]{2,1,0:T(8,128)(2,1)} %get-tuple-element.50), channel_id=1, source_target_pairs={{224,0},{64,32},{32,64},{128,96},{96,128},{192,160},{160,192},{0,2... | collective-permute-start | bytes 786440 | tf_op jit(solution)/shard_map/ppermute | solution.py:448
  95.6 14.6 %collective-permute-start.17 = (bf16[8,128,128]{2,1,0:T(8,128)(2,1)}, bf16[8,128,128]{2,1,0:T(8,128)(2,1)S(1)}, u32[]{:S(2)}, u32[]{:S(2)}) collective-permute-start(bf16[8,128,128]{2,1,0:T(8,128)(2,1)} %get-tuple-element.48), channel_id=1, source_target_pairs={{192,0},{96,32},{0,64},{160,96},{64,128},{224,160},{128,192},{32,2... | collective-permute-start | bytes 786440 | tf_op jit(solution)/shard_map/ppermute | solution.py:448
  96.7 19.7 %collective-permute-start.15 = (bf16[8,128,128]{2,1,0:T(8,128)(2,1)}, bf16[8,128,128]{2,1,0:T(8,128)(2,1)S(1)}, u32[]{:S(2)}, u32[]{:S(2)}) collective-permute-start(bf16[8,128,128]{2,1,0:T(8,128)(2,1)} %get-tuple-element.45), channel_id=1, source_target_pairs={{160,0},{128,32},{224,64},{192,96},{32,128},{0,160},{96,192},{64,2... | collective-permute-start | bytes 786440 | tf_op jit(solution)/shard_map/ppermute | solution.py:448
  98.3 22.3 %collective-permute-start.21 = (bf16[8,128,128]{2,1,0:T(8,128)(2,1)}, bf16[8,128,128]{2,1,0:T(8,128)(2,1)S(1)}, u32[]{:S(2)}, u32[]{:S(2)}) collective-permute-start(bf16[8,128,128]{2,1,0:T(8,128)(2,1)} %copy-done.5), channel_id=1, source_target_pairs={{0,32},{32,0},{64,96},{96,64},{128,160},{160,128},{192,224},{224,1... | collective-permute-start | bytes 786440 | tf_op jit(solution)/shard_map/ppermute | solution.py:436
  108.8 16.0 %collective-permute-start.20 = (bf16[8,128,128]{2,1,0:T(8,128)(2,1)S(1)}, bf16[8,128,128]{2,1,0:T(8,128)(2,1)S(1)}, u32[]{:S(2)}, u32[]{:S(2)}) collective-permute-start(bf16[8,128,128]{2,1,0:T(8,128)(2,1)S(1)} %get-tuple-element.51), channel_id=1, source_target_pairs={{0,32},{32,0},{64,96},{96,64},{128,160},{160,128},{192,224},{224,1... | collective-permute-start | bytes 786440 | tf_op jit(solution)/shard_map/ppermute | solution.py:436
  110.9 14.8 %collective-permute-start.18 = (bf16[8,128,128]{2,1,0:T(8,128)(2,1)S(1)}, bf16[8,128,128]{2,1,0:T(8,128)(2,1)S(1)}, u32[]{:S(2)}, u32[]{:S(2)}) collective-permute-start(bf16[8,128,128]{2,1,0:T(8,128)(2,1)S(1)} %get-tuple-element.49), channel_id=1, source_target_pairs={{0,32},{32,0},{64,96},{96,64},{128,160},{160,128},{192,224},{224,1... | collective-permute-start | bytes 786440 | tf_op jit(solution)/shard_map/ppermute | solution.py:436
  117.2 14.1 %collective-permute-start.16 = (bf16[8,128,128]{2,1,0:T(8,128)(2,1)S(1)}, bf16[8,128,128]{2,1,0:T(8,128)(2,1)S(1)}, u32[]{:S(2)}, u32[]{:S(2)}) collective-permute-start(bf16[8,128,128]{2,1,0:T(8,128)(2,1)S(1)} %get-tuple-element.46), channel_id=1, source_target_pairs={{0,32},{32,0},{64,96},{96,64},{128,160},{160,128},{192,224},{224,1... | collective-permute-start | bytes 786440 | tf_op jit(solution)/shard_map/ppermute | solution.py:436

commit v4 on v3

--- a/solution.py
+++ b/solution.py
@@ -168,7 +168,8 @@
     return lax.rem(own + 4 + {1: -1, 2: 1, 3: 2}[a] * signed(place), 4)
 
 
-def join_kernel(a, place, d_ref, keep_ref, got_ref, out_ref):
+def join_kernel(a, place, d_ref, keep_ref, got_ref, *refs):
+    out_ref = refs[-1]
     even = lax.rem(place[0], 2) == 0
     group = group_at(place, a)
     for h in range(GROUP):
@@ -177,15 +178,15 @@
         out_ref[h] = (first * d_ref[group * GROUP + h] + second).astype(BF16)
 
 
-def join(a, place, over_odd, keep, got):
+def join(a, place, over_odd, keep, got, after):
     return pl.pallas_call(
         functools.partial(join_kernel, a),
-        in_specs=[SM, SM, VM, VM],
+        in_specs=[SM, SM, VM, VM] + [ANY] * len(after),
         out_specs=VM,
         out_shape=STATE,
         compiler_params=params(),
         cost_estimate=cost(GROUP * DH * DH * 4, 800000),
-    )(place, over_odd, keep, got)
+    )(place, over_odd, keep, got, *after)
 
 
 def part_kernel(a, place, d_ref, start_ref, keep_ref, got_ref, *refs):
@@ -380,8 +381,9 @@
     )(place, decays, keep, got, *pieces)
 
 
-def finish_kernel(count, chunks, qd_ref, o_ref, *refs):
-    entries, out_ref, held = refs[:count], refs[-2], refs[-1]
+def finish_kernel(count, chunks, *refs):
+    qd_ref, o_ref, *entries = refs[-4 - count : -2]
+    out_ref, held = refs[-2], refs[-1]
     step = pl.program_id(0)
     for k in range(count):
 
@@ -408,14 +410,11 @@
 def finish(chunks, qd, o, entries, held):
     count = len(entries)
     wide = pl.BlockSpec((ROWS, WIDE), lambda i, c: (0, c[i]))
-    specs = [pl.BlockSpec((ROWS, 2 * WIDE), lambda i, c: (0, c[i])), wide]
+    specs = [] if held is None else [ANY]
+    specs += [pl.BlockSpec((ROWS, 2 * WIDE), lambda i, c: (0, c[i])), wide]
     specs += [pl.BlockSpec((GROUP, DH, DH), lambda i, c: (0, 0, 0))] * count
-    args = [chunks, qd, o, *entries]
-    aliases = {}
-    if held is not None:
-        specs.append(ANY)
-        args.append(held)
-        aliases = {len(args) - 1: 0}
+    args = [chunks] + ([] if held is None else [held]) + [qd, o, *entries]
+    aliases = {} if held is None else {1: 0}
     return pl.pallas_call(
         functools.partial(finish_kernel, count),
         grid_spec=pltpu.PrefetchScalarGridSpec(
@@ -520,8 +519,10 @@
     )
     for a in (3, 2, 1, 0):
         got[a] = swap_near(give[a + 1])
+    after = []
     for a in FAR:
-        joined[a] = to_owner(join(a, place, over_odd, kept[a], got[a]), a)
+        pair = join(a, place, over_odd, kept[a], got[a], after)
+        joined[a], after = to_owner(pair, a), [pair]
 
     pieces = [kept[0], got[0]] + [joined[a] for a in FAR]
     mine, other = row_states(place, closing, rows, pieces)
@@ -531,13 +532,18 @@
     o, qd = intra(queries, key_rows, value_rows, ld, own)
     entry[0] = own
     near = swap_near(near)
+    sent = {a: from_owner(x, a) for a, x in zip(FAR, far)}
     passed = {}
-    for a, x in zip(FAR, far):
-        entry[a], x = part(a, place, over_even, from_owner(x, a), kept[a], got[a], [qd])
+
+    def pass_on(a, after):
+        entry[a], x = part(a, place, over_even, sent[a], kept[a], got[a], after)
         passed[a] = swap_near(x)
 
+    pass_on(2, [qd])
+    pass_on(1, [qd])
     early = [entry[0], near, entry[1], entry[2]]
     out = finish(jnp.stack(keeps(0) + gives(1) + keeps(1, 2)), qd, o, early, None)
+    pass_on(3, [out])
     middle = [entry[3], passed[2], passed[1]]
     out = finish(jnp.stack(keeps(3) + gives(3, 2)), qd, o, middle, out)
     return finish(jnp.stack(gives(4)), qd, o, [passed[3]], out)

time: 134 us -> 132 us (0.985)
  waiting for transfers between devices: 46.4 us -> 43.5 us
  starting transfers between devices: 39.5 us -> 41.5 us
    ppermute x3, waiting for transfers between devices: 5.49 us -> 1.94 us  [from_owner(): return lax.ppermute(x, 'head', [(j, i) for i, j in hops(a)])]
    ppermute x8, starting transfers between devices: 8.11 us -> 10.5 us  [swap_near(): return lax.ppermute(a, 'head', [(i, i ^ 1) for i in range(NZ)])]
    ppermute x3, starting transfers between devices: 0.55 us -> 2.84 us  [to_owner(): return lax.ppermute(x, 'head', hops(a))]
    ppermute x2, starting transfers between devices: 8.37 us -> 6.65 us  [swap_core(): return lax.ppermute(a, 'seq', [(i, i ^ 1) for i in range(NX * NY * 2)])]
  transfers between devices with their start and end apart: 23 -> 23, of which waited for: 16 -> 14; matrix products, arithmetic and copies ran while one was open for 1% -> 1% of each run, Pallas kernels for 23% -> 23%
where the time goes in v4:
time: 132 us; the launch traced here: 131 us
  waiting for transfers between devices  43.5 us (33%)
  starting transfers between devices  41.5 us (31%)
  Pallas kernels  40.3 us (31%)
  local copies, waits for them, and re-layouts  4.34 us (3%)
    ppermute x8, waiting for transfers between devices, swap_near(): return lax.ppermute(a, 'head', [(i, i ^ 1) for i in range(NZ)])  16.5 us
    pallas_call x3, Pallas kernels, block_states(): pl.pallas_call(functools.partial(state_kernel, count), grid_spec=pltpu.Pr...  11 us
    ppermute x8, starting transfers between devices, swap_near(): return lax.ppermute(a, 'head', [(i, i ^ 1) for i in range(NZ)])  10.5 us
    pallas_call x1, Pallas kernels, intra(): pl.pallas_call(intra_kernel, grid=(NZ,), in_specs=[BLOCK, BLOCK, BLOCK, p...  9.53 us
    all_to_all x1, starting transfers between devices, local(): ld = lax.all_to_all(with_near(by_block), 'head', 0, 0, tiled=True)  9.01 us
    pallas_call x3, Pallas kernels, finish(): pl.pallas_call(functools.partial(finish_kernel, count), grid_spec=pltpu.P...  8.74 us
    all_to_all x1, waiting for transfers between devices, local(): ld = lax.all_to_all(with_near(by_block), 'head', 0, 0, tiled=True)  6.99 us
    ppermute x2, starting transfers between devices, swap_core(): return lax.ppermute(a, 'seq', [(i, i ^ 1) for i in range(NX * NY * 2)])  6.65 us
  transfers between devices with their start and end apart: 23, of which 14 were waited for; matrix products, arithmetic and copies ran while one was open for 1% of the time, Pallas kernels for 23%

profile of v4, /device:TPU:1, one launch (start us, length us, event | category | flops | bytes accessed | tf_op | source)
XLA Modules:
  0.0 130.8 jit_solution(14808196905124082250)
XLA Ops:
  1.4 9.0 %all-to-all-start = ((f32[8,16,128]{2,1,0:T(8,128)}), f32[8,16,128]{2,1,0:T(8,128)S(1)}, u32[]{:S(2)}, u32[]{:S(2)}) async-start(f32[8,16,128]{2,1,0:T(8,128)} %shard_map.55), calls=%async_computation | async-start | bytes 131072 | tf_op jit(solution)/shard_map/all_to_all | solution.py:490
  10.7 7.0 %all-to-all-done.ld_ref = f32[8,16,128]{2,1,0:T(8,128)S(1)} async-done(((f32[8,16,128]{2,1,0:T(8,128)}), f32[8,16,128]{2,1,0:T(8,128)S(1)}, u32[]{:S(2)}, u32[]{:S(2)}) %all-to-all-start) | async-done | bytes 65568 | tf_op jit(solution)/shard_map/all_to_all | solution.py:490
  17.6 2.7 %shard_map.58 = (bf16[8,128,128]{2,1,0:T(8,128)(2,1)S(1)}, bf16[8,128,128]{2,1,0:T(8,128)(2,1)S(1)}) custom-call(s32[2]{0:T(128)S(1)} %pad_add_fusion.5.chunks, bf16[128,8192]{1,0:T(8,128)(2,1)} %k_ref.7, bf16[128,8192]{1,0:T(8,128)(2,1)} %v_ref.7, f32[8,16,128]{2,1,0:T(8,128)S(1)} %all-to-all-done.ld_ref), custom_call_target="tpu_custom_call" | custom-call | flops 134217728 | bytes 1600000 | tf_op jit(solution)/shard_map/pallas_call | solution.py:105
  22.0 4.4 %shard_map.57 = (bf16[8,128,128]{2,1,0:T(8,128)(2,1)S(1)}, bf16[8,128,128]{2,1,0:T(8,128)(2,1)}, bf16[8,128,128]{2,1,0:T(8,128)(2,1)}) custom-call(s32[3]{0:T(128)S(1)} %pad_add_fusion.4.chunks, bf16[128,8192]{1,0:T(8,128)(2,1)} %k_ref.7, bf16[128,8192]{1,0:T(8,128)(2,1)} %v_ref.7, f32[8,16,128]{2,1,0:T(8,128)S(1)} %all-to-all-done.ld_ref), custom_call_target="tpu_custom_call" | custom-call | flops 201326592 | bytes 2400000 | tf_op jit(solution)/shard_map/pallas_call | solution.py:105
  27.1 1.2 collective-permute-start
  28.3 3.8 %shard_map.56 = (bf16[8,128,128]{2,1,0:T(8,128)(2,1)S(1)}, bf16[8,128,128]{2,1,0:T(8,128)(2,1)S(1)}, bf16[8,128,128]{2,1,0:T(8,128)(2,1)S(1)}) custom-call(s32[3]{0:T(128)S(1)} %pad_add_fusion.3.chunks, bf16[128,8192]{1,0:T(8,128)(2,1)} %k_ref.7, bf16[128,8192]{1,0:T(8,128)(2,1)} %v_ref.7, f32[8,16,128]{2,1,0:T(8,128)S(1)} %all-to-all-done.ld_ref), custom_call_target="tpu_custom_call" | custom-call | flops 201326592 | bytes 2400000 | tf_op jit(solution)/shard_map/pallas_call | solution.py:105
  34.0 2.3 %collective-permute-start.4 = (bf16[8,128,128]{2,1,0:T(8,128)(2,1)S(1)}, bf16[8,128,128]{2,1,0:T(8,128)(2,1)S(1)}, u32[]{:S(2)}, u32[]{:S(2)}) collective-permute-start(bf16[8,128,128]{2,1,0:T(8,128)(2,1)S(1)} %shard_map.60.refs_0_), channel_id=1, source_target_pairs={{0,192},{32,96},{64,0},{96,160},{128,64},{160,224},{192,128},{224,... | collective-permute-start | bytes 786440 | tf_op jit(solution)/shard_map/ppermute | solution.py:443
  36.3 4.7 %collective-permute-done.5.got_ref = bf16[8,128,128]{2,1,0:T(8,128)(2,1)S(1)} collective-permute-done((bf16[8,128,128]{2,1,0:T(8,128)(2,1)}, bf16[8,128,128]{2,1,0:T(8,128)(2,1)S(1)}, u32[]{:S(2)}, u32[]{:S(2)}) %collective-permute-start.5) | collective-permute-done | bytes 262176 | tf_op jit(solution)/shard_map/ppermute | solution.py:435
  41.1 1.4 %shard_map.61 = bf16[8,128,128]{2,1,0:T(8,128)(2,1)} custom-call(s32[4]{0:T(128)S(1)} %pad_add_fusion.2.place, f32[64]{0:T(128)S(1)} %exp.29.d_ref, bf16[8,128,128]{2,1,0:T(8,128)(2,1)S(1)} %get-tuple-element.36.keep_ref, bf16[8,128,128]{2,1,0:T(8,128)(2,1)S(1)} %collective-permute-done.5.got_ref, bf16[8,128,128]{2,1,0:T(8,128)(2,1)S(1)} %shard_map.60.refs_0_), custom_call_target="tpu_custom_call" | custom-call | flops 524288 | bytes 800000 | tf_op jit(solution)/shard_map/pallas_call | solution.py:182
  42.9 9.0 %collective-permute-done.near_ref = bf16[8,128,128]{2,1,0:T(8,128)(2,1)S(1)} collective-permute-done((bf16[8,128,128]{2,1,0:T(8,128)(2,1)}, bf16[8,128,128]{2,1,0:T(8,128)(2,1)S(1)}, u32[]{:S(2)}, u32[]{:S(2)}) %collective-permute-start) | collective-permute-done | bytes 262176 | tf_op jit(solution)/shard_map/ppermute | solution.py:435
  51.9 4.5 %collective-permute-done.6.refs_2_ = bf16[8,128,128]{2,1,0:T(8,128)(2,1)S(1)} collective-permute-done((bf16[8,128,128]{2,1,0:T(8,128)(2,1)}, bf16[8,128,128]{2,1,0:T(8,128)(2,1)S(1)}, u32[]{:S(2)}, u32[]{:S(2)}) %collective-permute-start.6) | collective-permute-done | bytes 262176 | tf_op jit(solution)/shard_map/ppermute | solution.py:443
  57.2 4.4 %collective-permute-start.7 = (f32[4,136,128]{2,1,0:T(8,128)S(1)}, f32[4,136,128]{2,1,0:T(8,128)S(1)}, u32[]{:S(2)}, u32[]{:S(2)}) collective-permute-start(f32[4,136,128]{2,1,0:T(8,128)S(1)} %get-tuple-element.39), channel_id=1, source_target_pairs={{0,1},{1,0},{2,3},{3,2},{4,5},{5,4},{6,7},{7,6},{8,9},{9,8},{10,11... | collective-permute-start | bytes 835592 | tf_op jit(solution)/shard_map/ppermute | solution.py:455
  63.4 3.0 %collective-permute-start.10 = (bf16[4,144,128]{2,1,0:T(8,128)(2,1)S(1)}, bf16[4,144,128]{2,1,0:T(8,128)(2,1)S(1)}, u32[]{:S(2)}, u32[]{:S(2)}) collective-permute-start(bf16[4,144,128]{2,1,0:T(8,128)(2,1)S(1)} %shard_map.63.refs_0_), channel_id=1, source_target_pairs={{0,4},{1,5},{2,6},{3,7},{4,0},{5,1},{6,2},{7,3},{8,12},{9,13},{10,... | collective-permute-start | bytes 442376 | tf_op jit(solution)/shard_map/ppermute | solution.py:465
  67.9 2.2 %collective-permute-done.10.refs_3_ = bf16[4,144,128]{2,1,0:T(8,128)(2,1)S(1)} collective-permute-done((bf16[4,144,128]{2,1,0:T(8,128)(2,1)S(1)}, bf16[4,144,128]{2,1,0:T(8,128)(2,1)S(1)}, u32[]{:S(2)}, u32[]{:S(2)}) %collective-permute-start.10) | collective-permute-done | bytes 147488 | tf_op jit(solution)/shard_map/ppermute | solution.py:465
  70.1 3.5 %collective-permute-done.9.refs_2_ = bf16[4,144,128]{2,1,0:T(8,128)(2,1)S(1)} collective-permute-done((bf16[4,144,128]{2,1,0:T(8,128)(2,1)S(1)}, bf16[4,144,128]{2,1,0:T(8,128)(2,1)S(1)}, u32[]{:S(2)}, u32[]{:S(2)}) %collective-permute-start.9) | collective-permute-done | bytes 147488 | tf_op jit(solution)/shard_map/ppermute | solution.py:465
  74.3 2.8 %collective-permute-start.13 = (bf16[4,144,128]{2,1,0:T(8,128)(2,1)S(1)}, bf16[4,144,128]{2,1,0:T(8,128)(2,1)S(1)}, u32[]{:S(2)}, u32[]{:S(2)}) collective-permute-start(bf16[4,144,128]{2,1,0:T(8,128)(2,1)S(1)} %shard_map.64.refs_4_), channel_id=1, source_target_pairs={{0,16},{1,17},{2,18},{3,19},{4,20},{5,21},{6,22},{7,23},{8,24},{9,... | collective-permute-start | bytes 442376 | tf_op jit(solution)/shard_map/ppermute | solution.py:475
  78.6 1.3 collective-permute-done.13.refs_7_
  79.9 3.2 %collective-permute-done.12.refs_6_ = bf16[4,144,128]{2,1,0:T(8,128)(2,1)S(1)} collective-permute-done((bf16[4,144,128]{2,1,0:T(8,128)(2,1)S(1)}, bf16[4,144,128]{2,1,0:T(8,128)(2,1)S(1)}, u32[]{:S(2)}, u32[]{:S(2)}) %collective-permute-start.12) | collective-permute-done | bytes 147488 | tf_op jit(solution)/shard_map/ppermute | solution.py:475
  84.0 1.6 %shard_map.65 = (f32[4,128,128]{2,1,0:T(8,128)S(1)}, f32[4,128,128]{2,1,0:T(8,128)}) custom-call(s32[4]{0:T(128)S(1)} %pad_add_fusion.2.place, f32[8,128,128]{2,1,0:T(8,128)S(1)} %copy-done.1, f32[4,136,128]{2,1,0:T(8,128)S(1)} %get-tuple-element.38.mine_ref, f32[4,136,128]{2,1,0:T(8,128)S(1)} %collective-permute-done.7.got_ref, ...), custom_call_target="tpu_custom_call" | custom-call | flops 1048576 | bytes 1048576 | tf_op jit(solution)/shard_map/pallas_call | solution.py:319
  85.6 2.3 %collective-permute-start.14 = (f32[4,128,128]{2,1,0:T(8,128)}, f32[4,128,128]{2,1,0:T(8,128)S(1)}, u32[]{:S(2)}, u32[]{:S(2)}) collective-permute-start(f32[4,128,128]{2,1,0:T(8,128)} %get-tuple-element.41), channel_id=1, source_target_pairs={{0,1},{1,0},{2,3},{3,2},{4,5},{5,4},{6,7},{7,6},{8,9},{9,8},{10,11... | collective-permute-start | bytes 786440 | tf_op jit(solution)/shard_map/ppermute | solution.py:455
  87.9 1.3 collective-permute-done.14.got_ref
  90.9 1.9 %shard_map.66 = (bf16[8,128,128]{2,1,0:T(8,128)(2,1)S(1)}, bf16[8,128,128]{2,1,0:T(8,128)(2,1)}, bf16[8,128,128]{2,1,0:T(8,128)(2,1)}, bf16[8,128,128]{2,1,0:T(8,128)(2,1)}, bf16[8,128,128]{2,1,0:T(8,128)(2,1)}) custom-call(s32[4]{0:T(128)S(1)} %pad_add_fusion.2.place, f32[64]{0:T(128)S(1)} %exp.25.d_ref, f32[4,128,128]{2,1,0:T(8,128)S(1)} %get-tuple-element.40.keep_ref, ...), custom_call_target="tpu_custom_call" | custom-call | flops 2097152 | bytes 5242880 | tf_op jit(solution)/shard_map/pallas_call | solution.py:373
  94.4 3.2 %collective-permute-start.18 = (bf16[8,128,128]{2,1,0:T(8,128)(2,1)}, bf16[8,128,128]{2,1,0:T(8,128)(2,1)S(1)}, u32[]{:S(2)}, u32[]{:S(2)}) collective-permute-start(bf16[8,128,128]{2,1,0:T(8,128)(2,1)} %get-tuple-element.50), channel_id=1, source_target_pairs={{160,0},{128,32},{224,64},{192,96},{32,128},{0,160},{96,192},{64,2... | collective-permute-start | bytes 786440 | tf_op jit(solution)/shard_map/ppermute | solution.py:447
  97.7 9.5 %shard_map.67 = (f32[128,8192]{1,0:T(8,128)S(1)}, bf16[128,16384]{1,0:T(8,128)(2,1)S(1)}) custom-call(bf16[128,8192]{1,0:T(8,128)(2,1)} %q_ref.1, bf16[128,8192]{1,0:T(8,128)(2,1)} %k_ref.7, bf16[128,8192]{1,0:T(8,128)(2,1)} %v_ref.7, f32[8,16,128]{2,1,0:T(8,128)S(1)} %all-to-all-done.ld_ref, bf16[8,128,128]{2,1,0:T(8,128)(2,1)S(1)} %get-tuple-element.42.after_ref.refs_2_), custom_call_target="tpu_custom_call" | custom-call | flops 805306368 | bytes 14680064 | tf_op jit(solution)/shard_map/pallas_call | solution.py:144
  108.0 1.5 %collective-permute-start.19 = (bf16[8,128,128]{2,1,0:T(8,128)(2,1)S(1)}, bf16[8,128,128]{2,1,0:T(8,128)(2,1)S(1)}, u32[]{:S(2)}, u32[]{:S(2)}) collective-permute-start(bf16[8,128,128]{2,1,0:T(8,128)(2,1)S(1)} %get-tuple-element.52), channel_id=1, source_target_pairs={{0,32},{32,0},{64,96},{96,64},{128,160},{160,128},{192,224},{224,1... | collective-permute-start | bytes 786440 | tf_op jit(solution)/shard_map/ppermute | solution.py:435
  110.3 4.1 %shard_map.70.refs_0_ = bf16[128,8192]{1,0:T(8,128)(2,1)} custom-call(s32[4]{0:T(128)S(1)} %pad_add_fusion.1.chunks, bf16[128,16384]{1,0:T(8,128)(2,1)S(1)} %get-tuple-element.43.refs_0_.refs_1_, f32[128,8192]{1,0:T(8,128)S(1)} %get-tuple-element.44.refs_1_.refs_2_, bf16[8,128,128]{2,1,0:T(8,128)(2,1)S(1)} %get-tuple-element.42.after_ref.refs_2_, ...), custom_call_target="tpu_custom_call" | custom-call | flops 268435456 | bytes 6000000 | tf_op jit(solution)/shard_map/pallas_call | solution.py:418
  114.5 1.9 %collective-permute-done.18.start_ref = bf16[8,128,128]{2,1,0:T(8,128)(2,1)S(1)} collective-permute-done((bf16[8,128,128]{2,1,0:T(8,128)(2,1)}, bf16[8,128,128]{2,1,0:T(8,128)(2,1)S(1)}, u32[]{:S(2)}, u32[]{:S(2)}) %collective-permute-start.18) | collective-permute-done | bytes 262176 | tf_op jit(solution)/shard_map/ppermute | solution.py:447
  116.4 1.6 %copy-done = bf16[128,8192]{1,0:T(8,128)(2,1)S(1)} copy-done((bf16[128,8192]{1,0:T(8,128)(2,1)S(1)}, bf16[128,8192]{1,0:T(8,128)(2,1)}, u32[]{:S(2)}) %copy-start) | copy-done | bytes 2097176
  118.7 4.7 %collective-permute-start.21 = (bf16[8,128,128]{2,1,0:T(8,128)(2,1)S(1)}, bf16[8,128,128]{2,1,0:T(8,128)(2,1)S(1)}, u32[]{:S(2)}, u32[]{:S(2)}) collective-permute-start(bf16[8,128,128]{2,1,0:T(8,128)(2,1)S(1)} %get-tuple-element.54), channel_id=1, source_target_pairs={{0,32},{32,0},{64,96},{96,64},{128,160},{160,128},{192,224},{224,1... | collective-permute-start | bytes 786440 | tf_op jit(solution)/shard_map/ppermute | solution.py:435
  124.0 3.4 %shard_map.72.refs_0_ = bf16[128,8192]{1,0:T(8,128)(2,1)} custom-call(s32[3]{0:T(128)S(1)} %pad_add_fusion.chunks, bf16[128,8192]{1,0:T(8,128)(2,1)} %shard_map.70.refs_0_, bf16[128,16384]{1,0:T(8,128)(2,1)S(1)} %get-tuple-element.43.refs_0_.refs_1_, f32[128,8192]{1,0:T(8,128)S(1)} %get-tuple-element.44.refs_1_.refs_2_, ...), custom_call_target="tpu_custom_call", output_to_operand_aliasing={{}: (1, {})} | custom-call | flops 201326592 | bytes 4500000 | tf_op jit(solution)/shard_map/pallas_call | solution.py:418
  127.4 2.2 %collective-permute-done.21.refs_3_ = bf16[8,128,128]{2,1,0:T(8,128)(2,1)S(1)} collective-permute-done((bf16[8,128,128]{2,1,0:T(8,128)(2,1)S(1)}, bf16[8,128,128]{2,1,0:T(8,128)(2,1)S(1)}, u32[]{:S(2)}, u32[]{:S(2)}) %collective-permute-start.21) | collective-permute-done | bytes 262176 | tf_op jit(solution)/shard_map/ppermute | solution.py:435
  129.6 1.2 shard_map.73
  (63 shorter events, 19.6 us)
Async XLA Ops:
  0.0 0.8 copy-start.2
  1.4 16.3 %all-to-all-start = ((f32[8,16,128]{2,1,0:T(8,128)}), f32[8,16,128]{2,1,0:T(8,128)S(1)}, u32[]{:S(2)}, u32[]{:S(2)}) async-start(f32[8,16,128]{2,1,0:T(8,128)} %shard_map.55), calls=%async_computation | async-start | bytes 131072 | tf_op jit(solution)/shard_map/all_to_all | solution.py:490
  20.4 11.7 %collective-permute-start.1 = (bf16[8,128,128]{2,1,0:T(8,128)(2,1)S(1)}, bf16[8,128,128]{2,1,0:T(8,128)(2,1)S(1)}, u32[]{:S(2)}, u32[]{:S(2)}) collective-permute-start(bf16[8,128,128]{2,1,0:T(8,128)(2,1)S(1)} %get-tuple-element.33), channel_id=1, source_target_pairs={{0,32},{32,0},{64,96},{96,64},{128,160},{160,128},{192,224},{224,1... | collective-permute-start | bytes 786440 | tf_op jit(solution)/shard_map/ppermute | solution.py:435
  20.8 12.6 %collective-permute-start.3 = (bf16[8,128,128]{2,1,0:T(8,128)(2,1)S(1)}, bf16[8,128,128]{2,1,0:T(8,128)(2,1)S(1)}, u32[]{:S(2)}, u32[]{:S(2)}) collective-permute-start(bf16[8,128,128]{2,1,0:T(8,128)(2,1)S(1)} %get-tuple-element.35), channel_id=1, source_target_pairs={{0,32},{32,0},{64,96},{96,64},{128,160},{160,128},{192,224},{224,1... | collective-permute-start | bytes 786440 | tf_op jit(solution)/shard_map/ppermute | solution.py:435
  26.4 14.7 %collective-permute-start.5 = (bf16[8,128,128]{2,1,0:T(8,128)(2,1)}, bf16[8,128,128]{2,1,0:T(8,128)(2,1)S(1)}, u32[]{:S(2)}, u32[]{:S(2)}) collective-permute-start(bf16[8,128,128]{2,1,0:T(8,128)(2,1)} %get-tuple-element.37), channel_id=1, source_target_pairs={{0,32},{32,0},{64,96},{96,64},{128,160},{160,128},{192,224},{224,1... | collective-permute-start | bytes 786440 | tf_op jit(solution)/shard_map/ppermute | solution.py:435
  27.1 24.8 %collective-permute-start = (bf16[8,128,128]{2,1,0:T(8,128)(2,1)}, bf16[8,128,128]{2,1,0:T(8,128)(2,1)S(1)}, u32[]{:S(2)}, u32[]{:S(2)}) collective-permute-start(bf16[8,128,128]{2,1,0:T(8,128)(2,1)} %get-tuple-element.31), channel_id=1, source_target_pairs={{0,32},{32,0},{64,96},{96,64},{128,160},{160,128},{192,224},{224,1... | collective-permute-start | bytes 786440 | tf_op jit(solution)/shard_map/ppermute | solution.py:435
  32.1 10.4 %copy-start.3 = (f32[1024,8]{0,1:T(8,128)S(1)}, f32[1024,8]{0,1:T(8,128)}, u32[]{:S(2)}) copy-start(f32[1024,8]{0,1:T(8,128)} %param.8) | copy-start | bytes 98308
  32.8 19.1 %collective-permute-start.2 = (bf16[8,128,128]{2,1,0:T(8,128)(2,1)S(1)}, bf16[8,128,128]{2,1,0:T(8,128)(2,1)S(1)}, u32[]{:S(2)}, u32[]{:S(2)}) collective-permute-start(bf16[8,128,128]{2,1,0:T(8,128)(2,1)S(1)} %shard_map.59.refs_0_), channel_id=1, source_target_pairs={{0,160},{32,128},{64,224},{96,192},{128,32},{160,0},{192,96},{224,... | collective-permute-start | bytes 786440 | tf_op jit(solution)/shard_map/ppermute | solution.py:443
  34.0 22.4 %collective-permute-start.4 = (bf16[8,128,128]{2,1,0:T(8,128)(2,1)S(1)}, bf16[8,128,128]{2,1,0:T(8,128)(2,1)S(1)}, u32[]{:S(2)}, u32[]{:S(2)}) collective-permute-start(bf16[8,128,128]{2,1,0:T(8,128)(2,1)S(1)} %shard_map.60.refs_0_), channel_id=1, source_target_pairs={{0,192},{32,96},{64,0},{96,160},{128,64},{160,224},{192,128},{224,... | collective-permute-start | bytes 786440 | tf_op jit(solution)/shard_map/ppermute | solution.py:443
  42.5 14.0 %collective-permute-start.6 = (bf16[8,128,128]{2,1,0:T(8,128)(2,1)}, bf16[8,128,128]{2,1,0:T(8,128)(2,1)S(1)}, u32[]{:S(2)}, u32[]{:S(2)}) collective-permute-start(bf16[8,128,128]{2,1,0:T(8,128)(2,1)} %shard_map.61), channel_id=1, source_target_pairs={{0,224},{32,64},{64,32},{96,128},{128,96},{160,192},{192,160},{224... | collective-permute-start | bytes 786440 | tf_op jit(solution)/shard_map/ppermute | solution.py:443
  42.9 41.1 %copy-start.1 = (f32[8,128,128]{2,1,0:T(8,128)S(1)}, f32[8,128,128]{2,1,0:T(8,128)}, u32[]{:S(2)}) copy-start(f32[8,128,128]{2,1,0:T(8,128)} %start_ref.1) | copy-start | bytes 1572868
  57.2 5.6 %collective-permute-start.7 = (f32[4,136,128]{2,1,0:T(8,128)S(1)}, f32[4,136,128]{2,1,0:T(8,128)S(1)}, u32[]{:S(2)}, u32[]{:S(2)}) collective-permute-start(f32[4,136,128]{2,1,0:T(8,128)S(1)} %get-tuple-element.39), channel_id=1, source_target_pairs={{0,1},{1,0},{2,3},{3,2},{4,5},{5,4},{6,7},{7,6},{8,9},{9,8},{10,11... | collective-permute-start | bytes 835592 | tf_op jit(solution)/shard_map/ppermute | solution.py:455
  63.4 6.7 %collective-permute-start.10 = (bf16[4,144,128]{2,1,0:T(8,128)(2,1)S(1)}, bf16[4,144,128]{2,1,0:T(8,128)(2,1)S(1)}, u32[]{:S(2)}, u32[]{:S(2)}) collective-permute-start(bf16[4,144,128]{2,1,0:T(8,128)(2,1)S(1)} %shard_map.63.refs_0_), channel_id=1, source_target_pairs={{0,4},{1,5},{2,6},{3,7},{4,0},{5,1},{6,2},{7,3},{8,12},{9,13},{10,... | collective-permute-start | bytes 442376 | tf_op jit(solution)/shard_map/ppermute | solution.py:465
  66.4 7.2 %collective-permute-start.9 = (bf16[4,144,128]{2,1,0:T(8,128)(2,1)S(1)}, bf16[4,144,128]{2,1,0:T(8,128)(2,1)S(1)}, u32[]{:S(2)}, u32[]{:S(2)}) collective-permute-start(bf16[4,144,128]{2,1,0:T(8,128)(2,1)S(1)} %shard_map.63.refs_0_), channel_id=1, source_target_pairs={{0,6},{1,7},{2,0},{3,1},{4,2},{5,3},{6,4},{7,5},{8,14},{9,15},{10,... | collective-permute-start | bytes 442376 | tf_op jit(solution)/shard_map/ppermute | solution.py:465
  67.2 6.4 %collective-permute-start.8 = (bf16[4,144,128]{2,1,0:T(8,128)(2,1)S(1)}, bf16[4,144,128]{2,1,0:T(8,128)(2,1)S(1)}, u32[]{:S(2)}, u32[]{:S(2)}) collective-permute-start(bf16[4,144,128]{2,1,0:T(8,128)(2,1)S(1)} %shard_map.63.refs_0_), channel_id=1, source_target_pairs={{0,2},{1,3},{2,4},{3,5},{4,6},{5,7},{6,0},{7,1},{8,10},{9,11},{10,... | collective-permute-start | bytes 442376 | tf_op jit(solution)/shard_map/ppermute | solution.py:465
  74.3 5.6 %collective-permute-start.13 = (bf16[4,144,128]{2,1,0:T(8,128)(2,1)S(1)}, bf16[4,144,128]{2,1,0:T(8,128)(2,1)S(1)}, u32[]{:S(2)}, u32[]{:S(2)}) collective-permute-start(bf16[4,144,128]{2,1,0:T(8,128)(2,1)S(1)} %shard_map.64.refs_4_), channel_id=1, source_target_pairs={{0,16},{1,17},{2,18},{3,19},{4,20},{5,21},{6,22},{7,23},{8,24},{9,... | collective-permute-start | bytes 442376 | tf_op jit(solution)/shard_map/ppermute | solution.py:475
  77.1 6.0 %collective-permute-start.12 = (bf16[4,144,128]{2,1,0:T(8,128)(2,1)S(1)}, bf16[4,144,128]{2,1,0:T(8,128)(2,1)S(1)}, u32[]{:S(2)}, u32[]{:S(2)}) collective-permute-start(bf16[4,144,128]{2,1,0:T(8,128)(2,1)S(1)} %shard_map.64.refs_4_), channel_id=1, source_target_pairs={{0,24},{1,25},{2,26},{3,27},{4,28},{5,29},{6,30},{7,31},{8,0},{9,1... | collective-permute-start | bytes 442376 | tf_op jit(solution)/shard_map/ppermute | solution.py:475
  78.0 6.0 %collective-permute-start.11 = (bf16[4,144,128]{2,1,0:T(8,128)(2,1)S(1)}, bf16[4,144,128]{2,1,0:T(8,128)(2,1)S(1)}, u32[]{:S(2)}, u32[]{:S(2)}) collective-permute-start(bf16[4,144,128]{2,1,0:T(8,128)(2,1)S(1)} %shard_map.64.refs_4_), channel_id=1, source_target_pairs={{0,8},{1,9},{2,10},{3,11},{4,12},{5,13},{6,14},{7,15},{8,16},{9,17... | collective-permute-start | bytes 442376 | tf_op jit(solution)/shard_map/ppermute | solution.py:475
  85.6 3.6 %collective-permute-start.14 = (f32[4,128,128]{2,1,0:T(8,128)}, f32[4,128,128]{2,1,0:T(8,128)S(1)}, u32[]{:S(2)}, u32[]{:S(2)}) collective-permute-start(f32[4,128,128]{2,1,0:T(8,128)} %get-tuple-element.41), channel_id=1, source_target_pairs={{0,1},{1,0},{2,3},{3,2},{4,5},{5,4},{6,7},{7,6},{8,9},{9,8},{10,11... | collective-permute-start | bytes 786440 | tf_op jit(solution)/shard_map/ppermute | solution.py:455
  89.2 0.7 copy-start.4
  89.9 0.9 copy-start.5
  92.8 14.5 %collective-permute-start.17 = (bf16[8,128,128]{2,1,0:T(8,128)(2,1)}, bf16[8,128,128]{2,1,0:T(8,128)(2,1)S(1)}, u32[]{:S(2)}, u32[]{:S(2)}) collective-permute-start(bf16[8,128,128]{2,1,0:T(8,128)(2,1)} %get-tuple-element.48), channel_id=1, source_target_pairs={{192,0},{96,32},{0,64},{160,96},{64,128},{224,160},{128,192},{32,2... | collective-permute-start | bytes 786440 | tf_op jit(solution)/shard_map/ppermute | solution.py:447
  92.8 16.7 %collective-permute-start.16 = (bf16[8,128,128]{2,1,0:T(8,128)(2,1)}, bf16[8,128,128]{2,1,0:T(8,128)(2,1)S(1)}, u32[]{:S(2)}, u32[]{:S(2)}) collective-permute-start(bf16[8,128,128]{2,1,0:T(8,128)(2,1)} %get-tuple-element.46), channel_id=1, source_target_pairs={{224,0},{64,32},{32,64},{128,96},{96,128},{192,160},{160,192},{0,2... | collective-permute-start | bytes 786440 | tf_op jit(solution)/shard_map/ppermute | solution.py:447
  93.3 17.0 %collective-permute-start.15 = (bf16[8,128,128]{2,1,0:T(8,128)(2,1)}, bf16[8,128,128]{2,1,0:T(8,128)(2,1)S(1)}, u32[]{:S(2)}, u32[]{:S(2)}) collective-permute-start(bf16[8,128,128]{2,1,0:T(8,128)(2,1)} %get-tuple-element.45), channel_id=1, source_target_pairs={{0,32},{32,0},{64,96},{96,64},{128,160},{160,128},{192,224},{224,1... | collective-permute-start | bytes 786440 | tf_op jit(solution)/shard_map/ppermute | solution.py:435
  94.4 22.0 %collective-permute-start.18 = (bf16[8,128,128]{2,1,0:T(8,128)(2,1)}, bf16[8,128,128]{2,1,0:T(8,128)(2,1)S(1)}, u32[]{:S(2)}, u32[]{:S(2)}) collective-permute-start(bf16[8,128,128]{2,1,0:T(8,128)(2,1)} %get-tuple-element.50), channel_id=1, source_target_pairs={{160,0},{128,32},{224,64},{192,96},{32,128},{0,160},{96,192},{64,2... | collective-permute-start | bytes 786440 | tf_op jit(solution)/shard_map/ppermute | solution.py:447
  108.0 15.5 %collective-permute-start.19 = (bf16[8,128,128]{2,1,0:T(8,128)(2,1)S(1)}, bf16[8,128,128]{2,1,0:T(8,128)(2,1)S(1)}, u32[]{:S(2)}, u32[]{:S(2)}) collective-permute-start(bf16[8,128,128]{2,1,0:T(8,128)(2,1)S(1)} %get-tuple-element.52), channel_id=1, source_target_pairs={{0,32},{32,0},{64,96},{96,64},{128,160},{160,128},{192,224},{224,1... | collective-permute-start | bytes 786440 | tf_op jit(solution)/shard_map/ppermute | solution.py:435
  110.2 13.8 %collective-permute-start.20 = (bf16[8,128,128]{2,1,0:T(8,128)(2,1)S(1)}, bf16[8,128,128]{2,1,0:T(8,128)(2,1)S(1)}, u32[]{:S(2)}, u32[]{:S(2)}) collective-permute-start(bf16[8,128,128]{2,1,0:T(8,128)(2,1)S(1)} %get-tuple-element.53), channel_id=1, source_target_pairs={{0,32},{32,0},{64,96},{96,64},{128,160},{160,128},{192,224},{224,1... | collective-permute-start | bytes 786440 | tf_op jit(solution)/shard_map/ppermute | solution.py:435
  116.4 1.6 %copy-start = (bf16[128,8192]{1,0:T(8,128)(2,1)S(1)}, bf16[128,8192]{1,0:T(8,128)(2,1)}, u32[]{:S(2)}) copy-start(bf16[128,8192]{1,0:T(8,128)(2,1)} %shard_map.70.refs_0_) | copy-start | bytes 6291460
  118.7 10.9 %collective-permute-start.21 = (bf16[8,128,128]{2,1,0:T(8,128)(2,1)S(1)}, bf16[8,128,128]{2,1,0:T(8,128)(2,1)S(1)}, u32[]{:S(2)}, u32[]{:S(2)}) collective-permute-start(bf16[8,128,128]{2,1,0:T(8,128)(2,1)S(1)} %get-tuple-element.54), channel_id=1, source_target_pairs={{0,32},{32,0},{64,96},{96,64},{128,160},{160,128},{192,224},{224,1... | collective-permute-start | bytes 786440 | tf_op jit(solution)/shard_map/ppermute | solution.py:435
